TPU v7x, 512 devices: a whole 4x8x8 slice. The times are simulated.
512 devices in a mesh: plane: 64 (over z, x, core), span: 8 (over y).
Axes of the slice: x: 4, y: 8, z: 8, core: 2. Of those that a mesh axis runs over, the one named last changes fastest.
Arguments:
- stress: float32 [6, 32, 7, 7, 8192], P(None, 'span', None, None, 'plane'), may hold values from -4 to 4
- velocity_grad: float32 [9, 32, 7, 7, 8192], P(None, 'span', None, None, 'plane'), may hold values from -4 to 4
- velocity: float32 [2, 32, 7, 7, 8192], P(None, 'span', None, None, 'plane'), may hold values from -4 to 4
- metric: float32 [3, 7, 7, 8192], P(None, None, None, 'plane'), may hold values from 0.3 to 3
- iteration_counts: int32 [32], replicated, may hold values from 1 to 8
Outputs:
- new_stress: float32 [6, 32, 7, 7, 8192], P(None, 'span', None, None, 'plane')
- pressure: float32 [32, 7, 7, 8192], P('span', None, None, 'plane')
All inputs are finite; a program needn't handle non-finite values.
Results may differ from a plain program's by a relative error of at most 0.0003.
Values sent between devices are 32-bit elements; how exact they have to be, the bound alone decides.
No kernel may reach another device: no remote copies, remote signals or barrier semaphores. Data moves between devices by JAX's collectives and lax.ppermute only.
A program may use at most 128 MiB of HBM per device.

v0:
```python
import jax
import jax.numpy as jnp
import numpy as np
from jax import lax
from jax.sharding import PartitionSpec as P

EX = 8
EY = 16
NDY = 4
NZ = 32
ITMAX = 8


HIGHEST = lax.Precision.HIGHEST
DT_STEP = 0.01
ETA_POLY = 0.5
RELAX_TIME = 1.0
SPAN_UNIT = 0.5
MASS_SCALE = 0.25
UPPER_PAIRS = ((0, 0), (1, 1), (2, 2), (0, 1), (0, 2), (1, 2))
COMPONENT_OF = {
    (0, 0): 0,
    (1, 1): 1,
    (2, 2): 2,
    (0, 1): 3,
    (1, 0): 3,
    (0, 2): 4,
    (2, 0): 4,
    (1, 2): 5,
    (2, 1): 5,
}


def from_behind(value, axis, steps):
    count = lax.axis_size(axis)
    first, last = (max(0, -steps), min(count, count - steps))
    return lax.ppermute(value, axis, [(source, source + steps) for source in range(first, last)])


def node_tables():
    gll_nodes = np.array(
        [
            -1.0,
            -0.830223896278567,
            -0.468848793470714,
            0.0,
            0.468848793470714,
            0.830223896278567,
            1.0,
        ]
    )
    gll_weights = np.array(
        [
            1.0 / 21.0,
            0.276826047361566,
            0.431745381209863,
            0.487619047619048,
            0.431745381209863,
            0.276826047361566,
            1.0 / 21.0,
        ]
    )
    barycentric = np.array(
        [
            1.0
            / np.prod(
                [
                    gll_nodes[col_index] - gll_nodes[other_index]
                    for other_index in range(7)
                    if other_index != col_index
                ]
            )
            for col_index in range(7)
        ]
    )
    derivative = np.zeros((7, 7))
    for row_index in range(7):
        for col_index in range(7):
            if row_index != col_index:
                derivative[row_index, col_index] = (
                    barycentric[col_index]
                    / barycentric[row_index]
                    / (gll_nodes[row_index] - gll_nodes[col_index])
                )
        derivative[row_index, row_index] = -np.sum(derivative[row_index])
    return (jnp.asarray(derivative, jnp.float32), jnp.asarray(gll_weights, jnp.float32))


def span_tables(plane_count):
    row_ids = jnp.arange(plane_count, dtype=jnp.int32)
    harmonic = jnp.where(row_ids == 1, plane_count // 2, row_ids // 2)
    is_sine = (row_ids % 2 == 1) & (row_ids != 1)
    turns = harmonic[:, None] * row_ids[None, :] % plane_count
    phase = 2.0 * np.pi / plane_count * turns.astype(jnp.float32)
    basis = jnp.where(is_sine[:, None], jnp.sin(phase), jnp.cos(phase))
    scale_row = jnp.where(
        row_ids < 2, 1.0 / np.sqrt(plane_count), np.sqrt(2.0 / plane_count)
    ).astype(jnp.float32)
    basis = basis * scale_row[:, None]
    wavenum = SPAN_UNIT * harmonic.astype(jnp.float32)
    partner = basis[jnp.bitwise_xor(row_ids, 1)]
    slope = jnp.where(row_ids < 2, 0.0, jnp.where(is_sine, -wavenum, wavenum))
    return (basis, slope[:, None] * partner, wavenum)


def span_apply(matrix, field):
    return jnp.einsum("rz,z...->r...", matrix, field, precision=HIGHEST)


def along_first(matrix, field):
    total = matrix[:, 0][:, None, None] * field[..., 0:1, :, :]
    for inner in range(1, 7):
        total = total + matrix[:, inner][:, None, None] * field[..., inner : inner + 1, :, :]
    return total


def along_second(matrix, field):
    total = matrix[:, 0][:, None] * field[..., :, 0:1, :]
    for inner in range(1, 7):
        total = total + matrix[:, inner][:, None] * field[..., :, inner : inner + 1, :]
    return total


def element_ids():
    flat_ids = jnp.arange(EX * EY)
    return (flat_ids // EY, flat_ids % EY)


def forcing_terms(tau, grads):
    rows_out = []
    for first_axis, second_axis in UPPER_PAIRS:
        stretch = ETA_POLY * (
            grads[3 * first_axis + second_axis] + grads[3 * second_axis + first_axis]
        )
        term_sum = (stretch - tau[COMPONENT_OF[first_axis, second_axis]]) / RELAX_TIME
        for inner_axis in range(3):
            term_sum = (
                term_sum
                + grads[3 * first_axis + inner_axis] * tau[COMPONENT_OF[inner_axis, second_axis]]
            )
            term_sum = (
                term_sum
                + tau[COMPONENT_OF[first_axis, inner_axis]] * grads[3 * second_axis + inner_axis]
            )
        rows_out.append(term_sum)
    return jnp.stack(rows_out)


def outside_traces(tau, from_left, from_right, from_below, from_above):
    flow_pos, cross_pos = element_ids()
    left = jnp.concatenate([from_left, tau[:, :, 6, :, :-EY]], axis=-1)
    right = jnp.concatenate([tau[:, :, 0, :, EY:], from_right], axis=-1)
    below = jnp.where(
        cross_pos == 0,
        jnp.repeat(from_below, EY, axis=-1),
        jnp.roll(tau[:, :, :, 6, :], 1, axis=-1),
    )
    above = jnp.where(
        cross_pos == EY - 1,
        jnp.repeat(from_above, EY, axis=-1),
        jnp.roll(tau[:, :, :, 0, :], -1, axis=-1),
    )
    return (left, right, below, above)


def advance_stress(tau, grads, velocity_field, outside, deriv, weights):
    left, right, below, above = outside
    flow_speed = velocity_field[0]
    cross_speed = velocity_field[1]
    advect = flow_speed * (2.0 * along_first(deriv, tau)) + cross_speed * (
        2.0 * along_second(deriv, tau)
    )
    lift = 2.0 / weights[0]
    advect = advect.at[:, :, 0].add(
        -lift * jnp.minimum(-flow_speed[:, 0], 0.0) * (tau[:, :, 0] - left)
    )
    advect = advect.at[:, :, 6].add(
        -lift * jnp.minimum(flow_speed[:, 6], 0.0) * (tau[:, :, 6] - right)
    )
    advect = advect.at[:, :, :, 0].add(
        -lift * jnp.minimum(-cross_speed[:, :, 0], 0.0) * (tau[:, :, :, 0] - below)
    )
    advect = advect.at[:, :, :, 6].add(
        -lift * jnp.minimum(cross_speed[:, :, 6], 0.0) * (tau[:, :, :, 6] - above)
    )
    return tau + DT_STEP * (forcing_terms(tau, grads) - advect)


def pressure_sources(tau, deriv):

    def grad_flow(field):
        return 2.0 * along_first(deriv, field)

    def grad_cross(field):
        return 2.0 * along_second(deriv, field)

    flux_flow = grad_flow(tau[0]) + grad_cross(tau[3])
    flux_cross = grad_flow(tau[3]) + grad_cross(tau[1])
    planar = grad_flow(flux_flow) + grad_cross(flux_cross)
    crossed = grad_flow(tau[4]) + grad_cross(tau[5])
    return jnp.stack([planar, crossed, tau[2]])


def quad_table(weights):
    return weights[:, None, None] * weights[None, :, None]


def share_table():
    node_ids = jnp.arange(7)
    edge_share = jnp.where((node_ids == 0) | (node_ids == 6), 0.5, 1.0).astype(jnp.float32)
    return edge_share[:, None, None] * edge_share[None, :, None]


def apply_operator(field, coef, wavesq, deriv, weights):
    quad = quad_table(weights)
    flux_first = along_first(deriv, field) * (quad * coef[0])
    flux_second = along_second(deriv, field) * (quad * coef[1])
    stiff_part = along_first(deriv.T, flux_first) + along_second(deriv.T, flux_second)
    return stiff_part + (MASS_SCALE * wavesq)[:, None, None, None] * (quad * coef[2]) * field


def join_first(field):
    joined = field[:, 6, :, :-EY] + field[:, 0, :, EY:]
    return field.at[:, 6, :, :-EY].set(joined).at[:, 0, :, EY:].set(joined)


def join_second(field):
    flow_pos, cross_pos = element_ids()
    upper = field[:, :, 6, :]
    lower = field[:, :, 0, :]
    joined_upper = upper + jnp.where(cross_pos < EY - 1, jnp.roll(lower, -1, axis=-1), 0.0)
    joined_lower = lower + jnp.where(cross_pos > 0, jnp.roll(upper, 1, axis=-1), 0.0)
    return field.at[:, :, 6, :].set(joined_upper).at[:, :, 0, :].set(joined_lower)


def interior_mask(low_first, high_first, low_second, high_second):
    node_ids = jnp.arange(7)
    flow_pos, cross_pos = element_ids()
    left = (node_ids[:, None, None] == 0) & (flow_pos[None, None, :] == 0) & low_first
    right = (node_ids[:, None, None] == 6) & (flow_pos[None, None, :] == EX - 1) & high_first
    bottom = (node_ids[None, :, None] == 0) & (cross_pos[None, None, :] == 0) & low_second
    top = (node_ids[None, :, None] == 6) & (cross_pos[None, None, :] == EY - 1) & high_second
    return jnp.logical_not(left | right | bottom | top).astype(jnp.float32)


def weighted_dot(first, second, share):
    return jnp.sum(first * second * share, axis=(1, 2, 3))


def stress_edge(slab, offset):
    return from_behind(slab, "plane", offset)


def node_share(slab, offset):
    return from_behind(slab, "plane", offset)


def row_total(values):
    return lax.psum(values, "plane")


def local(stress, velocity_grad, velocity, metric, iteration_counts):
    deriv, weights = node_tables()
    column_count = lax.axis_size("plane") // NDY
    plane_index = lax.axis_index("plane")
    across_pos = plane_index % NDY
    along_pos = plane_index // NDY
    span_index = lax.axis_index("span")
    row_count = NZ // lax.axis_size("span")
    first_row = span_index * row_count
    elem_count = EX * EY
    has_below = (across_pos > 0).astype(jnp.float32)
    has_above = (across_pos < NDY - 1).astype(jnp.float32)
    from_left = stress_edge(stress[:, :, 6, :, elem_count - EY :], NDY)
    from_right = stress_edge(stress[:, :, 0, :, :EY], -NDY)
    from_below = stress_edge(stress[:, :, :, 6, EY - 1 :: EY], 1) * has_below
    from_above = stress_edge(stress[:, :, :, 0, 0::EY], -1) * has_above
    outside = outside_traces(stress, from_left, from_right, from_below, from_above)
    new_tau = advance_stress(stress, velocity_grad, velocity, outside, deriv, weights)
    flat_sources = pressure_sources(new_tau, deriv)
    basis, slope_basis, wavenum = span_tables(NZ)
    wavesq_all = wavenum * wavenum
    row_wavesq = lax.dynamic_slice_in_dim(wavesq_all, first_row, row_count, 0)
    row_limits = lax.dynamic_slice_in_dim(iteration_counts, first_row, row_count, 0)
    row_basis = lax.dynamic_slice_in_dim(basis, first_row, row_count, 0)
    row_slope = lax.dynamic_slice_in_dim(slope_basis, first_row, row_count, 0)
    empty_rows = jnp.zeros((row_count,) + flat_sources.shape[2:], jnp.float32)
    piece = lax.all_gather(flat_sources, "span", axis=1, tiled=True)
    width = piece.shape[1]
    cols_basis = lax.slice_in_dim(row_basis, 0, width, axis=1)
    cols_slope = lax.slice_in_dim(row_slope, 0, width, axis=1)
    gained = span_apply(cols_basis, piece[0]) - row_wavesq[:, None, None, None] * span_apply(
        cols_basis, piece[2]
    )
    rows = empty_rows + gained + 2.0 * span_apply(cols_slope, piece[1])
    mask = interior_mask(
        along_pos == 0, along_pos == column_count - 1, across_pos == 0, across_pos == NDY - 1
    )

    def assemble(field):
        first = join_first(field)
        right_part = node_share(first[:, 0, :, :EY], -NDY)
        left_part = node_share(first[:, 6, :, elem_count - EY :], NDY)
        first = first.at[:, 6, :, elem_count - EY :].add(right_part).at[:, 0, :, :EY].add(left_part)
        second = join_second(first)
        above_part = node_share(second[:, :, 0, 0::EY], -1)
        below_part = node_share(second[:, :, 6, EY - 1 :: EY], 1)
        second = second.at[:, :, 6, EY - 1 :: EY].add(above_part).at[:, :, 0, 0::EY].add(below_part)
        return mask * second

    quad = quad_table(weights)
    rhs = assemble(MASS_SCALE * quad * metric[2] * rows)
    share = share_table()
    solution = jnp.zeros_like(rhs)
    residual = rhs
    direction = rhs
    norm_now = row_total(weighted_dot(residual, residual, share))
    for sweep_index in range(ITMAX):
        active = row_limits > sweep_index
        image = assemble(apply_operator(direction, metric, row_wavesq, deriv, weights))
        curvature = row_total(weighted_dot(direction, image, share))
        step_size = jnp.where(active, norm_now / curvature, 0.0)
        solution = solution + step_size[:, None, None, None] * direction
        residual = residual - step_size[:, None, None, None] * image
        fresh = row_total(weighted_dot(residual, residual, share))
        direction = jnp.where(
            active[:, None, None, None],
            residual + (fresh / norm_now)[:, None, None, None] * direction,
            direction,
        )
        norm_now = jnp.where(active, fresh, norm_now)
    plane_inverse = lax.dynamic_slice_in_dim(basis.T, first_row, row_count, 0)
    empty_planes = jnp.zeros(solution.shape, jnp.float32)
    piece = lax.all_gather(solution, "span", axis=0, tiled=True)
    cols_inverse = lax.slice_in_dim(plane_inverse, 0, piece.shape[0], axis=1)
    pressure = empty_planes + span_apply(cols_inverse, piece)
    return (new_tau, pressure)


def solution(mesh):
    return jax.shard_map(
        local,
        mesh=mesh,
        in_specs=(
            P(None, "span", None, None, "plane"),
            P(None, "span", None, None, "plane"),
            P(None, "span", None, None, "plane"),
            P(None, None, None, "plane"),
            P(),
        ),
        out_specs=(P(None, "span", None, None, "plane"), P("span", None, None, "plane")),
        check_vma=False,
    )
```

profile of v0, /device:TPU:256, one launch (start us, length us, event | category | flops | bytes accessed | tf_op | source)
XLA Modules:
  0.0 2329.8 jit_solution(3047284695458551797)
XLA Ops:
  7.2 19.7 slice.3472
  40.0 19.7 slice.3477
  83.5 42.4 %all-gather.2.cloned.1.call-done = f32[3,32,7,7,128]{4,3,2,0,1:T(8,128)} async-done(((f32[3,4,7,7,128]{4,3,2,0,1:T(8,128)}), f32[3,32,7,7,128]{4,3,2,0,1:T(8,128)}) %all-gather.2.cloned.1.call-update) | async-done | bytes 2408464 | tf_op jit(solution)/shard_map/all_gather | solution.py:288
  196.4 124.6 %all-reduce.2 = (f32[4]{0:T(128)S(1)}, f32[4]{0:T(128)S(1)}) all-reduce(f32[4]{0:T(128)S(1)} %get-tuple-element.703, f32[4]{0:T(128)S(1)} %get-tuple-element.702), channel_id=1, replica_groups=mesh['plane'=64,'span'=8] {'plane'}, use_global_device_ids=true, to_apply=%region_4.5 | all-reduce | flops 8 | bytes 64 | tf_op jit(solution)/shard_map/psum | solution.py:259
  321.8 124.0 %psum.114 = f32[4]{0:T(128)S(1)} all-reduce(f32[4]{0:T(128)S(1)} %multiply_reduce_fusion.13), channel_id=1, replica_groups=mesh['plane'=64,'span'=8] {'plane'}, use_global_device_ids=true, to_apply=%region_10.11 | all-reduce | flops 4 | bytes 32 | tf_op jit(solution)/shard_map/psum | solution.py:259
  453.3 5.4 collective-permute-start.13
  478.4 124.1 %psum.115 = f32[4]{0:T(128)S(1)} all-reduce(f32[4]{0:T(128)S(1)} %multiply_reduce_fusion.12), channel_id=1, replica_groups=mesh['plane'=64,'span'=8] {'plane'}, use_global_device_ids=true, to_apply=%region_14.15 | all-reduce | flops 4 | bytes 32 | tf_op jit(solution)/shard_map/psum | solution.py:259
  602.7 124.1 %psum.116 = f32[4]{0:T(128)S(1)} all-reduce(f32[4]{0:T(128)S(1)} %get-tuple-element.736), channel_id=1, replica_groups=mesh['plane'=64,'span'=8] {'plane'}, use_global_device_ids=true, to_apply=%region_16.17 | all-reduce | flops 4 | bytes 32 | tf_op jit(solution)/shard_map/psum | solution.py:259
  734.1 5.6 collective-permute-start.17
  759.3 124.1 %psum.117 = f32[4]{0:T(128)S(1)} all-reduce(f32[4]{0:T(128)S(1)} %multiply_reduce_fusion.10), channel_id=1, replica_groups=mesh['plane'=64,'span'=8] {'plane'}, use_global_device_ids=true, to_apply=%region_20.21 | all-reduce | flops 4 | bytes 32 | tf_op jit(solution)/shard_map/psum | solution.py:259
  883.6 124.1 %psum.118 = f32[4]{0:T(128)S(1)} all-reduce(f32[4]{0:T(128)S(1)} %get-tuple-element.730), channel_id=1, replica_groups=mesh['plane'=64,'span'=8] {'plane'}, use_global_device_ids=true, to_apply=%region_22.23 | all-reduce | flops 4 | bytes 32 | tf_op jit(solution)/shard_map/psum | solution.py:259
  1040.6 124.1 %psum.119 = f32[4]{0:T(128)S(1)} all-reduce(f32[4]{0:T(128)S(1)} %multiply_reduce_fusion.8), channel_id=1, replica_groups=mesh['plane'=64,'span'=8] {'plane'}, use_global_device_ids=true, to_apply=%region_26.27 | all-reduce | flops 4 | bytes 32 | tf_op jit(solution)/shard_map/psum | solution.py:259
  1165.0 124.1 %psum.120 = f32[4]{0:T(128)S(1)} all-reduce(f32[4]{0:T(128)S(1)} %get-tuple-element.724), channel_id=1, replica_groups=mesh['plane'=64,'span'=8] {'plane'}, use_global_device_ids=true, to_apply=%region_28.29 | all-reduce | flops 4 | bytes 32 | tf_op jit(solution)/shard_map/psum | solution.py:259
  1297.0 5.4 collective-permute-start.25
  1321.6 124.1 %psum.121 = f32[4]{0:T(128)S(1)} all-reduce(f32[4]{0:T(128)S(1)} %multiply_reduce_fusion.6), channel_id=1, replica_groups=mesh['plane'=64,'span'=8] {'plane'}, use_global_device_ids=true, to_apply=%region_32.33 | all-reduce | flops 4 | bytes 32 | tf_op jit(solution)/shard_map/psum | solution.py:259
  1446.1 124.3 %psum.122 = f32[4]{0:T(128)S(1)} all-reduce(f32[4]{0:T(128)S(1)} %get-tuple-element.718), channel_id=1, replica_groups=mesh['plane'=64,'span'=8] {'plane'}, use_global_device_ids=true, to_apply=%region_34.35 | all-reduce | flops 4 | bytes 32 | tf_op jit(solution)/shard_map/psum | solution.py:259
  1578.2 5.4 collective-permute-start.29
  1603.4 124.1 %psum.123 = f32[4]{0:T(128)S(1)} all-reduce(f32[4]{0:T(128)S(1)} %multiply_reduce_fusion.4), channel_id=1, replica_groups=mesh['plane'=64,'span'=8] {'plane'}, use_global_device_ids=true, to_apply=%region_38.39 | all-reduce | flops 4 | bytes 32 | tf_op jit(solution)/shard_map/psum | solution.py:259
  1727.7 124.1 %psum.124 = f32[4]{0:T(128)S(1)} all-reduce(f32[4]{0:T(128)S(1)} %get-tuple-element.712), channel_id=1, replica_groups=mesh['plane'=64,'span'=8] {'plane'}, use_global_device_ids=true, to_apply=%region_40.41 | all-reduce | flops 4 | bytes 32 | tf_op jit(solution)/shard_map/psum | solution.py:259
  1859.9 5.4 collective-permute-start.33
  1886.1 124.5 %psum.125 = f32[4]{0:T(128)S(1)} all-reduce(f32[4]{0:T(128)S(1)} %multiply_reduce_fusion.2), channel_id=1, replica_groups=mesh['plane'=64,'span'=8] {'plane'}, use_global_device_ids=true, to_apply=%region_44.45 | all-reduce | flops 4 | bytes 32 | tf_op jit(solution)/shard_map/psum | solution.py:259
  2011.5 124.1 %psum.126 = f32[4]{0:T(128)S(1)} all-reduce(f32[4]{0:T(128)S(1)} %multiply_reduce_fusion.1), channel_id=1, replica_groups=mesh['plane'=64,'span'=8] {'plane'}, use_global_device_ids=true, to_apply=%region_46.47 | all-reduce | flops 4 | bytes 32 | tf_op jit(solution)/shard_map/psum | solution.py:259
  2169.8 124.5 %psum.127 = f32[4]{0:T(128)S(1)} all-reduce(f32[4]{0:T(128)S(1)} %multiply_reduce_fusion), channel_id=1, replica_groups=mesh['plane'=64,'span'=8] {'plane'}, use_global_device_ids=true, to_apply=%region_50.51 | all-reduce | flops 4 | bytes 32 | tf_op jit(solution)/shard_map/psum | solution.py:259
  2294.6 26.6 %all_gather.7 = f32[32,7,7,128]{3,2,1,0:T(8,128)S(1)} all-gather(f32[4,7,7,128]{3,2,1,0:T(8,128)S(1)} %copy.834), channel_id=1, replica_groups=mesh['plane'=64,'span'=8] {'span'}, dimensions={0}, use_global_device_ids=true | all-gather | bytes 903168 | tf_op jit(solution)/shard_map/all_gather | solution.py:334
  (694 shorter events, 313.6 us)
Async XLA Ops:
  7.2 118.8 %all-gather.2.cloned.1.call-start = ((), (), s32[]{:S(2)}) async-start(), calls=%async_computation | async-start | bytes 3096576 | tf_op jit(solution)/shard_map/all_gather | solution.py:288
  26.9 44.7 %collective-permute-start.2 = (f32[6,4,7,8]{3,1,2,0:T(4,128)}, f32[6,4,7,8]{3,1,2,0:T(4,128)}, u32[]{:S(2)}, u32[]{:S(2)}) collective-permute-start(f32[6,4,7,8]{3,1,2,0:T(4,128)} %bitcast.23), channel_id=1, source_target_pairs={{0,8},{8,16},{16,24},{24,32},{32,40},{40,48},{48,56},{56,64},{64,7... | collective-permute-start | bytes 16136 | tf_op jit(solution)/shard_map/ppermute | solution.py:37
  30.6 43.9 %collective-permute-start = (f32[6,4,7,16]{3,1,2,0:T(4,128)}, f32[6,4,7,16]{3,1,2,0:T(4,128)}, u32[]{:S(2)}, u32[]{:S(2)}) collective-permute-start(f32[6,4,7,16]{3,1,2,0:T(4,128)} %get-tuple-element.769), channel_id=1, source_target_pairs={{0,32},{8,40},{16,48},{24,56},{32,64},{40,72},{48,80},{56,88},{64,... | collective-permute-start | bytes 32264 | tf_op jit(solution)/shard_map/ppermute | solution.py:37
  35.5 40.1 %collective-permute-start.1 = (f32[6,4,7,16]{3,1,2,0:T(4,128)}, f32[6,4,7,16]{3,1,2,0:T(4,128)}, u32[]{:S(2)}, u32[]{:S(2)}) collective-permute-start(f32[6,4,7,16]{3,1,2,0:T(4,128)} %get-tuple-element.768), channel_id=1, source_target_pairs={{32,0},{40,8},{48,16},{56,24},{64,32},{72,40},{80,48},{88,56},{96,... | collective-permute-start | bytes 32264 | tf_op jit(solution)/shard_map/ppermute | solution.py:37
  59.8 12.8 collective-permute-start.3
  139.0 9.2 collective-permute-start.5
  152.5 8.4 collective-permute-start.7
  171.3 9.2 collective-permute-start.9
  184.8 8.4 collective-permute-start.11
  453.3 9.2 collective-permute-start.13
  466.8 8.4 collective-permute-start.15
  732.2 7.5 collective-permute-start.16
  734.1 9.2 collective-permute-start.17
  747.7 8.4 collective-permute-start.19
  1015.4 9.2 collective-permute-start.21
  1029.0 8.4 collective-permute-start.23
  1297.0 9.2 collective-permute-start.25
  1310.0 8.4 collective-permute-start.27
  1578.2 9.2 collective-permute-start.29
  1591.8 8.4 collective-permute-start.31
  1859.9 9.2 collective-permute-start.33
  1873.5 8.7 collective-permute-start.35
  2144.3 9.2 collective-permute-start.37
  2157.3 8.4 collective-permute-start.39
  (103 other events, 12571.3 us)
Sparse Core Ops, SparseCore 0:
  79.8 46.1 all-gather.1
where the time goes:
time: 2340 us; the launch traced here: 2330 us
  blocking collectives  1890 us (81%)
  local copies, waits for them, and re-layouts  132 us (6%)
  starting transfers between devices  122 us (5%)
  waiting for transfers between devices  107 us (5%)
  other arithmetic  59.4 us (3%)
    psum x15, blocking collectives, row_total(): return lax.psum(values, 'plane')  1860 us
    ppermute x40, starting transfers between devices, from_behind(): lax.ppermute(value, axis, [(source, source + steps) for source in range(f...  122 us
    ppermute x40, waiting for transfers between devices, from_behind(): lax.ppermute(value, axis, [(source, source + steps) for source in range(f...  64.6 us
  transfers between devices with their start and end apart: 41, of which 19 were waited for; matrix products, arithmetic and copies ran while one was open for 3% of the time, Pallas kernels for 0%

commit v1 on v0

v1 whole, which is shorter than its diff:
```python
import jax
import jax.numpy as jnp
import numpy as np
from jax import lax
from jax.experimental import pallas as pl
from jax.experimental.pallas import tpu as pltpu
from jax.sharding import Mesh
from jax.sharding import PartitionSpec as P

FLOW = ("z", "xh")
CROSS = ("xl", "core")
PLANE = ("z", "xh", "xl", "core")
SPREAD = ("z", "xl", "core")
ROWS = ("xh", "y")
SPLIT = (4, 4, 2, 2, 8)

EY = 16
NZ = 32
DT_STEP = 0.01
SPAN_UNIT = 0.5
MASS_SCALE = 0.25
MIB = 1 << 20


def node_tables():
    nodes = np.array(
        [-1.0, -0.830223896278567, -0.468848793470714, 0.0,
         0.468848793470714, 0.830223896278567, 1.0]
    )
    weights = np.array(
        [1.0 / 21.0, 0.276826047361566, 0.431745381209863, 0.487619047619048,
         0.431745381209863, 0.276826047361566, 1.0 / 21.0]
    )
    bary = np.array(
        [1.0 / np.prod([nodes[c] - nodes[o] for o in range(7) if o != c]) for c in range(7)]
    )
    deriv = np.zeros((7, 7))
    for row in range(7):
        for col in range(7):
            if row != col:
                deriv[row, col] = bary[col] / bary[row] / (nodes[row] - nodes[col])
        deriv[row, row] = -np.sum(deriv[row])
    return deriv, weights


DERIV, WEIGHTS = node_tables()
LIFT = 2.0 / WEIGHTS[0]


def span_tables():
    ids = np.arange(NZ)
    harmonic = np.where(ids == 1, NZ // 2, ids // 2)
    sine = (ids % 2 == 1) & (ids != 1)
    phase = 2.0 * np.pi / NZ * (harmonic[:, None] * ids[None, :] % NZ)
    basis = np.where(sine[:, None], np.sin(phase), np.cos(phase))
    basis = basis * np.where(ids < 2, 1.0 / np.sqrt(NZ), np.sqrt(2.0 / NZ))[:, None]
    wavenum = SPAN_UNIT * harmonic
    slope = np.where(ids < 2, 0.0, np.where(sine, -wavenum, wavenum))
    return basis, slope[:, None] * basis[ids ^ 1], wavenum


BASIS, SLOPE, WAVENUM = span_tables()
ROW_AT = np.array([4 * (q % 8) + q // 8 for q in range(NZ)])


def source_coefs():
    table = np.zeros((8, NZ, 3, 4))
    for y in range(8):
        cols = slice(4 * y, 4 * y + 4)
        table[y, :, 0] = BASIS[ROW_AT, cols]
        table[y, :, 1] = -(WAVENUM[ROW_AT] ** 2)[:, None] * BASIS[ROW_AT, cols]
        table[y, :, 2] = 2.0 * SLOPE[ROW_AT, cols]
    return table.astype(np.float32).reshape(-1)


def plane_coefs():
    table = np.stack([BASIS.T[4 * y : 4 * y + 4][:, ROW_AT] for y in range(8)])
    return table.astype(np.float32).reshape(-1)


def line_apply(mat, f):
    even = [f[m] + f[6 - m] for m in range(3)]
    odd = [f[m] - f[6 - m] for m in range(3)]
    out = [None] * 7
    for i in range(3):
        from_odd = float(0.5 * (mat[i, 0] - mat[i, 6])) * odd[0]
        from_even = float(mat[i, 3]) * f[3]
        for m in range(3):
            from_even = from_even + float(0.5 * (mat[i, m] + mat[i, 6 - m])) * even[m]
            if m:
                from_odd = from_odd + float(0.5 * (mat[i, m] - mat[i, 6 - m])) * odd[m]
        out[i] = from_odd + from_even
        out[6 - i] = from_odd - from_even
    out[3] = float(mat[3, 0]) * odd[0] + float(mat[3, 1]) * odd[1] + float(mat[3, 2]) * odd[2]
    return out


def tree_sum(terms):
    while len(terms) > 1:
        terms = [sum(terms[i : i + 2][1:], terms[i]) for i in range(0, len(terms), 2)]
    return terms[0]


def lanes():
    return lax.broadcasted_iota(jnp.int32, (8, 128), 1)


def pack_kernel(s_ref, right_ref, left_ref, up_ref, down_ref, t_ref):
    lane = lanes()
    block, inner = lane // 16, lane % 16

    def plane(z, carry):
        for c in range(6):
            for i in range(7):
                t_ref[c, i, 0:7, :] = s_ref[c, z, i]
        zero = jnp.zeros((8, 128), jnp.float32)
        right, left = zero, zero
        for c in range(6):
            right = jnp.where(block == c, pltpu.roll(t_ref[c, 6], (16 * (c + 1)) % 128, 1), right)
            left = jnp.where(block == c, pltpu.roll(t_ref[c, 0], 16 * c, 1), left)
        right_ref[z] = right
        left_ref[z] = left
        for i in range(7):
            up, down = zero, zero
            for c in range(6):
                up = jnp.where(inner == c, pltpu.roll(t_ref[c, i], (c - 15) % 128, 1), up)
                down = jnp.where(inner == c, pltpu.roll(t_ref[c, i], c, 1), down)
            up_ref[z, i : i + 1, :] = up[6:7, :]
            down_ref[z, i : i + 1, :] = down[0:1, :]
        up_ref[z, 7:8, :] = zero[0:1, :]
        down_ref[z, 7:8, :] = zero[0:1, :]
        return carry

    for c in range(6):
        for i in range(7):
            t_ref[c, i] = jnp.zeros((8, 128), jnp.float32)
    lax.fori_loop(0, 4, plane, 0)


def pack_faces(stress):
    return pl.pallas_call(
        pack_kernel,
        out_shape=[jax.ShapeDtypeStruct((4, 8, 128), jnp.float32)] * 4,
        in_specs=[pl.BlockSpec(memory_space=pltpu.VMEM)],
        out_specs=[pl.BlockSpec(memory_space=pltpu.VMEM)] * 4,
        scratch_shapes=[pltpu.VMEM((6, 7, 8, 128), jnp.float32)],
        compiler_params=pltpu.CompilerParams(vmem_limit_bytes=16 * MIB),
    )(stress)


def stress_kernel(
    coef_ref, s_ref, g_ref, v_ref, left_ref, right_ref, below_ref, above_ref, dcol_ref,
    new_ref, rows_ref, t_ref, d_ref, n_ref, f_ref, p_ref, lb_ref,
):
    lane = lanes()
    inner = lane % 16
    row = lax.broadcasted_iota(jnp.int32, (8, 128), 0)
    twice = 2.0 * DERIV
    y = lax.axis_index("y")

    def across(ref, *at):
        total = dcol_ref[0] * ref[(*at, pl.ds(0, 1), slice(None))]
        for m in range(1, 7):
            total = total + dcol_ref[m] * ref[(*at, pl.ds(m, 1), slice(None))]
        return total

    zero = jnp.zeros((8, 128), jnp.float32)
    for i in range(7):
        for c in range(6):
            t_ref[c, i] = zero
        for c in range(11):
            lb_ref[c, i] = zero

    def plane(z, carry):
        for i in range(7):
            for c in range(6):
                t_ref[c, i, 0:7, :] = s_ref[c, z, i]
            for c in range(9):
                lb_ref[c, i, 0:7, :] = g_ref[c, z, i]
            for c in range(2):
                lb_ref[9 + c, i, 0:7, :] = v_ref[c, z, i]
        for c in range(6):
            slope = line_apply(twice, [t_ref[c, i] for i in range(7)])
            for i in range(7):
                d_ref[c, i] = slope[i]
        for i in range(7):
            u, v = lb_ref[9, i], lb_ref[10, i]
            away = jnp.where(row == 0, -v, v)
            away = jnp.where((row == 0) | (row == 6), jnp.minimum(away, 0.0), 0.0) * float(-LIFT)
            if i == 0:
                along = jnp.minimum(-u, 0.0) * float(-LIFT)
            if i == 6:
                along = jnp.minimum(u, 0.0) * float(-LIFT)
            grad = [lb_ref[c, i] for c in range(9)]
            tau = [t_ref[c, i] for c in range(6)]
            xx, yy, zz = tau[0] + 0.5, tau[1] + 0.5, tau[2] + 0.5
            full = ((xx, tau[3], tau[4]), (tau[3], yy, tau[5]), (tau[4], tau[5], zz))
            prod = [
                [tree_sum([grad[3 * a + k] * full[k][b] for k in range(3)]) for b in range(3)]
                for a in range(3)
            ]
            pairs = ((0, 0), (1, 1), (2, 2), (0, 1), (0, 2), (1, 2))
            for c, (a, b) in enumerate(pairs):
                forcing = prod[a][b] + prod[b][a] - tau[c]
                advect = u * d_ref[c, i] + v * across(t_ref, c, i)
                low = jnp.broadcast_to(t_ref[c, i, 6:7, :], (8, 128))
                low = pltpu.roll(low, 1, 1)
                got = jnp.broadcast_to(below_ref[z, i : i + 1, :], (8, 128))
                low = jnp.where(inner == 0, pltpu.roll(got, (128 - c) % 128, 1), low)
                high = jnp.broadcast_to(t_ref[c, i, 0:1, :], (8, 128))
                high = pltpu.roll(high, 127, 1)
                got = jnp.broadcast_to(above_ref[z, i : i + 1, :], (8, 128))
                high = jnp.where(inner == 15, pltpu.roll(got, 15 - c, 1), high)
                advect = advect + away * (tau[c] - jnp.where(row == 0, low, high))
                if i == 0:
                    mine = pltpu.roll(t_ref[c, 6], 16, 1)
                    got = pltpu.roll(left_ref[z], (128 - 16 * c) % 128, 1)
                    advect = advect + along * (tau[c] - jnp.where(lane < 16, got, mine))
                if i == 6:
                    mine = pltpu.roll(t_ref[c, 0], 112, 1)
                    got = pltpu.roll(right_ref[z], 112 - 16 * c, 1)
                    advect = advect + along * (tau[c] - jnp.where(lane >= 112, got, mine))
                fresh = tau[c] + DT_STEP * (forcing - advect)
                n_ref[c, i] = fresh
                new_ref[c, z, i] = fresh[0:7, :]
        first = line_apply(twice, [n_ref[0, i] for i in range(7)])
        first = [first[i] + across(n_ref, 3, i) for i in range(7)]
        planar = line_apply(twice, first)
        second = line_apply(twice, [n_ref[3, i] for i in range(7)])
        for i in range(7):
            f_ref[i] = second[i] + across(n_ref, 1, i)
        crossed = line_apply(twice, [n_ref[4, i] for i in range(7)])
        for i in range(7):
            p_ref[0, z, i] = planar[i] + across(f_ref, i)
            p_ref[1, z, i] = n_ref[2, i]
            p_ref[2, z, i] = crossed[i] + across(n_ref, 5, i)
        return carry

    lax.fori_loop(0, 4, plane, 0)

    def one_row(q, carry):
        base = (y * NZ + q) * 12
        coefs = [coef_ref[base + k] for k in range(12)]
        for i in range(7):
            rows_ref[q, i] = tree_sum(
                [coefs[4 * s + z] * p_ref[s, z, i] for s in range(3) for z in range(4)]
            )
        return carry

    lax.fori_loop(0, NZ, one_row, 0)


def stress_step(stress, grad, velocity, faces):
    dcol = np.zeros((7, 8, 128))
    dcol[:, :7, :] = 2.0 * DERIV.T[:, :, None]
    vmem = pl.BlockSpec(memory_space=pltpu.VMEM)
    return pl.pallas_call(
        stress_kernel,
        out_shape=[
            jax.ShapeDtypeStruct((6, 4, 7, 7, 128), jnp.float32),
            jax.ShapeDtypeStruct((NZ, 7, 8, 128), jnp.float32),
        ],
        in_specs=[pl.BlockSpec(memory_space=pltpu.SMEM)] + [vmem] * 8,
        out_specs=[vmem] * 2,
        scratch_shapes=[
            pltpu.VMEM((6, 7, 8, 128), jnp.float32),
            pltpu.VMEM((6, 7, 8, 128), jnp.float32),
            pltpu.VMEM((6, 7, 8, 128), jnp.float32),
            pltpu.VMEM((7, 8, 128), jnp.float32),
            pltpu.VMEM((3, 4, 7, 8, 128), jnp.float32),
            pltpu.VMEM((11, 7, 8, 128), jnp.float32),
        ],
        compiler_params=pltpu.CompilerParams(vmem_limit_bytes=24 * MIB),
    )(
        jnp.asarray(source_coefs()), stress, grad, velocity, *faces,
        jnp.asarray(dcol, jnp.float32),
    )


def turn(load, k, i, store):
    block = jnp.stack([load(k, s, i) for s in range(8)])
    block = jnp.swapaxes(block, 0, 1)
    for j in range(7):
        store(i * 7 + j, k, block[j])


def metric_kernel(m_ref, q_ref):
    def chunk(k, carry):
        here = pl.ds(pl.multiple_of(k * 8, 8), 8)
        for c in range(3):
            for i in range(7):
                def load(k, s, i):
                    return m_ref[((k % 2) * 8 + s) * 4 + k // 2, c, i]

                def store(n, k, value):
                    scale = WEIGHTS[n // 7] * WEIGHTS[n % 7] * (MASS_SCALE if c == 2 else 1.0)
                    q_ref[c, n, here, :] = float(scale) * value

                turn(load, k, i, store)
        return carry

    lax.fori_loop(0, 8, chunk, 0)


def metric_fields(gathered):
    vmem = pl.BlockSpec(memory_space=pltpu.VMEM)
    return pl.pallas_call(
        metric_kernel,
        out_shape=jax.ShapeDtypeStruct((3, 49, 64, 128), jnp.float32),
        in_specs=[vmem],
        out_specs=vmem,
        compiler_params=pltpu.CompilerParams(vmem_limit_bytes=24 * MIB),
    )(gathered)


def solve_kernel(count_ref, rows_ref, q_ref, out_ref, r_ref, d_ref, im_ref, mk_ref, x_ref, t_ref):
    z, xh, y = lax.axis_index("z"), lax.axis_index("xh"), lax.axis_index("y")
    e = lax.axis_index("xl") * 2 + lax.axis_index("core")
    row_id = 4 * y + xh
    harmonic = jnp.where(row_id == 1, NZ // 2, row_id // 2).astype(jnp.float32)
    wavesq = harmonic * harmonic * (SPAN_UNIT * SPAN_UNIT)
    own = pl.ds(pl.multiple_of((e * 2 + z // 2) * 8, 8), 8)
    flipped = DERIV.T
    zero = jnp.zeros((8, 128), jnp.float32)

    def here(k):
        return pl.ds(pl.multiple_of(k * 8, 8), 8)

    def chunk_in(k, carry):
        def load(k, s, i):
            return rows_ref[(k % 2) * 2 + s // 4, k // 2, s % 4, i]

        def store(n, k, value):
            mass = q_ref[2, n, here(k), :]
            im_ref[n, here(k), :] = mass * value
            mk_ref[n, here(k), :] = wavesq * mass
            d_ref[n, here(k), :] = zero

        for i in range(7):
            turn(load, k, i, store)
        return carry

    lax.fori_loop(0, 8, chunk_in, 0)
    for n in range(49):
        x_ref[n] = zero

    lane = lax.broadcasted_iota(jnp.int32, (64, 128), 1)
    spot = lax.broadcasted_iota(jnp.int32, (64, 128), 0)
    inner, c_pos = lane % 16, spot % 16
    wall = (
        (c_pos == 0) & (lane < 16),
        (c_pos == 15) & (lane >= 112),
        (spot < 16) & (inner == 0),
        (spot >= 48) & (inner == 15),
    )

    def join():
        for j in range(7):
            low, high = im_ref[j], im_ref[42 + j]
            moved = pltpu.roll(high, 16, 1)
            moved = jnp.where(lane < 16, pltpu.roll(moved, 1, 0), moved)
            back = pltpu.roll(low, 112, 1)
            back = jnp.where(lane >= 112, pltpu.roll(back, 63, 0), back)
            im_ref[j] = jnp.where(wall[0], 0.0, low + moved)
            im_ref[42 + j] = jnp.where(wall[1], 0.0, high + back)
        for i in range(7):
            low, high = im_ref[7 * i], im_ref[7 * i + 6]
            other = pltpu.roll(pltpu.roll(high, 113, 1), 16, 0)
            moved = jnp.where(inner == 0, other, pltpu.roll(high, 1, 1))
            other = pltpu.roll(pltpu.roll(low, 15, 1), 48, 0)
            back = jnp.where(inner == 15, other, pltpu.roll(low, 127, 1))
            im_ref[7 * i] = jnp.where(wall[2], 0.0, low + moved)
            im_ref[7 * i + 6] = jnp.where(wall[3], 0.0, high + back)

    def total(acc):
        return jnp.broadcast_to(jnp.sum(acc, axis=(0, 1), keepdims=True), (8, 128))

    def square(line, ends):
        inside = tree_sum([line[m] * line[m] for m in range(1, 6)])
        return ends * (inside + 0.5 * (line[0] * line[0] + line[6] * line[6]))

    def set_residual(k, acc):
        for i in range(7):
            line = []
            for j in range(7):
                value = im_ref[i * 7 + j, here(k), :]
                r_ref[i * 7 + j, here(k), :] = value
                line.append(value)
            acc = acc + square(line, 0.5 if i in (0, 6) else 1.0)
        return acc

    join()
    rho = total(lax.fori_loop(0, 8, set_residual, zero))

    def sweep(t, state):
        rho, beta = state

        def image(k, acc):
            at = here(k)
            for j in range(7):
                line = []
                for i in range(7):
                    n = i * 7 + j
                    value = r_ref[n, at, :] + beta * d_ref[n, at, :]
                    d_ref[n, at, :] = value
                    line.append(value)
                flux = line_apply(DERIV, line)
                flux = [flux[i] * q_ref[0, i * 7 + j, at, :] for i in range(7)]
                part = line_apply(flipped, flux)
                for i in range(7):
                    n = i * 7 + j
                    part[i] = part[i] + mk_ref[n, at, :] * line[i]
                    im_ref[n, at, :] = part[i]
                acc = acc + tree_sum([part[i] * line[i] for i in range(7)])
            for i in range(7):
                line = [d_ref[i * 7 + j, at, :] for j in range(7)]
                flux = line_apply(DERIV, line)
                flux = [flux[j] * q_ref[1, i * 7 + j, at, :] for j in range(7)]
                part = line_apply(flipped, flux)
                for j in range(7):
                    n = i * 7 + j
                    im_ref[n, at, :] = im_ref[n, at, :] + part[j]
                acc = acc + tree_sum([part[j] * line[j] for j in range(7)])
            return acc

        step = rho / total(lax.fori_loop(0, 8, image, zero))
        join()
        for n in range(49):
            x_ref[n] = x_ref[n] + step * d_ref[n, own, :]

        def descend(k, acc):
            at = here(k)
            for i in range(7):
                line = []
                for j in range(7):
                    n = i * 7 + j
                    value = r_ref[n, at, :] - step * im_ref[n, at, :]
                    r_ref[n, at, :] = value
                    line.append(value)
                acc = acc + square(line, 0.5 if i in (0, 6) else 1.0)
            return acc

        fresh = total(lax.fori_loop(0, 8, descend, zero))
        return fresh, fresh / rho

    lax.fori_loop(0, count_ref[row_id], sweep, (rho, zero))

    for i in range(7):
        block = jnp.stack([x_ref[i * 7 + j] for j in range(7)] + [zero])
        block = jnp.swapaxes(block, 0, 1)
        for s in range(8):
            t_ref[s, i] = block[s]
    first = (z % 2) * 4
    for to in range(4):
        for i in range(7):
            value = t_ref[first + to, i]
            for copy in range(8):
                out_ref[to * 8 + copy, i] = value


def solve(counts, rows, metrics):
    vmem = pl.BlockSpec(memory_space=pltpu.VMEM)
    field = pltpu.VMEM((49, 64, 128), jnp.float32)
    return pl.pallas_call(
        solve_kernel,
        out_shape=jax.ShapeDtypeStruct((NZ, 7, 8, 128), jnp.float32),
        in_specs=[pl.BlockSpec(memory_space=pltpu.SMEM), vmem, vmem],
        out_specs=vmem,
        scratch_shapes=[
            field, field, field, field,
            pltpu.VMEM((49, 8, 128), jnp.float32),
            pltpu.VMEM((8, 7, 8, 128), jnp.float32),
        ],
        compiler_params=pltpu.CompilerParams(vmem_limit_bytes=40 * MIB),
    )(counts, rows, metrics)


def pressure_kernel(coef_ref, rows_ref, out_ref):
    y = lax.axis_index("y")
    for zl in range(4):
        coefs = [coef_ref[(y * 4 + zl) * NZ + q] for q in range(NZ)]
        for i in range(7):
            value = tree_sum([coefs[q] * rows_ref[q, i] for q in range(NZ)])
            out_ref[zl, i] = value[0:7, :]


def pressure_planes(rows):
    vmem = pl.BlockSpec(memory_space=pltpu.VMEM)
    return pl.pallas_call(
        pressure_kernel,
        out_shape=jax.ShapeDtypeStruct((4, 7, 7, 128), jnp.float32),
        in_specs=[pl.BlockSpec(memory_space=pltpu.SMEM), vmem],
        out_specs=vmem,
        compiler_params=pltpu.CompilerParams(vmem_limit_bytes=16 * MIB),
    )(jnp.asarray(plane_coefs()), rows)


def local(stress, velocity_grad, velocity, metric, iteration_counts):
    padded = jnp.pad(metric, ((0, 0), (0, 0), (0, 1), (0, 0)))
    gathered = lax.all_gather(padded, PLANE)
    metrics = metric_fields(gathered)
    right, left, up, down = pack_faces(stress)
    ahead = [(c, c + 1) for c in range(15)]
    above = [(e, e + 1) for e in range(3)]
    faces = (
        lax.ppermute(right, FLOW, ahead),
        lax.ppermute(left, FLOW, [(b, a) for a, b in ahead]),
        lax.ppermute(up, CROSS, above),
        lax.ppermute(down, CROSS, [(b, a) for a, b in above]),
    )
    new_stress, parts = stress_step(stress, velocity_grad, velocity, faces)
    parts = lax.all_to_all(parts, ROWS, 0, 0, tiled=True)
    mine = jnp.sum(parts.reshape(4, 8, 7, 8, 128), axis=1)
    whole = lax.all_gather(mine, SPREAD)
    whole = whole.reshape(4, 4, 4, 7, 8, 128)
    answer = solve(iteration_counts, whole, metrics)
    answer = lax.all_to_all(answer, ROWS, 0, 0, tiled=True)
    return new_stress, pressure_planes(answer)


def solution(mesh):
    fine = Mesh(mesh.devices.reshape(SPLIT), PLANE + ("y",))
    field = P(None, "y", None, None, PLANE)
    return jax.shard_map(
        local,
        mesh=fine,
        in_specs=(field, field, field, P(None, None, None, PLANE), P()),
        out_specs=(field, P("y", None, None, PLANE)),
        check_vma=False,
    )
```

time: 2340 us -> 228 us (0.10)
  the two profiles are of different devices: /device:TPU:256 before, /device:TPU:8 now
where the time goes in v1:
time: 228 us
  waiting for transfers between devices  103 us (45%)
  blocking collectives  39.5 us (17%)
  Pallas kernels  35.1 us (15%)
  starting transfers between devices  18.7 us (8%)
  local copies, waits for them, and re-layouts  16.7 us (7%)
  between operations  14.2 us (6%)
    all_gather x1, waiting for transfers between devices, local(): whole = lax.all_gather(mine, SPREAD)  41.5 us
    all_to_all x1, blocking collectives, local(): parts = lax.all_to_all(parts, ROWS, 0, 0, tiled=True)  39.5 us
    all_gather x1, waiting for transfers between devices, local(): gathered = lax.all_gather(padded, PLANE)  34.4 us
    pallas_call x1, Pallas kernels, solve(): pl.pallas_call(solve_kernel, out_shape=jax.ShapeDtypeStruct((NZ, 7, 8, 12...  28.8 us
    all_to_all x1, waiting for transfers between devices, local(): answer = lax.all_to_all(answer, ROWS, 0, 0, tiled=True)  25.9 us
    unnamed x21, local copies, waits for them, and re-layouts  15.1 us
    all_to_all x1, starting transfers between devices, local(): answer = lax.all_to_all(answer, ROWS, 0, 0, tiled=True)  9.69 us
    ppermute x1, starting transfers between devices, local(): lax.ppermute(right, FLOW, ahead)  4.93 us
  transfers between devices with their start and end apart: 7, of which 4 were waited for; matrix products, arithmetic and copies ran while one was open for 2% of the time, Pallas kernels for 2%

profile of v1, /device:TPU:8, one launch (start us, length us, event | category | flops | bytes accessed | tf_op | source)
XLA Modules:
  0.0 227.5 jit_solution(11666867227572552752)
XLA Ops:
  7.2 1.5 pad.4
  8.8 1.2 copy.17.s_ref
  10.7 4.9 %collective-permute-start = (f32[4,8,128]{2,1,0:T(8,128)S(1)}, f32[4,8,128]{2,1,0:T(8,128)S(1)}, u32[]{:S(2)}, u32[]{:S(2)}) collective-permute-start(f32[4,8,128]{2,1,0:T(8,128)S(1)} %get-tuple-element.8), channel_id=1, source_target_pairs={{0,32},{32,64},{64,96},{96,128},{128,160},{160,192},{192,224},{224... | collective-permute-start | bytes 49160 | tf_op jit(solution)/shard_map/ppermute | solution.py:506
  15.6 1.3 collective-permute-start.1
  16.9 1.5 collective-permute-start.2
  18.4 1.3 collective-permute-start.3
  19.7 1.0 copy.19.v_ref
  20.6 1.3 copy.18.g_ref
  22.0 0.8 collective-permute-done.1.right_ref
  22.8 0.7 copy-done.4
  24.2 3.6 %shard_map.96 = (f32[6,4,7,7,128]{4,3,2,1,0:T(8,128)S(1)}, f32[32,7,8,128]{3,2,1,0:T(8,128)S(1)}) custom-call(f32[3072]{0:T(1024)S(1)} %copy-done.5, f32[6,4,7,7,128]{4,3,2,1,0:T(8,128)S(1)} %copy.17.s_ref, f32[9,4,7,7,128]{4,3,2,1,0:T(8,128)S(1)} %copy.18.g_ref, f32[2,4,7,7,128]{4,3,2,1,0:T(8,128)S(1)} %copy.19.v_ref, ...), custom_call_target="tpu_custom_call" | custom-call | tf_op jit(solution)/shard_map/pallas_call | solution.py:257
  27.8 39.5 %all_to_all.10 = f32[32,7,8,128]{3,2,1,0:T(8,128)S(1)} all-to-all(f32[32,7,8,128]{3,2,1,0:T(8,128)S(1)} %get-tuple-element.13), channel_id=1, replica_groups=mesh['z'=4,'xh'=4,'xl'=2,'core'=2,'y'=8] {'xh','y'}, dimensions={0} | all-to-all | bytes 1835008 | tf_op jit(solution)/shard_map/all_to_all | solution.py:512
  68.0 34.4 %all-gather.7.cloned.1.call-done = f32[192,7,8,128]{3,2,1,0:T(8,128)} async-done(((f32[3,7,8,128]{3,2,1,0:T(8,128)}), f32[192,7,8,128]{3,2,1,0:T(8,128)}) %all-gather.7.cloned.1.call-update) | async-done | bytes 5505040 | tf_op jit(solution)/shard_map/all_gather | solution.py:500
  102.4 2.6 %copy-done.2 = f32[192,7,8,128]{3,2,1,0:T(8,128)S(1)} copy-done((f32[192,7,8,128]{3,2,1,0:T(8,128)S(1)}, f32[192,7,8,128]{3,2,1,0:T(8,128)}, u32[]{:S(2)}) %copy-start.2) | copy-done | bytes 5505048
  105.0 1.2 shard_map.97.q_ref
  106.2 2.2 copy-done
  108.4 41.5 %all-gather.5.cloned.1.call-done = f32[64,7,8,128]{3,2,1,0:T(8,128)} async-done(((f32[4,7,8,128]{3,2,1,0:T(8,128)}), f32[64,7,8,128]{3,2,1,0:T(8,128)}) %all-gather.5.cloned.1.call-update) | async-done | bytes 1835024 | tf_op jit(solution)/shard_map/all_gather | solution.py:514
  149.8 2.4 %copy-done.1 = f32[3,49,64,128]{3,2,1,0:T(8,128)S(1)} copy-done((f32[3,49,64,128]{3,2,1,0:T(8,128)S(1)}, f32[3,49,64,128]{3,2,1,0:T(8,128)}, u32[]{:S(2)}) %copy-start.1) | copy-done | bytes 4816920
  152.2 1.5 copy-done.3
  153.7 28.8 %shard_map.98 = f32[32,7,8,128]{3,2,1,0:T(8,128)} custom-call(s32[32]{0:T(128)S(1)} %copy-done.7, f32[4,4,4,7,8,128]{5,4,3,2,1,0:T(8,128)S(1)} %bitcast.5, f32[3,49,64,128]{3,2,1,0:T(8,128)S(1)} %copy-done.1), custom_call_target="tpu_custom_call" | custom-call | tf_op jit(solution)/shard_map/pallas_call | solution.py:464
  182.5 9.7 %all-to-all-start.1 = ((f32[32,7,8,128]{3,2,1,0:T(8,128)}), f32[32,7,8,128]{3,2,1,0:T(8,128)S(1)}, u32[]{:S(2)}, u32[]{:S(2)}) async-start(f32[32,7,8,128]{3,2,1,0:T(8,128)} %shard_map.98), calls=%async_computation.1 | async-start | bytes 1835008 | tf_op jit(solution)/shard_map/all_to_all | solution.py:517
  192.2 1.0 copy.20
  193.2 25.9 %all-to-all-done.1.rows_ref = f32[32,7,8,128]{3,2,1,0:T(8,128)S(1)} async-done(((f32[32,7,8,128]{3,2,1,0:T(8,128)}), f32[32,7,8,128]{3,2,1,0:T(8,128)S(1)}, u32[]{:S(2)}, u32[]{:S(2)}) %all-to-all-start.1) | async-done | bytes 917536 | tf_op jit(solution)/shard_map/all_to_all | solution.py:517
  219.1 0.9 shard_map.99
  (21 shorter events, 2.9 us)
Async XLA Ops:
  7.2 95.3 %all-gather.7.cloned.1.call-start = ((), (), s32[]{:S(2)}) async-start(), calls=%async_computation.3 | async-start | bytes 5591040 | tf_op jit(solution)/shard_map/all_gather | solution.py:500
  8.8 141.1 %all-gather.5.cloned.1.call-start = ((), (), s32[]{:S(2)}) async-start(), calls=%async_computation.2 | async-start | bytes 1949696 | tf_op jit(solution)/shard_map/all_gather | solution.py:514
  10.7 11.3 %collective-permute-start = (f32[4,8,128]{2,1,0:T(8,128)S(1)}, f32[4,8,128]{2,1,0:T(8,128)S(1)}, u32[]{:S(2)}, u32[]{:S(2)}) collective-permute-start(f32[4,8,128]{2,1,0:T(8,128)S(1)} %get-tuple-element.8), channel_id=1, source_target_pairs={{0,32},{32,64},{64,96},{96,128},{128,160},{160,192},{192,224},{224... | collective-permute-start | bytes 49160 | tf_op jit(solution)/shard_map/ppermute | solution.py:506
  15.6 7.1 %collective-permute-start.1 = (f32[4,8,128]{2,1,0:T(8,128)S(1)}, f32[4,8,128]{2,1,0:T(8,128)S(1)}, u32[]{:S(2)}, u32[]{:S(2)}) collective-permute-start(f32[4,8,128]{2,1,0:T(8,128)S(1)} %get-tuple-element.9), channel_id=1, source_target_pairs={{32,0},{64,32},{96,64},{128,96},{160,128},{192,160},{224,192},{256... | collective-permute-start | bytes 49160 | tf_op jit(solution)/shard_map/ppermute | solution.py:507
  16.9 5.8 %collective-permute-start.2 = (f32[4,8,128]{2,1,0:T(8,128)S(1)}, f32[4,8,128]{2,1,0:T(8,128)S(1)}, u32[]{:S(2)}, u32[]{:S(2)}) collective-permute-start(f32[4,8,128]{2,1,0:T(8,128)S(1)} %get-tuple-element.10), channel_id=1, source_target_pairs={{0,8},{8,16},{16,24},{1,9},{9,17},{17,25},{2,10},{10,18},{18,26},{... | collective-permute-start | bytes 49160 | tf_op jit(solution)/shard_map/ppermute | solution.py:508
  18.4 4.4 %collective-permute-start.3 = (f32[4,8,128]{2,1,0:T(8,128)S(1)}, f32[4,8,128]{2,1,0:T(8,128)S(1)}, u32[]{:S(2)}, u32[]{:S(2)}) collective-permute-start(f32[4,8,128]{2,1,0:T(8,128)S(1)} %get-tuple-element.11), channel_id=1, source_target_pairs={{8,0},{16,8},{24,16},{9,1},{17,9},{25,17},{10,2},{18,10},{26,18},{... | collective-permute-start | bytes 49160 | tf_op jit(solution)/shard_map/ppermute | solution.py:509
  22.8 0.8 copy-start.4
  23.5 0.7 copy-start.5
  102.4 2.6 %copy-start.2 = (f32[192,7,8,128]{3,2,1,0:T(8,128)S(1)}, f32[192,7,8,128]{3,2,1,0:T(8,128)}, u32[]{:S(2)}) copy-start(f32[192,7,8,128]{3,2,1,0:T(8,128)} %all-gather.7.cloned.1.call-done) | copy-start | bytes 16515076
  105.0 44.8 %copy-start.7 = (s32[32]{0:T(128)S(1)}, s32[32]{0:T(128)}, u32[]{:S(2)}) copy-start(s32[32]{0:T(128)} %count_ref.1) | copy-start | bytes 388
  106.2 2.2 copy-start
  149.8 2.4 %copy-start.1 = (f32[3,49,64,128]{3,2,1,0:T(8,128)S(1)}, f32[3,49,64,128]{3,2,1,0:T(8,128)}, u32[]{:S(2)}) copy-start(f32[3,49,64,128]{3,2,1,0:T(8,128)} %copy-done) | copy-start | bytes 14450692
  152.2 1.5 copy-start.3
  153.7 65.5 %copy-start.6 = (f32[1024]{0:T(1024)S(1)}, f32[1024]{0:T(1024)}, u32[]{:S(2)}) copy-start(f32[1024]{0:T(1024)} %constant.12.clone.coef_ref) | copy-start | bytes 12292
  182.5 36.6 %all-to-all-start.1 = ((f32[32,7,8,128]{3,2,1,0:T(8,128)}), f32[32,7,8,128]{3,2,1,0:T(8,128)S(1)}, u32[]{:S(2)}, u32[]{:S(2)}) async-start(f32[32,7,8,128]{3,2,1,0:T(8,128)} %shard_map.98), calls=%async_computation.1 | async-start | bytes 1835008 | tf_op jit(solution)/shard_map/all_to_all | solution.py:517
Sparse Core Ops, SparseCore 0:
  11.8 90.5 all-gather.6
  105.2 44.6 all-gather.4

commit v2 on v1

--- a/solution.py
+++ b/solution.py
@@ -277,26 +277,18 @@
     )
 
 
-def turn(load, k, i, store):
-    block = jnp.stack([load(k, s, i) for s in range(8)])
-    block = jnp.swapaxes(block, 0, 1)
-    for j in range(7):
-        store(i * 7 + j, k, block[j])
-
-
 def metric_kernel(m_ref, q_ref):
     def chunk(k, carry):
         here = pl.ds(pl.multiple_of(k * 8, 8), 8)
-        for c in range(3):
-            for i in range(7):
-                def load(k, s, i):
-                    return m_ref[((k % 2) * 8 + s) * 4 + k // 2, c, i]
-
-                def store(n, k, value):
+        source = [((k % 2) * 8 + s) * 4 + k // 2 for s in range(8)]
+        for tile in range(19):
+            block = jnp.stack([m_ref[at, 8 * tile : 8 * tile + 8, :] for at in source])
+            block = jnp.swapaxes(block, 0, 1)
+            for j in range(8):
+                c, n = divmod(8 * tile + j, 49)
+                if c < 3:
                     scale = WEIGHTS[n // 7] * WEIGHTS[n % 7] * (MASS_SCALE if c == 2 else 1.0)
-                    q_ref[c, n, here, :] = float(scale) * value
-
-                turn(load, k, i, store)
+                    q_ref[c, n, here, :] = float(scale) * block[j]
         return carry
 
     lax.fori_loop(0, 8, chunk, 0)
@@ -313,9 +305,12 @@
     )(gathered)
 
 
-def solve_kernel(count_ref, rows_ref, q_ref, out_ref, r_ref, d_ref, im_ref, mk_ref, x_ref, t_ref):
+def solve_kernel(
+    count_ref, same_ref, other_ref, q_ref, out_ref, r_ref, d_ref, im_ref, mk_ref, x_ref, t_ref
+):
     z, xh, y = lax.axis_index("z"), lax.axis_index("xh"), lax.axis_index("y")
-    e = lax.axis_index("xl") * 2 + lax.axis_index("core")
+    xl, core = lax.axis_index("xl"), lax.axis_index("core")
+    e = xl * 2 + core
     row_id = 4 * y + xh
     harmonic = jnp.where(row_id == 1, NZ // 2, row_id // 2).astype(jnp.float32)
     wavesq = harmonic * harmonic * (SPAN_UNIT * SPAN_UNIT)
@@ -326,21 +321,24 @@
     def here(k):
         return pl.ds(pl.multiple_of(k * 8, 8), 8)
 
-    def chunk_in(k, carry):
-        def load(k, s, i):
-            return rows_ref[(k % 2) * 2 + s // 4, k // 2, s % 4, i]
-
-        def store(n, k, value):
-            mass = q_ref[2, n, here(k), :]
-            im_ref[n, here(k), :] = mass * value
-            mk_ref[n, here(k), :] = wavesq * mass
-            d_ref[n, here(k), :] = zero
-
-        for i in range(7):
-            turn(load, k, i, store)
+    def chunk_in(quarter, carry):
+        from_xl, half = quarter // 2, quarter % 2
+        for ref, from_core in ((same_ref, core), (other_ref, 1 - core)):
+            at = here((from_xl * 2 + from_core) * 2 + half)
+            flip = (xl + from_xl) % 2
+            back = [(z - half * 2 - s + 4) % 4 for s in range(2)]
+            for i in range(7):
+                block = jnp.stack([ref[flip, back[s // 4], s % 4, i] for s in range(8)])
+                block = jnp.swapaxes(block, 0, 1)
+                for j in range(7):
+                    n = i * 7 + j
+                    mass = q_ref[2, n, at, :]
+                    im_ref[n, at, :] = mass * block[j]
+                    mk_ref[n, at, :] = wavesq * mass
+                    d_ref[n, at, :] = zero
         return carry
 
-    lax.fori_loop(0, 8, chunk_in, 0)
+    lax.fori_loop(0, 4, chunk_in, 0)
     for n in range(49):
         x_ref[n] = zero
 
@@ -458,13 +456,13 @@
                 out_ref[to * 8 + copy, i] = value
 
 
-def solve(counts, rows, metrics):
+def solve(counts, same, other, metrics):
     vmem = pl.BlockSpec(memory_space=pltpu.VMEM)
     field = pltpu.VMEM((49, 64, 128), jnp.float32)
     return pl.pallas_call(
         solve_kernel,
         out_shape=jax.ShapeDtypeStruct((NZ, 7, 8, 128), jnp.float32),
-        in_specs=[pl.BlockSpec(memory_space=pltpu.SMEM), vmem, vmem],
+        in_specs=[pl.BlockSpec(memory_space=pltpu.SMEM)] + [vmem] * 3,
         out_specs=vmem,
         scratch_shapes=[
             field, field, field, field,
@@ -472,7 +470,7 @@
             pltpu.VMEM((8, 7, 8, 128), jnp.float32),
         ],
         compiler_params=pltpu.CompilerParams(vmem_limit_bytes=40 * MIB),
-    )(counts, rows, metrics)
+    )(counts, same, other, metrics)
 
 
 def pressure_kernel(coef_ref, rows_ref, out_ref):
@@ -495,9 +493,19 @@
     )(jnp.asarray(plane_coefs()), rows)
 
 
+def gather_row(mine):
+    swap = [(0, 1), (1, 0)]
+    turns = [[(z, (z + back) % 4) for z in range(4)] for back in range(1, 4)]
+    beside = lax.ppermute(mine, "xl", swap)
+    pieces = [mine] + [lax.ppermute(mine, "z", turn) for turn in turns]
+    pieces += [beside] + [lax.ppermute(beside, "z", turn) for turn in turns]
+    same = jnp.stack(pieces).reshape(2, 4, 4, 7, 8, 128)
+    return same, lax.ppermute(same, "core", swap)
+
+
 def local(stress, velocity_grad, velocity, metric, iteration_counts):
-    padded = jnp.pad(metric, ((0, 0), (0, 0), (0, 1), (0, 0)))
-    gathered = lax.all_gather(padded, PLANE)
+    packed = jnp.pad(metric.reshape(147, 128), ((0, 5), (0, 0)))
+    gathered = lax.all_gather(packed, PLANE)
     metrics = metric_fields(gathered)
     right, left, up, down = pack_faces(stress)
     ahead = [(c, c + 1) for c in range(15)]
@@ -511,9 +519,8 @@
     new_stress, parts = stress_step(stress, velocity_grad, velocity, faces)
     parts = lax.all_to_all(parts, ROWS, 0, 0, tiled=True)
     mine = jnp.sum(parts.reshape(4, 8, 7, 8, 128), axis=1)
-    whole = lax.all_gather(mine, SPREAD)
-    whole = whole.reshape(4, 4, 4, 7, 8, 128)
-    answer = solve(iteration_counts, whole, metrics)
+    same, other = gather_row(mine)
+    answer = solve(iteration_counts, same, other, metrics)
     answer = lax.all_to_all(answer, ROWS, 0, 0, tiled=True)
     return new_stress, pressure_planes(answer)
 

time: 228 us -> 192 us (0.84)
  waiting for transfers between devices: 103 us -> 36.3 us
  starting transfers between devices: 18.7 us -> 55.2 us
  local copies, waits for them, and re-layouts: 16.7 us -> 10.6 us
    all_gather x2 -> x1, waiting for transfers between devices: 75.9 us -> 0.02 us  [local(): gathered = lax.all_gather(packed, PLANE)]
    ppermute x0 -> x8, starting transfers between devices: none -> 36.6 us  [the longest x3 16.8 us: gather_row(): pieces = [mine] + [lax.ppermute(mine, 'z', turn) for turn in turns]]
    ppermute x0 -> x8, waiting for transfers between devices: none -> 9.53 us  [the longest x3 9.51 us: gather_row(): pieces += [beside] + [lax.ppermute(beside, 'z', turn) for turn in turns]]
    unnamed x21 -> x22, local copies, waits for them, and re-layouts: 15.1 us -> 9.03 us
  transfers between devices with their start and end apart: 7 -> 14, of which waited for: 4 -> 3; matrix products, arithmetic and copies ran while one was open for 2% -> 2% of each run, Pallas kernels for 2% -> 3%
where the time goes in v2:
time: 192 us; the launch traced here: 191 us
  starting transfers between devices  55.2 us (29%)
  blocking collectives  39.5 us (21%)
  waiting for transfers between devices  36.3 us (19%)
  Pallas kernels  35.1 us (18%)
  between operations  14.3 us (7%)
  local copies, waits for them, and re-layouts  10.6 us (6%)
    all_to_all x1, blocking collectives, local(): parts = lax.all_to_all(parts, ROWS, 0, 0, tiled=True)  39.5 us
    pallas_call x1, Pallas kernels, solve(): pl.pallas_call(solve_kernel, out_shape=jax.ShapeDtypeStruct((NZ, 7, 8, 12...  28.9 us
    all_to_all x1, waiting for transfers between devices, local(): answer = lax.all_to_all(answer, ROWS, 0, 0, tiled=True)  25.9 us
    ppermute x3, starting transfers between devices, gather_row(): pieces = [mine] + [lax.ppermute(mine, 'z', turn) for turn in turns]  16.8 us
    ppermute x3, starting transfers between devices, gather_row(): pieces += [beside] + [lax.ppermute(beside, 'z', turn) for turn in turns]  14.6 us
    all_to_all x1, starting transfers between devices, local(): answer = lax.all_to_all(answer, ROWS, 0, 0, tiled=True)  9.59 us
    ppermute x3, waiting for transfers between devices, gather_row(): pieces += [beside] + [lax.ppermute(beside, 'z', turn) for turn in turns]  9.51 us
    unnamed x22, local copies, waits for them, and re-layouts  9.03 us
  transfers between devices with their start and end apart: 14, of which 3 were waited for; matrix products, arithmetic and copies ran while one was open for 2% of the time, Pallas kernels for 3%

profile of v2, /device:TPU:8, one launch (start us, length us, event | category | flops | bytes accessed | tf_op | source)
XLA Modules:
  0.0 191.1 jit_solution(18265625293916630346)
XLA Ops:
  8.8 1.2 copy.11.s_ref
  10.6 4.9 %collective-permute-start = (f32[4,8,128]{2,1,0:T(8,128)S(1)}, f32[4,8,128]{2,1,0:T(8,128)S(1)}, u32[]{:S(2)}, u32[]{:S(2)}) collective-permute-start(f32[4,8,128]{2,1,0:T(8,128)S(1)} %get-tuple-element.8), channel_id=1, source_target_pairs={{0,32},{32,64},{64,96},{96,128},{128,160},{160,192},{192,224},{224... | collective-permute-start | bytes 49160 | tf_op jit(solution)/shard_map/ppermute | solution.py:514
  15.6 1.3 collective-permute-start.1
  16.9 1.5 collective-permute-start.2
  18.3 1.3 collective-permute-start.3
  19.6 1.0 copy.13.v_ref
  20.6 1.3 copy.12.g_ref
  24.2 3.6 %shard_map.96 = (f32[6,4,7,7,128]{4,3,2,1,0:T(8,128)S(1)}, f32[32,7,8,128]{3,2,1,0:T(8,128)S(1)}) custom-call(f32[3072]{0:T(1024)S(1)} %copy-done.2, f32[6,4,7,7,128]{4,3,2,1,0:T(8,128)S(1)} %copy.11.s_ref, f32[9,4,7,7,128]{4,3,2,1,0:T(8,128)S(1)} %copy.12.g_ref, f32[2,4,7,7,128]{4,3,2,1,0:T(8,128)S(1)} %copy.13.v_ref, ...), custom_call_target="tpu_custom_call" | custom-call | tf_op jit(solution)/shard_map/pallas_call | solution.py:257
  27.7 39.5 %all_to_all.10 = f32[32,7,8,128]{3,2,1,0:T(8,128)S(1)} all-to-all(f32[32,7,8,128]{3,2,1,0:T(8,128)S(1)} %get-tuple-element.13), channel_id=1, replica_groups=mesh['z'=4,'xh'=4,'xl'=2,'core'=2,'y'=8] {'xh','y'}, dimensions={0} | all-to-all | bytes 1835008 | tf_op jit(solution)/shard_map/all_to_all | solution.py:520
  67.3 3.3 %collective-permute-start.7 = (f32[4,7,8,128]{3,2,1,0:T(8,128)S(1)}, f32[4,7,8,128]{3,2,1,0:T(8,128)S(1)}, u32[]{:S(2)}, u32[]{:S(2)}) collective-permute-start(f32[4,7,8,128]{3,2,1,0:T(8,128)S(1)} %bitcast_reduce_fusion), channel_id=1, source_target_pairs={{0,16},{16,0},{1,17},{17,1},{2,18},{18,2},{3,19},{19,3},{4,20},{20... | collective-permute-start | bytes 344072 | tf_op jit(solution)/shard_map/ppermute | solution.py:499
  70.6 10.0 %collective-permute-start.6 = (f32[4,7,8,128]{3,2,1,0:T(8,128)S(1)}, f32[4,7,8,128]{3,2,1,0:T(8,128)S(1)}, u32[]{:S(2)}, u32[]{:S(2)}) collective-permute-start(f32[4,7,8,128]{3,2,1,0:T(8,128)S(1)} %bitcast_reduce_fusion), channel_id=1, source_target_pairs={{0,384},{128,0},{256,128},{384,256},{1,385},{129,1},{257,129},{385... | collective-permute-start | bytes 344072 | tf_op jit(solution)/shard_map/ppermute | solution.py:500
  80.6 2.5 %collective-permute-start.5 = (f32[4,7,8,128]{3,2,1,0:T(8,128)S(1)}, f32[4,7,8,128]{3,2,1,0:T(8,128)S(1)}, u32[]{:S(2)}, u32[]{:S(2)}) collective-permute-start(f32[4,7,8,128]{3,2,1,0:T(8,128)S(1)} %bitcast_reduce_fusion), channel_id=1, source_target_pairs={{0,256},{128,384},{256,0},{384,128},{1,257},{129,385},{257,1},{385... | collective-permute-start | bytes 344072 | tf_op jit(solution)/shard_map/ppermute | solution.py:500
  83.1 4.2 %collective-permute-start.4 = (f32[4,7,8,128]{3,2,1,0:T(8,128)S(1)}, f32[4,7,8,128]{3,2,1,0:T(8,128)S(1)}, u32[]{:S(2)}, u32[]{:S(2)}) collective-permute-start(f32[4,7,8,128]{3,2,1,0:T(8,128)S(1)} %bitcast_reduce_fusion), channel_id=1, source_target_pairs={{0,128},{128,256},{256,384},{384,0},{1,129},{129,257},{257,385},{3... | collective-permute-start | bytes 344072 | tf_op jit(solution)/shard_map/ppermute | solution.py:500
  87.4 3.7 %collective-permute-start.10 = (f32[4,7,8,128]{3,2,1,0:T(8,128)S(1)}, f32[4,7,8,128]{3,2,1,0:T(8,128)S(1)}, u32[]{:S(2)}, u32[]{:S(2)}) collective-permute-start(f32[4,7,8,128]{3,2,1,0:T(8,128)S(1)} %collective-permute-done.7), channel_id=1, source_target_pairs={{0,384},{128,0},{256,128},{384,256},{1,385},{129,1},{257,129},{385... | collective-permute-start | bytes 344072 | tf_op jit(solution)/shard_map/ppermute | solution.py:501
  91.1 7.3 %collective-permute-start.9 = (f32[4,7,8,128]{3,2,1,0:T(8,128)S(1)}, f32[4,7,8,128]{3,2,1,0:T(8,128)S(1)}, u32[]{:S(2)}, u32[]{:S(2)}) collective-permute-start(f32[4,7,8,128]{3,2,1,0:T(8,128)S(1)} %collective-permute-done.7), channel_id=1, source_target_pairs={{0,256},{128,384},{256,0},{384,128},{1,257},{129,385},{257,1},{385... | collective-permute-start | bytes 344072 | tf_op jit(solution)/shard_map/ppermute | solution.py:501
  98.4 3.6 %collective-permute-start.8 = (f32[4,7,8,128]{3,2,1,0:T(8,128)S(1)}, f32[4,7,8,128]{3,2,1,0:T(8,128)S(1)}, u32[]{:S(2)}, u32[]{:S(2)}) collective-permute-start(f32[4,7,8,128]{3,2,1,0:T(8,128)S(1)} %collective-permute-done.7), channel_id=1, source_target_pairs={{0,128},{128,256},{256,384},{384,0},{1,129},{129,257},{257,385},{3... | collective-permute-start | bytes 344072 | tf_op jit(solution)/shard_map/ppermute | solution.py:501
  102.2 9.5 %collective-permute-done.8 = f32[4,7,8,128]{3,2,1,0:T(8,128)S(1)} collective-permute-done((f32[4,7,8,128]{3,2,1,0:T(8,128)S(1)}, f32[4,7,8,128]{3,2,1,0:T(8,128)S(1)}, u32[]{:S(2)}, u32[]{:S(2)}) %collective-permute-start.8) | collective-permute-done | bytes 114720 | tf_op jit(solution)/shard_map/ppermute | solution.py:501
  111.7 1.9 %collective-permute-start.11 = (f32[2,4,4,7,8,128]{5,4,3,2,1,0:T(8,128)S(1)}, f32[2,4,4,7,8,128]{5,4,3,2,1,0:T(8,128)S(1)}, u32[]{:S(2)}, u32[]{:S(2)}) collective-permute-start(f32[2,4,4,7,8,128]{5,4,3,2,1,0:T(8,128)S(1)} %bitcast.21), channel_id=1, source_target_pairs={{0,8},{8,0},{1,9},{9,1},{2,10},{10,2},{3,11},{11,3},{4,12},{12,4},... | collective-permute-start | bytes 2752520 | tf_op jit(solution)/shard_map/ppermute | solution.py:503
  113.7 2.4 %copy-done = f32[9728,128]{1,0:T(8,128)S(1)} copy-done((f32[9728,128]{1,0:T(8,128)S(1)}, f32[9728,128]{1,0:T(8,128)}, u32[]{:S(2)}) %copy-start) | copy-done | bytes 4980760
  116.1 1.1 shard_map.97.q_ref
  117.3 28.9 %shard_map.98 = f32[32,7,8,128]{3,2,1,0:T(8,128)} custom-call(s32[32]{0:T(128)S(1)} %copy-done.4, f32[2,4,4,7,8,128]{5,4,3,2,1,0:T(8,128)S(1)} %bitcast.22, f32[2,4,4,7,8,128]{5,4,3,2,1,0:T(8,128)S(1)} %collective-permute-done.11.other_ref, f32[3,49,64,128]{3,2,1,0:T(8,128)S(1)} %shard_map.97.q_ref), custom_call_target="tpu_custom_call" | custom-call | tf_op jit(solution)/shard_map/pallas_call | solution.py:462
  146.2 9.6 %all-to-all-start.1 = ((f32[32,7,8,128]{3,2,1,0:T(8,128)}), f32[32,7,8,128]{3,2,1,0:T(8,128)S(1)}, u32[]{:S(2)}, u32[]{:S(2)}) async-start(f32[32,7,8,128]{3,2,1,0:T(8,128)} %shard_map.98), calls=%async_computation.1 | async-start | bytes 1835008 | tf_op jit(solution)/shard_map/all_to_all | solution.py:524
  155.8 1.0 copy.14
  156.7 25.9 %all-to-all-done.1.rows_ref = f32[32,7,8,128]{3,2,1,0:T(8,128)S(1)} async-done(((f32[32,7,8,128]{3,2,1,0:T(8,128)}), f32[32,7,8,128]{3,2,1,0:T(8,128)S(1)}, u32[]{:S(2)}, u32[]{:S(2)}) %all-to-all-start.1) | async-done | bytes 917536 | tf_op jit(solution)/shard_map/all_to_all | solution.py:524
  (37 shorter events, 6.2 us)
Async XLA Ops:
  7.2 106.5 %all-gather.3.cloned.1.call-start = ((), (), s32[]{:S(2)}) async-start(), calls=%async_computation.2 | async-start | bytes 5058560 | tf_op jit(solution)/shard_map/all_gather | solution.py:508
  10.6 11.3 %collective-permute-start = (f32[4,8,128]{2,1,0:T(8,128)S(1)}, f32[4,8,128]{2,1,0:T(8,128)S(1)}, u32[]{:S(2)}, u32[]{:S(2)}) collective-permute-start(f32[4,8,128]{2,1,0:T(8,128)S(1)} %get-tuple-element.8), channel_id=1, source_target_pairs={{0,32},{32,64},{64,96},{96,128},{128,160},{160,192},{192,224},{224... | collective-permute-start | bytes 49160 | tf_op jit(solution)/shard_map/ppermute | solution.py:514
  15.6 7.1 %collective-permute-start.1 = (f32[4,8,128]{2,1,0:T(8,128)S(1)}, f32[4,8,128]{2,1,0:T(8,128)S(1)}, u32[]{:S(2)}, u32[]{:S(2)}) collective-permute-start(f32[4,8,128]{2,1,0:T(8,128)S(1)} %get-tuple-element.9), channel_id=1, source_target_pairs={{32,0},{64,32},{96,64},{128,96},{160,128},{192,160},{224,192},{256... | collective-permute-start | bytes 49160 | tf_op jit(solution)/shard_map/ppermute | solution.py:515
  16.9 5.8 %collective-permute-start.2 = (f32[4,8,128]{2,1,0:T(8,128)S(1)}, f32[4,8,128]{2,1,0:T(8,128)S(1)}, u32[]{:S(2)}, u32[]{:S(2)}) collective-permute-start(f32[4,8,128]{2,1,0:T(8,128)S(1)} %get-tuple-element.10), channel_id=1, source_target_pairs={{0,8},{8,16},{16,24},{1,9},{9,17},{17,25},{2,10},{10,18},{18,26},{... | collective-permute-start | bytes 49160 | tf_op jit(solution)/shard_map/ppermute | solution.py:516
  18.3 4.4 %collective-permute-start.3 = (f32[4,8,128]{2,1,0:T(8,128)S(1)}, f32[4,8,128]{2,1,0:T(8,128)S(1)}, u32[]{:S(2)}, u32[]{:S(2)}) collective-permute-start(f32[4,8,128]{2,1,0:T(8,128)S(1)} %get-tuple-element.11), channel_id=1, source_target_pairs={{8,0},{16,8},{24,16},{9,1},{17,9},{25,17},{10,2},{18,10},{26,18},{... | collective-permute-start | bytes 49160 | tf_op jit(solution)/shard_map/ppermute | solution.py:517
  22.7 0.8 copy-start.1
  23.5 0.7 copy-start.2
  67.3 20.1 %collective-permute-start.7 = (f32[4,7,8,128]{3,2,1,0:T(8,128)S(1)}, f32[4,7,8,128]{3,2,1,0:T(8,128)S(1)}, u32[]{:S(2)}, u32[]{:S(2)}) collective-permute-start(f32[4,7,8,128]{3,2,1,0:T(8,128)S(1)} %bitcast_reduce_fusion), channel_id=1, source_target_pairs={{0,16},{16,0},{1,17},{17,1},{2,18},{18,2},{3,19},{19,3},{4,20},{20... | collective-permute-start | bytes 344072 | tf_op jit(solution)/shard_map/ppermute | solution.py:499
  70.6 31.5 %collective-permute-start.6 = (f32[4,7,8,128]{3,2,1,0:T(8,128)S(1)}, f32[4,7,8,128]{3,2,1,0:T(8,128)S(1)}, u32[]{:S(2)}, u32[]{:S(2)}) collective-permute-start(f32[4,7,8,128]{3,2,1,0:T(8,128)S(1)} %bitcast_reduce_fusion), channel_id=1, source_target_pairs={{0,384},{128,0},{256,128},{384,256},{1,385},{129,1},{257,129},{385... | collective-permute-start | bytes 344072 | tf_op jit(solution)/shard_map/ppermute | solution.py:500
  80.6 21.4 %collective-permute-start.5 = (f32[4,7,8,128]{3,2,1,0:T(8,128)S(1)}, f32[4,7,8,128]{3,2,1,0:T(8,128)S(1)}, u32[]{:S(2)}, u32[]{:S(2)}) collective-permute-start(f32[4,7,8,128]{3,2,1,0:T(8,128)S(1)} %bitcast_reduce_fusion), channel_id=1, source_target_pairs={{0,256},{128,384},{256,0},{384,128},{1,257},{129,385},{257,1},{385... | collective-permute-start | bytes 344072 | tf_op jit(solution)/shard_map/ppermute | solution.py:500
  83.1 15.3 %collective-permute-start.4 = (f32[4,7,8,128]{3,2,1,0:T(8,128)S(1)}, f32[4,7,8,128]{3,2,1,0:T(8,128)S(1)}, u32[]{:S(2)}, u32[]{:S(2)}) collective-permute-start(f32[4,7,8,128]{3,2,1,0:T(8,128)S(1)} %bitcast_reduce_fusion), channel_id=1, source_target_pairs={{0,128},{128,256},{256,384},{384,0},{1,129},{129,257},{257,385},{3... | collective-permute-start | bytes 344072 | tf_op jit(solution)/shard_map/ppermute | solution.py:500
  87.4 24.3 %collective-permute-start.10 = (f32[4,7,8,128]{3,2,1,0:T(8,128)S(1)}, f32[4,7,8,128]{3,2,1,0:T(8,128)S(1)}, u32[]{:S(2)}, u32[]{:S(2)}) collective-permute-start(f32[4,7,8,128]{3,2,1,0:T(8,128)S(1)} %collective-permute-done.7), channel_id=1, source_target_pairs={{0,384},{128,0},{256,128},{384,256},{1,385},{129,1},{257,129},{385... | collective-permute-start | bytes 344072 | tf_op jit(solution)/shard_map/ppermute | solution.py:501
  91.1 20.6 %collective-permute-start.9 = (f32[4,7,8,128]{3,2,1,0:T(8,128)S(1)}, f32[4,7,8,128]{3,2,1,0:T(8,128)S(1)}, u32[]{:S(2)}, u32[]{:S(2)}) collective-permute-start(f32[4,7,8,128]{3,2,1,0:T(8,128)S(1)} %collective-permute-done.7), channel_id=1, source_target_pairs={{0,256},{128,384},{256,0},{384,128},{1,257},{129,385},{257,1},{385... | collective-permute-start | bytes 344072 | tf_op jit(solution)/shard_map/ppermute | solution.py:501
  98.4 13.2 %collective-permute-start.8 = (f32[4,7,8,128]{3,2,1,0:T(8,128)S(1)}, f32[4,7,8,128]{3,2,1,0:T(8,128)S(1)}, u32[]{:S(2)}, u32[]{:S(2)}) collective-permute-start(f32[4,7,8,128]{3,2,1,0:T(8,128)S(1)} %collective-permute-done.7), channel_id=1, source_target_pairs={{0,128},{128,256},{256,384},{384,0},{1,129},{129,257},{257,385},{3... | collective-permute-start | bytes 344072 | tf_op jit(solution)/shard_map/ppermute | solution.py:501
  111.7 5.6 %copy-start.4 = (s32[32]{0:T(128)S(1)}, s32[32]{0:T(128)}, u32[]{:S(2)}) copy-start(s32[32]{0:T(128)} %count_ref.1) | copy-start | bytes 388
  111.7 5.5 %collective-permute-start.11 = (f32[2,4,4,7,8,128]{5,4,3,2,1,0:T(8,128)S(1)}, f32[2,4,4,7,8,128]{5,4,3,2,1,0:T(8,128)S(1)}, u32[]{:S(2)}, u32[]{:S(2)}) collective-permute-start(f32[2,4,4,7,8,128]{5,4,3,2,1,0:T(8,128)S(1)} %bitcast.21), channel_id=1, source_target_pairs={{0,8},{8,0},{1,9},{9,1},{2,10},{10,2},{3,11},{11,3},{4,12},{12,4},... | collective-permute-start | bytes 2752520 | tf_op jit(solution)/shard_map/ppermute | solution.py:503
  113.7 2.4 %copy-start = (f32[9728,128]{1,0:T(8,128)S(1)}, f32[9728,128]{1,0:T(8,128)}, u32[]{:S(2)}) copy-start(f32[9728,128]{1,0:T(8,128)} %all-gather.3.cloned.1.call-done) | copy-start | bytes 14942212
  117.2 65.5 %copy-start.3 = (f32[1024]{0:T(1024)S(1)}, f32[1024]{0:T(1024)}, u32[]{:S(2)}) copy-start(f32[1024]{0:T(1024)} %constant.12.clone.coef_ref) | copy-start | bytes 12292
  146.2 36.5 %all-to-all-start.1 = ((f32[32,7,8,128]{3,2,1,0:T(8,128)}), f32[32,7,8,128]{3,2,1,0:T(8,128)S(1)}, u32[]{:S(2)}, u32[]{:S(2)}) async-start(f32[32,7,8,128]{3,2,1,0:T(8,128)} %shard_map.98), calls=%async_computation.1 | async-start | bytes 1835008 | tf_op jit(solution)/shard_map/all_to_all | solution.py:524
Sparse Core Ops, SparseCore 0:
  11.8 100.2 all-gather.2

commit v3 on v2

--- a/solution.py
+++ b/solution.py
@@ -10,7 +10,6 @@
 FLOW = ("z", "xh")
 CROSS = ("xl", "core")
 PLANE = ("z", "xh", "xl", "core")
-SPREAD = ("z", "xl", "core")
 ROWS = ("xh", "y")
 SPLIT = (4, 4, 2, 2, 8)
 
@@ -277,32 +276,43 @@
     )
 
 
-def metric_kernel(m_ref, q_ref):
-    def chunk(k, carry):
-        here = pl.ds(pl.multiple_of(k * 8, 8), 8)
-        source = [((k % 2) * 8 + s) * 4 + k // 2 for s in range(8)]
-        for tile in range(19):
-            block = jnp.stack([m_ref[at, 8 * tile : 8 * tile + 8, :] for at in source])
-            block = jnp.swapaxes(block, 0, 1)
-            for j in range(8):
-                c, n = divmod(8 * tile + j, 49)
-                if c < 3:
-                    scale = WEIGHTS[n // 7] * WEIGHTS[n % 7] * (MASS_SCALE if c == 2 else 1.0)
-                    q_ref[c, n, here, :] = float(scale) * block[j]
+def metric_kernel(same_ref, other_ref, q_ref):
+    z, xh = lax.axis_index("z"), lax.axis_index("xh")
+    xl, core = lax.axis_index("xl"), lax.axis_index("core")
+
+    def chunk(quarter, carry):
+        from_xl, half = quarter // 2, quarter % 2
+        flip = (xl + from_xl) % 2
+        back_z = [(z - half * 2 - s + 4) % 4 for s in range(2)]
+        back_h = [(xh - s + 4) % 4 for s in range(4)]
+        for ref, from_core in ((same_ref, core), (other_ref, 1 - core)):
+            start = ((from_xl * 2 + from_core) * 2 + half) * 8
+            here = pl.ds(pl.multiple_of(start, 8), 8)
+            for tile in range(19):
+                rows = slice(8 * tile, 8 * tile + 8)
+                block = jnp.stack(
+                    [ref[back_z[s // 4], back_h[s % 4], flip, rows, :] for s in range(8)]
+                )
+                block = jnp.swapaxes(block, 0, 1)
+                for j in range(8):
+                    c, n = divmod(8 * tile + j, 49)
+                    if c < 3:
+                        scale = WEIGHTS[n // 7] * WEIGHTS[n % 7] * (MASS_SCALE if c == 2 else 1.0)
+                        q_ref[c, n, here, :] = float(scale) * block[j]
         return carry
 
-    lax.fori_loop(0, 8, chunk, 0)
-
-
-def metric_fields(gathered):
+    lax.fori_loop(0, 4, chunk, 0)
+
+
+def metric_fields(same, other):
     vmem = pl.BlockSpec(memory_space=pltpu.VMEM)
     return pl.pallas_call(
         metric_kernel,
         out_shape=jax.ShapeDtypeStruct((3, 49, 64, 128), jnp.float32),
-        in_specs=[vmem],
+        in_specs=[vmem] * 2,
         out_specs=vmem,
         compiler_params=pltpu.CompilerParams(vmem_limit_bytes=24 * MIB),
-    )(gathered)
+    )(same, other)
 
 
 def solve_kernel(
@@ -493,20 +503,28 @@
     )(jnp.asarray(plane_coefs()), rows)
 
 
+SWAP = [(0, 1), (1, 0)]
+TURNS = [[(at, (at + back) % 4) for at in range(4)] for back in range(1, 4)]
+
+
 def gather_row(mine):
-    swap = [(0, 1), (1, 0)]
-    turns = [[(z, (z + back) % 4) for z in range(4)] for back in range(1, 4)]
-    beside = lax.ppermute(mine, "xl", swap)
-    pieces = [mine] + [lax.ppermute(mine, "z", turn) for turn in turns]
-    pieces += [beside] + [lax.ppermute(beside, "z", turn) for turn in turns]
+    beside = lax.ppermute(mine, "xl", SWAP)
+    pieces = [mine] + [lax.ppermute(mine, "z", turn) for turn in TURNS]
+    pieces += [beside] + [lax.ppermute(beside, "z", turn) for turn in TURNS]
     same = jnp.stack(pieces).reshape(2, 4, 4, 7, 8, 128)
-    return same, lax.ppermute(same, "core", swap)
+    return same, lax.ppermute(same, "core", SWAP)
+
+
+def gather_metric(mine):
+    pair = jnp.stack([mine, lax.ppermute(mine, "xl", SWAP)])
+    ring = jnp.stack([pair] + [lax.ppermute(pair, "xh", turn) for turn in TURNS])
+    same = jnp.stack([ring] + [lax.ppermute(ring, "z", turn) for turn in TURNS])
+    return same, lax.ppermute(same, "core", SWAP)
 
 
 def local(stress, velocity_grad, velocity, metric, iteration_counts):
     packed = jnp.pad(metric.reshape(147, 128), ((0, 5), (0, 0)))
-    gathered = lax.all_gather(packed, PLANE)
-    metrics = metric_fields(gathered)
+    metrics = metric_fields(*gather_metric(packed))
     right, left, up, down = pack_faces(stress)
     ahead = [(c, c + 1) for c in range(15)]
     above = [(e, e + 1) for e in range(3)]

time: 192 us -> 237 us (1.23)
  the two profiles are of different devices: /device:TPU:8 before, /device:TPU:10 now
where the time goes in v3:
time: 237 us; the launch traced here: 236 us
  starting transfers between devices  100 us (42%)
  waiting for transfers between devices  91.5 us (39%)
  Pallas kernels  38.1 us (16%)
  local copies, waits for them, and re-layouts  3.21 us (1%)
    ppermute x3, waiting for transfers between devices, gather_metric(): same = jnp.stack([ring] + [lax.ppermute(ring, 'z', turn) for turn in TURNS])  49.5 us
    pallas_call x1, Pallas kernels, solve(): pl.pallas_call(solve_kernel, out_shape=jax.ShapeDtypeStruct((NZ, 7, 8, 12...  28.9 us
    all_to_all x1, waiting for transfers between devices, local(): answer = lax.all_to_all(answer, ROWS, 0, 0, tiled=True)  26.5 us
    ppermute x3, starting transfers between devices, gather_metric(): same = jnp.stack([ring] + [lax.ppermute(ring, 'z', turn) for turn in TURNS])  18 us
    all_to_all x1, starting transfers between devices, local(): parts = lax.all_to_all(parts, ROWS, 0, 0, tiled=True)  13.1 us
    ppermute x3, starting transfers between devices, gather_row(): pieces = [mine] + [lax.ppermute(mine, 'z', turn) for turn in TURNS]  13 us
    ppermute x3, starting transfers between devices, gather_row(): pieces += [beside] + [lax.ppermute(beside, 'z', turn) for turn in TURNS]  12 us
    ppermute x3, starting transfers between devices, gather_metric(): lax.ppermute(pair, 'xh', turn)  11.6 us
  transfers between devices with their start and end apart: 22, of which 11 were waited for; matrix products, arithmetic and copies ran while one was open for 1% of the time, Pallas kernels for 1%

profile of v3, /device:TPU:10, one launch (start us, length us, event | category | flops | bytes accessed | tf_op | source)
XLA Modules:
  0.0 235.6 jit_solution(12065426928846585496)
XLA Ops:
  2.6 4.0 %collective-permute-start = (f32[4,8,128]{2,1,0:T(8,128)S(1)}, f32[4,8,128]{2,1,0:T(8,128)S(1)}, u32[]{:S(2)}, u32[]{:S(2)}) collective-permute-start(f32[4,8,128]{2,1,0:T(8,128)S(1)} %get-tuple-element.8), channel_id=1, source_target_pairs={{0,32},{32,64},{64,96},{96,128},{128,160},{160,192},{192,224},{224... | collective-permute-start | bytes 49160 | tf_op jit(solution)/shard_map/ppermute | solution.py:532
  9.9 3.6 %collective-permute-start.3 = (f32[4,8,128]{2,1,0:T(8,128)S(1)}, f32[4,8,128]{2,1,0:T(8,128)S(1)}, u32[]{:S(2)}, u32[]{:S(2)}) collective-permute-start(f32[4,8,128]{2,1,0:T(8,128)S(1)} %get-tuple-element.11), channel_id=1, source_target_pairs={{8,0},{16,8},{24,16},{9,1},{17,9},{25,17},{10,2},{18,10},{26,18},{... | collective-permute-start | bytes 49160 | tf_op jit(solution)/shard_map/ppermute | solution.py:535
  15.0 4.5 %shard_map.96 = (f32[6,4,7,7,128]{4,3,2,1,0:T(8,128)S(1)}, f32[32,7,8,128]{3,2,1,0:T(8,128)}) custom-call(f32[3072]{0:T(1024)S(1)} %copy-done.1, f32[6,4,7,7,128]{4,3,2,1,0:T(8,128)S(1)} %copy.11.s_ref, f32[9,4,7,7,128]{4,3,2,1,0:T(8,128)S(1)} %copy.12.g_ref, f32[2,4,7,7,128]{4,3,2,1,0:T(8,128)S(1)} %copy.13.v_ref, ...), custom_call_target="tpu_custom_call" | custom-call | tf_op jit(solution)/shard_map/pallas_call | solution.py:256
  19.5 13.1 %all-to-all-start = ((f32[32,7,8,128]{3,2,1,0:T(8,128)}), f32[32,7,8,128]{3,2,1,0:T(8,128)}, u32[]{:S(2)}, u32[]{:S(2)}) async-start(f32[32,7,8,128]{3,2,1,0:T(8,128)} %get-tuple-element.13), calls=%async_computation | async-start | bytes 1835008 | tf_op jit(solution)/shard_map/all_to_all | solution.py:538
  34.8 5.3 %collective-permute-done.12 = f32[152,128]{1,0:T(8,128)S(1)} collective-permute-done((f32[152,128]{1,0:T(8,128)S(1)}, f32[152,128]{1,0:T(8,128)S(1)}, u32[]{:S(2)}, u32[]{:S(2)}) %collective-permute-start.12) | collective-permute-done | bytes 77856 | tf_op jit(solution)/shard_map/ppermute | solution.py:519
  40.2 4.5 %collective-permute-start.13 = (f32[2,152,128]{2,1,0:T(8,128)S(1)}, f32[2,152,128]{2,1,0:T(8,128)S(1)}, u32[]{:S(2)}, u32[]{:S(2)}) collective-permute-start(f32[2,152,128]{2,1,0:T(8,128)S(1)} %get-tuple-element.19), channel_id=1, source_target_pairs={{0,32},{32,64},{64,96},{96,0},{1,33},{33,65},{65,97},{97,1},{2,34}... | collective-permute-start | bytes 466952 | tf_op jit(solution)/shard_map/ppermute | solution.py:520
  44.7 3.1 %collective-permute-start.14 = (f32[2,152,128]{2,1,0:T(8,128)S(1)}, f32[2,152,128]{2,1,0:T(8,128)S(1)}, u32[]{:S(2)}, u32[]{:S(2)}) collective-permute-start(f32[2,152,128]{2,1,0:T(8,128)S(1)} %get-tuple-element.19), channel_id=1, source_target_pairs={{0,64},{32,96},{64,0},{96,32},{1,65},{33,97},{65,1},{97,33},{2,66}... | collective-permute-start | bytes 466952 | tf_op jit(solution)/shard_map/ppermute | solution.py:520
  47.8 4.0 %collective-permute-start.15 = (f32[2,152,128]{2,1,0:T(8,128)S(1)}, f32[2,152,128]{2,1,0:T(8,128)S(1)}, u32[]{:S(2)}, u32[]{:S(2)}) collective-permute-start(f32[2,152,128]{2,1,0:T(8,128)S(1)} %get-tuple-element.19), channel_id=1, source_target_pairs={{0,96},{32,0},{64,32},{96,64},{1,97},{33,1},{65,33},{97,65},{2,98}... | collective-permute-start | bytes 466952 | tf_op jit(solution)/shard_map/ppermute | solution.py:520
  54.1 3.7 %collective-permute-done.15 = f32[2,152,128]{2,1,0:T(8,128)S(1)} collective-permute-done((f32[2,152,128]{2,1,0:T(8,128)S(1)}, f32[2,152,128]{2,1,0:T(8,128)S(1)}, u32[]{:S(2)}, u32[]{:S(2)}) %collective-permute-start.15) | collective-permute-done | bytes 155680 | tf_op jit(solution)/shard_map/ppermute | solution.py:520
  57.9 7.4 %collective-permute-start.16 = (f32[4,2,152,128]{3,2,1,0:T(8,128)S(1)}, f32[4,2,152,128]{3,2,1,0:T(8,128)S(1)}, u32[]{:S(2)}, u32[]{:S(2)}) collective-permute-start(f32[4,2,152,128]{3,2,1,0:T(8,128)S(1)} %get-tuple-element.17), channel_id=1, source_target_pairs={{0,128},{128,256},{256,384},{384,0},{1,129},{129,257},{257,385},{3... | collective-permute-start | bytes 1867784 | tf_op jit(solution)/shard_map/ppermute | solution.py:521
  65.4 6.9 %collective-permute-start.17 = (f32[4,2,152,128]{3,2,1,0:T(8,128)S(1)}, f32[4,2,152,128]{3,2,1,0:T(8,128)S(1)}, u32[]{:S(2)}, u32[]{:S(2)}) collective-permute-start(f32[4,2,152,128]{3,2,1,0:T(8,128)S(1)} %get-tuple-element.17), channel_id=1, source_target_pairs={{0,256},{128,384},{256,0},{384,128},{1,257},{129,385},{257,1},{385... | collective-permute-start | bytes 1867784 | tf_op jit(solution)/shard_map/ppermute | solution.py:521
  72.3 3.7 %collective-permute-start.18 = (f32[4,2,152,128]{3,2,1,0:T(8,128)S(1)}, f32[4,2,152,128]{3,2,1,0:T(8,128)S(1)}, u32[]{:S(2)}, u32[]{:S(2)}) collective-permute-start(f32[4,2,152,128]{3,2,1,0:T(8,128)S(1)} %get-tuple-element.17), channel_id=1, source_target_pairs={{0,384},{128,0},{256,128},{384,256},{1,385},{129,1},{257,129},{385... | collective-permute-start | bytes 1867784 | tf_op jit(solution)/shard_map/ppermute | solution.py:521
  75.9 9.7 %collective-permute-done.16 = f32[4,2,152,128]{3,2,1,0:T(8,128)S(1)} collective-permute-done((f32[4,2,152,128]{3,2,1,0:T(8,128)S(1)}, f32[4,2,152,128]{3,2,1,0:T(8,128)S(1)}, u32[]{:S(2)}, u32[]{:S(2)}) %collective-permute-start.16) | collective-permute-done | bytes 622624 | tf_op jit(solution)/shard_map/ppermute | solution.py:521
  85.6 13.2 %collective-permute-done.17 = f32[4,2,152,128]{3,2,1,0:T(8,128)S(1)} collective-permute-done((f32[4,2,152,128]{3,2,1,0:T(8,128)S(1)}, f32[4,2,152,128]{3,2,1,0:T(8,128)S(1)}, u32[]{:S(2)}, u32[]{:S(2)}) %collective-permute-start.17) | collective-permute-done | bytes 622624 | tf_op jit(solution)/shard_map/ppermute | solution.py:521
  98.9 26.6 %collective-permute-done.18 = f32[4,2,152,128]{3,2,1,0:T(8,128)S(1)} collective-permute-done((f32[4,2,152,128]{3,2,1,0:T(8,128)S(1)}, f32[4,2,152,128]{3,2,1,0:T(8,128)S(1)}, u32[]{:S(2)}, u32[]{:S(2)}) %collective-permute-start.18) | collective-permute-done | bytes 622624 | tf_op jit(solution)/shard_map/ppermute | solution.py:521
  131.5 5.0 %collective-permute-start.7 = (f32[4,7,8,128]{3,2,1,0:T(8,128)S(1)}, f32[4,7,8,128]{3,2,1,0:T(8,128)S(1)}, u32[]{:S(2)}, u32[]{:S(2)}) collective-permute-start(f32[4,7,8,128]{3,2,1,0:T(8,128)S(1)} %bitcast_reduce_fusion), channel_id=1, source_target_pairs={{0,16},{16,0},{1,17},{17,1},{2,18},{18,2},{3,19},{19,3},{4,20},{20... | collective-permute-start | bytes 344072 | tf_op jit(solution)/shard_map/ppermute | solution.py:511
  136.5 6.3 %collective-permute-start.5 = (f32[4,7,8,128]{3,2,1,0:T(8,128)S(1)}, f32[4,7,8,128]{3,2,1,0:T(8,128)S(1)}, u32[]{:S(2)}, u32[]{:S(2)}) collective-permute-start(f32[4,7,8,128]{3,2,1,0:T(8,128)S(1)} %bitcast_reduce_fusion), channel_id=1, source_target_pairs={{0,256},{128,384},{256,0},{384,128},{1,257},{129,385},{257,1},{385... | collective-permute-start | bytes 344072 | tf_op jit(solution)/shard_map/ppermute | solution.py:512
  142.9 3.9 %collective-permute-start.6 = (f32[4,7,8,128]{3,2,1,0:T(8,128)S(1)}, f32[4,7,8,128]{3,2,1,0:T(8,128)S(1)}, u32[]{:S(2)}, u32[]{:S(2)}) collective-permute-start(f32[4,7,8,128]{3,2,1,0:T(8,128)S(1)} %bitcast_reduce_fusion), channel_id=1, source_target_pairs={{0,384},{128,0},{256,128},{384,256},{1,385},{129,1},{257,129},{385... | collective-permute-start | bytes 344072 | tf_op jit(solution)/shard_map/ppermute | solution.py:512
  149.6 3.4 %collective-permute-start.9 = (f32[4,7,8,128]{3,2,1,0:T(8,128)S(1)}, f32[4,7,8,128]{3,2,1,0:T(8,128)S(1)}, u32[]{:S(2)}, u32[]{:S(2)}) collective-permute-start(f32[4,7,8,128]{3,2,1,0:T(8,128)S(1)} %collective-permute-done.7), channel_id=1, source_target_pairs={{0,256},{128,384},{256,0},{384,128},{1,257},{129,385},{257,1},{385... | collective-permute-start | bytes 344072 | tf_op jit(solution)/shard_map/ppermute | solution.py:513
  153.1 5.8 %collective-permute-start.10 = (f32[4,7,8,128]{3,2,1,0:T(8,128)S(1)}, f32[4,7,8,128]{3,2,1,0:T(8,128)S(1)}, u32[]{:S(2)}, u32[]{:S(2)}) collective-permute-start(f32[4,7,8,128]{3,2,1,0:T(8,128)S(1)} %collective-permute-done.7), channel_id=1, source_target_pairs={{0,384},{128,0},{256,128},{384,256},{1,385},{129,1},{257,129},{385... | collective-permute-start | bytes 344072 | tf_op jit(solution)/shard_map/ppermute | solution.py:513
  163.8 3.1 %shard_map.97.q_ref = f32[3,49,64,128]{3,2,1,0:T(8,128)S(1)} custom-call(f32[4,4,2,152,128]{4,3,2,1,0:T(8,128)S(1)} %pad_maximum_fusion.same_ref, f32[4,4,2,152,128]{4,3,2,1,0:T(8,128)} %collective-permute-done.19.other_ref), custom_call_target="tpu_custom_call" | custom-call | tf_op jit(solution)/shard_map/pallas_call | solution.py:309
  166.9 28.9 %shard_map.98 = f32[32,7,8,128]{3,2,1,0:T(8,128)} custom-call(s32[32]{0:T(128)S(1)} %copy-done.3, f32[2,4,4,7,8,128]{5,4,3,2,1,0:T(8,128)S(1)} %bitcast.33, f32[2,4,4,7,8,128]{5,4,3,2,1,0:T(8,128)S(1)} %collective-permute-done.11.other_ref, f32[3,49,64,128]{3,2,1,0:T(8,128)S(1)} %shard_map.97.q_ref), custom_call_target="tpu_custom_call" | custom-call | tf_op jit(solution)/shard_map/pallas_call | solution.py:472
  195.9 10.7 %all-to-all-start.1 = ((f32[32,7,8,128]{3,2,1,0:T(8,128)}), f32[32,7,8,128]{3,2,1,0:T(8,128)S(1)}, u32[]{:S(2)}, u32[]{:S(2)}) async-start(f32[32,7,8,128]{3,2,1,0:T(8,128)} %shard_map.98), calls=%async_computation.1 | async-start | bytes 1835008 | tf_op jit(solution)/shard_map/all_to_all | solution.py:542
  207.6 26.5 %all-to-all-done.1.rows_ref = f32[32,7,8,128]{3,2,1,0:T(8,128)S(1)} async-done(((f32[32,7,8,128]{3,2,1,0:T(8,128)}), f32[32,7,8,128]{3,2,1,0:T(8,128)S(1)}, u32[]{:S(2)}, u32[]{:S(2)}) %all-to-all-start.1) | async-done | bytes 917536 | tf_op jit(solution)/shard_map/all_to_all | solution.py:542
  (58 shorter events, 27.3 us)
Async XLA Ops:
  2.6 11.1 %collective-permute-start = (f32[4,8,128]{2,1,0:T(8,128)S(1)}, f32[4,8,128]{2,1,0:T(8,128)S(1)}, u32[]{:S(2)}, u32[]{:S(2)}) collective-permute-start(f32[4,8,128]{2,1,0:T(8,128)S(1)} %get-tuple-element.8), channel_id=1, source_target_pairs={{0,32},{32,64},{64,96},{96,128},{128,160},{160,192},{192,224},{224... | collective-permute-start | bytes 49160 | tf_op jit(solution)/shard_map/ppermute | solution.py:532
  6.7 7.1 %collective-permute-start.1 = (f32[4,8,128]{2,1,0:T(8,128)S(1)}, f32[4,8,128]{2,1,0:T(8,128)S(1)}, u32[]{:S(2)}, u32[]{:S(2)}) collective-permute-start(f32[4,8,128]{2,1,0:T(8,128)S(1)} %get-tuple-element.9), channel_id=1, source_target_pairs={{32,0},{64,32},{96,64},{128,96},{160,128},{192,160},{224,192},{256... | collective-permute-start | bytes 49160 | tf_op jit(solution)/shard_map/ppermute | solution.py:533
  8.0 5.8 %collective-permute-start.2 = (f32[4,8,128]{2,1,0:T(8,128)S(1)}, f32[4,8,128]{2,1,0:T(8,128)S(1)}, u32[]{:S(2)}, u32[]{:S(2)}) collective-permute-start(f32[4,8,128]{2,1,0:T(8,128)S(1)} %get-tuple-element.10), channel_id=1, source_target_pairs={{0,8},{8,16},{16,24},{1,9},{9,17},{17,25},{2,10},{10,18},{18,26},{... | collective-permute-start | bytes 49160 | tf_op jit(solution)/shard_map/ppermute | solution.py:534
  9.9 5.1 %collective-permute-start.3 = (f32[4,8,128]{2,1,0:T(8,128)S(1)}, f32[4,8,128]{2,1,0:T(8,128)S(1)}, u32[]{:S(2)}, u32[]{:S(2)}) collective-permute-start(f32[4,8,128]{2,1,0:T(8,128)S(1)} %get-tuple-element.11), channel_id=1, source_target_pairs={{8,0},{16,8},{24,16},{9,1},{17,9},{25,17},{10,2},{18,10},{26,18},{... | collective-permute-start | bytes 49160 | tf_op jit(solution)/shard_map/ppermute | solution.py:535
  13.7 18.9 %copy-start.6 = (f32[3,7,7,128]{3,2,1,0:T(8,128)S(1)}, f32[3,7,7,128]{3,2,1,0:T(8,128)}, u32[]{:S(2)}) copy-start(f32[3,7,7,128]{3,2,1,0:T(8,128)} %param.11) | copy-start | bytes 225796
  19.5 108.1 %all-to-all-start = ((f32[32,7,8,128]{3,2,1,0:T(8,128)}), f32[32,7,8,128]{3,2,1,0:T(8,128)}, u32[]{:S(2)}, u32[]{:S(2)}) async-start(f32[32,7,8,128]{3,2,1,0:T(8,128)} %get-tuple-element.13), calls=%async_computation | async-start | bytes 1835008 | tf_op jit(solution)/shard_map/all_to_all | solution.py:538
  32.7 7.5 %collective-permute-start.12 = (f32[152,128]{1,0:T(8,128)S(1)}, f32[152,128]{1,0:T(8,128)S(1)}, u32[]{:S(2)}, u32[]{:S(2)}) collective-permute-start(f32[152,128]{1,0:T(8,128)S(1)} %get-tuple-element.21), channel_id=1, source_target_pairs={{0,16},{16,0},{1,17},{17,1},{2,18},{18,2},{3,19},{19,3},{4,20},{20... | collective-permute-start | bytes 233480 | tf_op jit(solution)/shard_map/ppermute | solution.py:519
  40.2 13.6 %collective-permute-start.13 = (f32[2,152,128]{2,1,0:T(8,128)S(1)}, f32[2,152,128]{2,1,0:T(8,128)S(1)}, u32[]{:S(2)}, u32[]{:S(2)}) collective-permute-start(f32[2,152,128]{2,1,0:T(8,128)S(1)} %get-tuple-element.19), channel_id=1, source_target_pairs={{0,32},{32,64},{64,96},{96,0},{1,33},{33,65},{65,97},{97,1},{2,34}... | collective-permute-start | bytes 466952 | tf_op jit(solution)/shard_map/ppermute | solution.py:520
  44.7 9.5 %collective-permute-start.14 = (f32[2,152,128]{2,1,0:T(8,128)S(1)}, f32[2,152,128]{2,1,0:T(8,128)S(1)}, u32[]{:S(2)}, u32[]{:S(2)}) collective-permute-start(f32[2,152,128]{2,1,0:T(8,128)S(1)} %get-tuple-element.19), channel_id=1, source_target_pairs={{0,64},{32,96},{64,0},{96,32},{1,65},{33,97},{65,1},{97,33},{2,66}... | collective-permute-start | bytes 466952 | tf_op jit(solution)/shard_map/ppermute | solution.py:520
  47.8 10.1 %collective-permute-start.15 = (f32[2,152,128]{2,1,0:T(8,128)S(1)}, f32[2,152,128]{2,1,0:T(8,128)S(1)}, u32[]{:S(2)}, u32[]{:S(2)}) collective-permute-start(f32[2,152,128]{2,1,0:T(8,128)S(1)} %get-tuple-element.19), channel_id=1, source_target_pairs={{0,96},{32,0},{64,32},{96,64},{1,97},{33,1},{65,33},{97,65},{2,98}... | collective-permute-start | bytes 466952 | tf_op jit(solution)/shard_map/ppermute | solution.py:520
  57.9 27.7 %collective-permute-start.16 = (f32[4,2,152,128]{3,2,1,0:T(8,128)S(1)}, f32[4,2,152,128]{3,2,1,0:T(8,128)S(1)}, u32[]{:S(2)}, u32[]{:S(2)}) collective-permute-start(f32[4,2,152,128]{3,2,1,0:T(8,128)S(1)} %get-tuple-element.17), channel_id=1, source_target_pairs={{0,128},{128,256},{256,384},{384,0},{1,129},{129,257},{257,385},{3... | collective-permute-start | bytes 1867784 | tf_op jit(solution)/shard_map/ppermute | solution.py:521
  65.4 33.5 %collective-permute-start.17 = (f32[4,2,152,128]{3,2,1,0:T(8,128)S(1)}, f32[4,2,152,128]{3,2,1,0:T(8,128)S(1)}, u32[]{:S(2)}, u32[]{:S(2)}) collective-permute-start(f32[4,2,152,128]{3,2,1,0:T(8,128)S(1)} %get-tuple-element.17), channel_id=1, source_target_pairs={{0,256},{128,384},{256,0},{384,128},{1,257},{129,385},{257,1},{385... | collective-permute-start | bytes 1867784 | tf_op jit(solution)/shard_map/ppermute | solution.py:521
  72.3 53.2 %collective-permute-start.18 = (f32[4,2,152,128]{3,2,1,0:T(8,128)S(1)}, f32[4,2,152,128]{3,2,1,0:T(8,128)S(1)}, u32[]{:S(2)}, u32[]{:S(2)}) collective-permute-start(f32[4,2,152,128]{3,2,1,0:T(8,128)S(1)} %get-tuple-element.17), channel_id=1, source_target_pairs={{0,384},{128,0},{256,128},{384,256},{1,385},{129,1},{257,129},{385... | collective-permute-start | bytes 1867784 | tf_op jit(solution)/shard_map/ppermute | solution.py:521
  125.6 38.2 %collective-permute-start.19 = (f32[4,4,2,152,128]{4,3,2,1,0:T(8,128)S(1)}, f32[4,4,2,152,128]{4,3,2,1,0:T(8,128)}, u32[]{:S(2)}, u32[]{:S(2)}) collective-permute-start(f32[4,4,2,152,128]{4,3,2,1,0:T(8,128)S(1)} %pad_maximum_fusion.same_ref), channel_id=1, source_target_pairs={{0,8},{8,0},{1,9},{9,1},{2,10},{10,2},{3,11},{11,3},{4,12},{12,4},... | collective-permute-start | bytes 7471112 | tf_op jit(solution)/shard_map/ppermute | solution.py:522
  128.8 20.8 %collective-permute-start.4 = (f32[4,7,8,128]{3,2,1,0:T(8,128)S(1)}, f32[4,7,8,128]{3,2,1,0:T(8,128)S(1)}, u32[]{:S(2)}, u32[]{:S(2)}) collective-permute-start(f32[4,7,8,128]{3,2,1,0:T(8,128)S(1)} %bitcast_reduce_fusion), channel_id=1, source_target_pairs={{0,128},{128,256},{256,384},{384,0},{1,129},{129,257},{257,385},{3... | collective-permute-start | bytes 344072 | tf_op jit(solution)/shard_map/ppermute | solution.py:512
  131.5 15.3 %collective-permute-start.7 = (f32[4,7,8,128]{3,2,1,0:T(8,128)S(1)}, f32[4,7,8,128]{3,2,1,0:T(8,128)S(1)}, u32[]{:S(2)}, u32[]{:S(2)}) collective-permute-start(f32[4,7,8,128]{3,2,1,0:T(8,128)S(1)} %bitcast_reduce_fusion), channel_id=1, source_target_pairs={{0,16},{16,0},{1,17},{17,1},{2,18},{18,2},{3,19},{19,3},{4,20},{20... | collective-permute-start | bytes 344072 | tf_op jit(solution)/shard_map/ppermute | solution.py:511
  136.5 16.6 %collective-permute-start.5 = (f32[4,7,8,128]{3,2,1,0:T(8,128)S(1)}, f32[4,7,8,128]{3,2,1,0:T(8,128)S(1)}, u32[]{:S(2)}, u32[]{:S(2)}) collective-permute-start(f32[4,7,8,128]{3,2,1,0:T(8,128)S(1)} %bitcast_reduce_fusion), channel_id=1, source_target_pairs={{0,256},{128,384},{256,0},{384,128},{1,257},{129,385},{257,1},{385... | collective-permute-start | bytes 344072 | tf_op jit(solution)/shard_map/ppermute | solution.py:512
  142.9 16.0 %collective-permute-start.6 = (f32[4,7,8,128]{3,2,1,0:T(8,128)S(1)}, f32[4,7,8,128]{3,2,1,0:T(8,128)S(1)}, u32[]{:S(2)}, u32[]{:S(2)}) collective-permute-start(f32[4,7,8,128]{3,2,1,0:T(8,128)S(1)} %bitcast_reduce_fusion), channel_id=1, source_target_pairs={{0,384},{128,0},{256,128},{384,256},{1,385},{129,1},{257,129},{385... | collective-permute-start | bytes 344072 | tf_op jit(solution)/shard_map/ppermute | solution.py:512
  146.8 12.1 %collective-permute-start.8 = (f32[4,7,8,128]{3,2,1,0:T(8,128)S(1)}, f32[4,7,8,128]{3,2,1,0:T(8,128)S(1)}, u32[]{:S(2)}, u32[]{:S(2)}) collective-permute-start(f32[4,7,8,128]{3,2,1,0:T(8,128)S(1)} %collective-permute-done.7), channel_id=1, source_target_pairs={{0,128},{128,256},{256,384},{384,0},{1,129},{129,257},{257,385},{3... | collective-permute-start | bytes 344072 | tf_op jit(solution)/shard_map/ppermute | solution.py:513
  149.6 10.7 %collective-permute-start.9 = (f32[4,7,8,128]{3,2,1,0:T(8,128)S(1)}, f32[4,7,8,128]{3,2,1,0:T(8,128)S(1)}, u32[]{:S(2)}, u32[]{:S(2)}) collective-permute-start(f32[4,7,8,128]{3,2,1,0:T(8,128)S(1)} %collective-permute-done.7), channel_id=1, source_target_pairs={{0,256},{128,384},{256,0},{384,128},{1,257},{129,385},{257,1},{385... | collective-permute-start | bytes 344072 | tf_op jit(solution)/shard_map/ppermute | solution.py:513
  153.1 8.8 %collective-permute-start.10 = (f32[4,7,8,128]{3,2,1,0:T(8,128)S(1)}, f32[4,7,8,128]{3,2,1,0:T(8,128)S(1)}, u32[]{:S(2)}, u32[]{:S(2)}) collective-permute-start(f32[4,7,8,128]{3,2,1,0:T(8,128)S(1)} %collective-permute-done.7), channel_id=1, source_target_pairs={{0,384},{128,0},{256,128},{384,256},{1,385},{129,1},{257,129},{385... | collective-permute-start | bytes 344072 | tf_op jit(solution)/shard_map/ppermute | solution.py:513
  161.9 5.0 %collective-permute-start.11 = (f32[2,4,4,7,8,128]{5,4,3,2,1,0:T(8,128)S(1)}, f32[2,4,4,7,8,128]{5,4,3,2,1,0:T(8,128)S(1)}, u32[]{:S(2)}, u32[]{:S(2)}) collective-permute-start(f32[2,4,4,7,8,128]{5,4,3,2,1,0:T(8,128)S(1)} %bitcast.32), channel_id=1, source_target_pairs={{0,8},{8,0},{1,9},{9,1},{2,10},{10,2},{3,11},{11,3},{4,12},{12,4},... | collective-permute-start | bytes 2752520 | tf_op jit(solution)/shard_map/ppermute | solution.py:515
  195.9 38.2 %copy-start.2 = (f32[1024]{0:T(1024)S(1)}, f32[1024]{0:T(1024)}, u32[]{:S(2)}) copy-start(f32[1024]{0:T(1024)} %constant.12.clone.coef_ref) | copy-start | bytes 12292
  195.9 38.2 %all-to-all-start.1 = ((f32[32,7,8,128]{3,2,1,0:T(8,128)}), f32[32,7,8,128]{3,2,1,0:T(8,128)S(1)}, u32[]{:S(2)}, u32[]{:S(2)}) async-start(f32[32,7,8,128]{3,2,1,0:T(8,128)} %shard_map.98), calls=%async_computation.1 | async-start | bytes 1835008 | tf_op jit(solution)/shard_map/all_to_all | solution.py:542
  (5 other events, 59.6 us)

commit v4 on v3

--- a/solution.py
+++ b/solution.py
@@ -338,7 +338,7 @@
             flip = (xl + from_xl) % 2
             back = [(z - half * 2 - s + 4) % 4 for s in range(2)]
             for i in range(7):
-                block = jnp.stack([ref[flip, back[s // 4], s % 4, i] for s in range(8)])
+                block = jnp.stack([ref[back[s // 4], flip, s % 4, i] for s in range(8)])
                 block = jnp.swapaxes(block, 0, 1)
                 for j in range(7):
                     n = i * 7 + j
@@ -507,25 +507,33 @@
 TURNS = [[(at, (at + back) % 4) for at in range(4)] for back in range(1, 4)]
 
 
+def around(mine):
+    behind = lax.ppermute(mine, "z", TURNS[0])
+    before = lax.ppermute(mine, "z", TURNS[2])
+    half = mine.shape[0] // 2
+    far = [
+        lax.ppermute(behind[:half], "z", TURNS[0]),
+        lax.ppermute(before[half:], "z", TURNS[2]),
+    ]
+    return behind, far, before
+
+
 def gather_row(mine):
-    beside = lax.ppermute(mine, "xl", SWAP)
-    pieces = [mine] + [lax.ppermute(mine, "z", turn) for turn in TURNS]
-    pieces += [beside] + [lax.ppermute(beside, "z", turn) for turn in TURNS]
-    same = jnp.stack(pieces).reshape(2, 4, 4, 7, 8, 128)
+    pair = jnp.stack([mine, lax.ppermute(mine, "xl", SWAP)])
+    behind, far, before = around(pair)
+    same = jnp.concatenate([pair, behind, *far, before]).reshape(4, 2, 4, 7, 8, 128)
     return same, lax.ppermute(same, "core", SWAP)
 
 
-def gather_metric(mine):
-    pair = jnp.stack([mine, lax.ppermute(mine, "xl", SWAP)])
-    ring = jnp.stack([pair] + [lax.ppermute(pair, "xh", turn) for turn in TURNS])
-    same = jnp.stack([ring] + [lax.ppermute(ring, "z", turn) for turn in TURNS])
-    return same, lax.ppermute(same, "core", SWAP)
+def after(value, other):
+    return lax.optimization_barrier((value, other))[0]
 
 
 def local(stress, velocity_grad, velocity, metric, iteration_counts):
     packed = jnp.pad(metric.reshape(147, 128), ((0, 5), (0, 0)))
-    metrics = metric_fields(*gather_metric(packed))
+    beside = lax.ppermute(packed, "xl", SWAP)
     right, left, up, down = pack_faces(stress)
+    pair = jnp.stack([after(packed, right), beside])
     ahead = [(c, c + 1) for c in range(15)]
     above = [(e, e + 1) for e in range(3)]
     faces = (
@@ -534,9 +542,16 @@
         lax.ppermute(up, CROSS, above),
         lax.ppermute(down, CROSS, [(b, a) for a, b in above]),
     )
+    faces = after(faces, pair)
     new_stress, parts = stress_step(stress, velocity_grad, velocity, faces)
+    ring = jnp.stack([pair] + [lax.ppermute(pair, "xh", turn) for turn in TURNS])
+    parts = after(parts, ring)
+    behind, far, before = around(ring)
     parts = lax.all_to_all(parts, ROWS, 0, 0, tiled=True)
     mine = jnp.sum(parts.reshape(4, 8, 7, 8, 128), axis=1)
+    ring = after(ring, mine)
+    plane = jnp.concatenate([ring, behind, *far, before]).reshape(4, 4, 2, 152, 128)
+    metrics = metric_fields(plane, lax.ppermute(plane, "core", SWAP))
     same, other = gather_row(mine)
     answer = solve(iteration_counts, same, other, metrics)
     answer = lax.all_to_all(answer, ROWS, 0, 0, tiled=True)

time: 237 us -> 229 us (0.966)
  the two profiles are of different devices: /device:TPU:10 before, /device:TPU:8 now
where the time goes in v4:
time: 229 us; the launch traced here: 228 us
  waiting for transfers between devices  95.9 us (42%)
  starting transfers between devices  83.2 us (36%)
  Pallas kernels  40 us (17%)
  local copies, waits for them, and re-layouts  7.67 us (3%)
    ppermute x2, waiting for transfers between devices, around(): behind = lax.ppermute(mine, 'z', TURNS[0])  37.1 us
    pallas_call x1, Pallas kernels, solve(): pl.pallas_call(solve_kernel, out_shape=jax.ShapeDtypeStruct((NZ, 7, 8, 12...  32.5 us
    all_to_all x1, waiting for transfers between devices, local(): answer = lax.all_to_all(answer, ROWS, 0, 0, tiled=True)  25.8 us
    all_to_all x1, starting transfers between devices, local(): parts = lax.all_to_all(parts, ROWS, 0, 0, tiled=True)  13.1 us
    ppermute x3, starting transfers between devices, local(): lax.ppermute(pair, 'xh', turn)  12.5 us
    ppermute x2, waiting for transfers between devices, around(): lax.ppermute(before[half:], 'z', TURNS[2])  12.3 us
    ppermute x2, starting transfers between devices, around(): lax.ppermute(before[half:], 'z', TURNS[2])  11.5 us
    ppermute x2, starting transfers between devices, around(): behind = lax.ppermute(mine, 'z', TURNS[0])  10.2 us
  transfers between devices with their start and end apart: 21, of which 13 were waited for; matrix products, arithmetic and copies ran while one was open for 2% of the time, Pallas kernels for 3%

profile of v4, /device:TPU:8, one launch (start us, length us, event | category | flops | bytes accessed | tf_op | source)
XLA Modules:
  0.0 228.0 jit_solution(14508348968152258529)
XLA Ops:
  1.7 3.4 %collective-permute-start.4 = (f32[152,128]{1,0:T(8,128)S(1)}, f32[152,128]{1,0:T(8,128)S(1)}, u32[]{:S(2)}, u32[]{:S(2)}) collective-permute-start(f32[152,128]{1,0:T(8,128)S(1)} %pad.4), channel_id=1, source_target_pairs={{0,16},{16,0},{1,17},{17,1},{2,18},{18,2},{3,19},{19,3},{4,20},{20... | collective-permute-start | bytes 233480 | tf_op jit(solution)/shard_map/ppermute | solution.py:534
  8.0 4.9 %collective-permute-start.5 = (f32[2,152,128]{2,1,0:T(8,128)S(1)}, f32[2,152,128]{2,1,0:T(8,128)S(1)}, u32[]{:S(2)}, u32[]{:S(2)}) collective-permute-start(f32[2,152,128]{2,1,0:T(8,128)S(1)} %get-tuple-element.31), channel_id=1, source_target_pairs={{0,32},{32,64},{64,96},{96,0},{1,33},{33,65},{65,97},{97,1},{2,34}... | collective-permute-start | bytes 466952 | tf_op jit(solution)/shard_map/ppermute | solution.py:547
  12.9 4.3 %collective-permute-start.6 = (f32[2,152,128]{2,1,0:T(8,128)S(1)}, f32[2,152,128]{2,1,0:T(8,128)S(1)}, u32[]{:S(2)}, u32[]{:S(2)}) collective-permute-start(f32[2,152,128]{2,1,0:T(8,128)S(1)} %get-tuple-element.31), channel_id=1, source_target_pairs={{0,64},{32,96},{64,0},{96,32},{1,65},{33,97},{65,1},{97,33},{2,66}... | collective-permute-start | bytes 466952 | tf_op jit(solution)/shard_map/ppermute | solution.py:547
  17.2 3.3 %collective-permute-start.7 = (f32[2,152,128]{2,1,0:T(8,128)S(1)}, f32[2,152,128]{2,1,0:T(8,128)S(1)}, u32[]{:S(2)}, u32[]{:S(2)}) collective-permute-start(f32[2,152,128]{2,1,0:T(8,128)S(1)} %get-tuple-element.31), channel_id=1, source_target_pairs={{0,96},{32,0},{64,32},{96,64},{1,97},{33,1},{65,33},{97,65},{2,98}... | collective-permute-start | bytes 466952 | tf_op jit(solution)/shard_map/ppermute | solution.py:547
  20.5 4.0 %collective-permute-start = (f32[4,8,128]{2,1,0:T(8,128)S(1)}, f32[4,8,128]{2,1,0:T(8,128)S(1)}, u32[]{:S(2)}, u32[]{:S(2)}) collective-permute-start(f32[4,8,128]{2,1,0:T(8,128)S(1)} %get-tuple-element.15), channel_id=1, source_target_pairs={{0,32},{32,64},{64,96},{96,128},{128,160},{160,192},{192,224},{224... | collective-permute-start | bytes 49160 | tf_op jit(solution)/shard_map/ppermute | solution.py:540
  27.3 4.4 %collective-permute-done.1.right_ref = f32[4,8,128]{2,1,0:T(8,128)S(1)} collective-permute-done((f32[4,8,128]{2,1,0:T(8,128)S(1)}, f32[4,8,128]{2,1,0:T(8,128)S(1)}, u32[]{:S(2)}, u32[]{:S(2)}) %collective-permute-start.1) | collective-permute-done | bytes 16416 | tf_op jit(solution)/shard_map/ppermute | solution.py:541
  34.8 4.5 %shard_map.96 = (f32[6,4,7,7,128]{4,3,2,1,0:T(8,128)S(1)}, f32[32,7,8,128]{3,2,1,0:T(8,128)}) custom-call(f32[3072]{0:T(1024)S(1)} %copy-done.1, f32[6,4,7,7,128]{4,3,2,1,0:T(8,128)S(1)} %copy.11.s_ref, f32[9,4,7,7,128]{4,3,2,1,0:T(8,128)S(1)} %copy.12.g_ref, f32[2,4,7,7,128]{4,3,2,1,0:T(8,128)S(1)} %copy.13.v_ref, ...), custom_call_target="tpu_custom_call" | custom-call | tf_op jit(solution)/shard_map/pallas_call | solution.py:256
  39.3 13.1 %all-to-all-start = ((f32[32,7,8,128]{3,2,1,0:T(8,128)}), f32[32,7,8,128]{3,2,1,0:T(8,128)S(1)}, u32[]{:S(2)}, u32[]{:S(2)}) async-start(f32[32,7,8,128]{3,2,1,0:T(8,128)} %get-tuple-element.26), calls=%async_computation | async-start | bytes 1835008 | tf_op jit(solution)/shard_map/all_to_all | solution.py:550
  52.4 7.6 %collective-permute-start.14 = (f32[4,2,152,128]{3,2,1,0:T(8,128)S(1)}, f32[4,2,152,128]{3,2,1,0:T(8,128)S(1)}, u32[]{:S(2)}, u32[]{:S(2)}) collective-permute-start(f32[4,2,152,128]{3,2,1,0:T(8,128)S(1)} %pad_maximum_fusion), channel_id=1, source_target_pairs={{0,128},{128,256},{256,384},{384,0},{1,129},{129,257},{257,385},{3... | collective-permute-start | bytes 1867784 | tf_op jit(solution)/shard_map/ppermute | solution.py:511
  62.0 33.2 %collective-permute-done.14 = f32[4,2,152,128]{3,2,1,0:T(8,128)S(1)} collective-permute-done((f32[4,2,152,128]{3,2,1,0:T(8,128)S(1)}, f32[4,2,152,128]{3,2,1,0:T(8,128)S(1)}, u32[]{:S(2)}, u32[]{:S(2)}) %collective-permute-start.14) | collective-permute-done | bytes 622624 | tf_op jit(solution)/shard_map/ppermute | solution.py:511
  95.9 2.9 %collective-permute-start.15 = (f32[2,2,152,128]{3,2,1,0:T(8,128)}, f32[2,2,152,128]{3,2,1,0:T(8,128)}, u32[]{:S(2)}, u32[]{:S(2)}) collective-permute-start(f32[2,2,152,128]{3,2,1,0:T(8,128)} %slice.18), channel_id=1, source_target_pairs={{0,128},{128,256},{256,384},{384,0},{1,129},{129,257},{257,385},{3... | collective-permute-start | bytes 933896 | tf_op jit(solution)/shard_map/ppermute | solution.py:515
  99.5 5.0 %collective-permute-start.17 = (f32[2,2,152,128]{3,2,1,0:T(8,128)}, f32[2,2,152,128]{3,2,1,0:T(8,128)}, u32[]{:S(2)}, u32[]{:S(2)}) collective-permute-start(f32[2,2,152,128]{3,2,1,0:T(8,128)} %slice.19), channel_id=1, source_target_pairs={{0,384},{128,0},{256,128},{384,256},{1,385},{129,1},{257,129},{385... | collective-permute-start | bytes 933896 | tf_op jit(solution)/shard_map/ppermute | solution.py:516
  104.7 6.6 %collective-permute-done.15 = f32[2,2,152,128]{3,2,1,0:T(8,128)} collective-permute-done((f32[2,2,152,128]{3,2,1,0:T(8,128)}, f32[2,2,152,128]{3,2,1,0:T(8,128)}, u32[]{:S(2)}, u32[]{:S(2)}) %collective-permute-start.15) | collective-permute-done | bytes 311328 | tf_op jit(solution)/shard_map/ppermute | solution.py:515
  112.3 8.5 %collective-permute-done.17 = f32[2,2,152,128]{3,2,1,0:T(8,128)} collective-permute-done((f32[2,2,152,128]{3,2,1,0:T(8,128)}, f32[2,2,152,128]{3,2,1,0:T(8,128)}, u32[]{:S(2)}, u32[]{:S(2)}) %collective-permute-start.17) | collective-permute-done | bytes 311328 | tf_op jit(solution)/shard_map/ppermute | solution.py:516
  125.7 5.5 %collective-permute-done.8 = f32[4,7,8,128]{3,2,1,0:T(8,128)S(1)} collective-permute-done((f32[4,7,8,128]{3,2,1,0:T(8,128)S(1)}, f32[4,7,8,128]{3,2,1,0:T(8,128)S(1)}, u32[]{:S(2)}, u32[]{:S(2)}) %collective-permute-start.8) | collective-permute-done | bytes 114720 | tf_op jit(solution)/shard_map/ppermute | solution.py:522
  131.2 2.6 %collective-permute-start.9 = (f32[2,4,7,8,128]{4,3,2,1,0:T(8,128)S(1)}, f32[2,4,7,8,128]{4,3,2,1,0:T(8,128)S(1)}, u32[]{:S(2)}, u32[]{:S(2)}) collective-permute-start(f32[2,4,7,8,128]{4,3,2,1,0:T(8,128)S(1)} %pad_maximum_fusion.1), channel_id=1, source_target_pairs={{0,128},{128,256},{256,384},{384,0},{1,129},{129,257},{257,385},{3... | collective-permute-start | bytes 688136 | tf_op jit(solution)/shard_map/ppermute | solution.py:511
  133.8 5.4 %collective-permute-start.11 = (f32[2,4,7,8,128]{4,3,2,1,0:T(8,128)S(1)}, f32[2,4,7,8,128]{4,3,2,1,0:T(8,128)S(1)}, u32[]{:S(2)}, u32[]{:S(2)}) collective-permute-start(f32[2,4,7,8,128]{4,3,2,1,0:T(8,128)S(1)} %pad_maximum_fusion.1), channel_id=1, source_target_pairs={{0,384},{128,0},{256,128},{384,256},{1,385},{129,1},{257,129},{385... | collective-permute-start | bytes 688136 | tf_op jit(solution)/shard_map/ppermute | solution.py:512
  139.2 3.9 %collective-permute-done.9 = f32[2,4,7,8,128]{4,3,2,1,0:T(8,128)S(1)} collective-permute-done((f32[2,4,7,8,128]{4,3,2,1,0:T(8,128)S(1)}, f32[2,4,7,8,128]{4,3,2,1,0:T(8,128)S(1)}, u32[]{:S(2)}, u32[]{:S(2)}) %collective-permute-start.9) | collective-permute-done | bytes 229408 | tf_op jit(solution)/shard_map/ppermute | solution.py:511
  143.1 3.7 %collective-permute-start.10 = (f32[1,4,7,8,128]{4,3,2,1,0:T(8,128)S(1)}, f32[1,4,7,8,128]{4,3,2,1,0:T(8,128)S(1)}, u32[]{:S(2)}, u32[]{:S(2)}) collective-permute-start(f32[1,4,7,8,128]{4,3,2,1,0:T(8,128)S(1)} %slice.16), channel_id=1, source_target_pairs={{0,128},{128,256},{256,384},{384,0},{1,129},{129,257},{257,385},{3... | collective-permute-start | bytes 344072 | tf_op jit(solution)/shard_map/ppermute | solution.py:515
  147.3 6.5 %collective-permute-start.12 = (f32[1,4,7,8,128]{4,3,2,1,0:T(8,128)S(1)}, f32[1,4,7,8,128]{4,3,2,1,0:T(8,128)S(1)}, u32[]{:S(2)}, u32[]{:S(2)}) collective-permute-start(f32[1,4,7,8,128]{4,3,2,1,0:T(8,128)S(1)} %slice.17), channel_id=1, source_target_pairs={{0,384},{128,0},{256,128},{384,256},{1,385},{129,1},{257,129},{385... | collective-permute-start | bytes 344072 | tf_op jit(solution)/shard_map/ppermute | solution.py:516
  153.9 3.8 %collective-permute-done.12 = f32[1,4,7,8,128]{4,3,2,1,0:T(8,128)S(1)} collective-permute-done((f32[1,4,7,8,128]{4,3,2,1,0:T(8,128)S(1)}, f32[1,4,7,8,128]{4,3,2,1,0:T(8,128)S(1)}, u32[]{:S(2)}, u32[]{:S(2)}) %collective-permute-start.12) | collective-permute-done | bytes 114720 | tf_op jit(solution)/shard_map/ppermute | solution.py:516
  162.1 32.5 %shard_map.98 = f32[32,7,8,128]{3,2,1,0:T(8,128)} custom-call(s32[32]{0:T(128)S(1)} %copy-done.3, f32[4,2,4,7,8,128]{5,4,3,2,1,0:T(8,128)S(1)} %bitcast.18, f32[4,2,4,7,8,128]{5,4,3,2,1,0:T(8,128)S(1)} %collective-permute-done.13.other_ref, f32[3,49,64,128]{3,2,1,0:T(8,128)S(1)} %shard_map.97.q_ref), custom_call_target="tpu_custom_call" | custom-call | tf_op jit(solution)/shard_map/pallas_call | solution.py:472
  194.7 5.0 %all-to-all-start.1 = ((f32[32,7,8,128]{3,2,1,0:T(8,128)}), f32[32,7,8,128]{3,2,1,0:T(8,128)S(1)}, u32[]{:S(2)}, u32[]{:S(2)}) async-start(f32[32,7,8,128]{3,2,1,0:T(8,128)} %shard_map.98), calls=%async_computation.1 | async-start | bytes 1835008 | tf_op jit(solution)/shard_map/all_to_all | solution.py:557
  200.7 25.8 %all-to-all-done.1.rows_ref = f32[32,7,8,128]{3,2,1,0:T(8,128)S(1)} async-done(((f32[32,7,8,128]{3,2,1,0:T(8,128)}), f32[32,7,8,128]{3,2,1,0:T(8,128)S(1)}, u32[]{:S(2)}, u32[]{:S(2)}) %all-to-all-start.1) | async-done | bytes 917536 | tf_op jit(solution)/shard_map/all_to_all | solution.py:557
  (61 shorter events, 26.6 us)
Async XLA Ops:
  0.6 32.5 %copy-start.5 = (f32[2,4,7,7,128]{4,1,3,2,0:T(4,128)S(1)}, f32[2,4,7,7,128]{4,1,3,2,0:T(4,128)}, u32[]{:S(2)}) copy-start(f32[2,4,7,7,128]{4,1,3,2,0:T(4,128)} %param.10) | copy-start | bytes 602116
  1.6 33.1 %copy-start = (f32[7,8,128]{2,1,0:T(8,128)S(1)}, f32[7,8,128]{2,1,0:T(8,128)}, u32[]{:S(2)}) copy-start(f32[7,8,128]{2,1,0:T(8,128)} %constant.11.clone.dcol_ref) | copy-start | bytes 86020
  1.6 33.1 %copy-start.1 = (f32[3072]{0:T(1024)S(1)}, f32[3072]{0:T(1024)}, u32[]{:S(2)}) copy-start(f32[3072]{0:T(1024)} %constant.10.clone.coef_ref) | copy-start | bytes 36868
  1.7 6.3 %collective-permute-start.4 = (f32[152,128]{1,0:T(8,128)S(1)}, f32[152,128]{1,0:T(8,128)S(1)}, u32[]{:S(2)}, u32[]{:S(2)}) collective-permute-start(f32[152,128]{1,0:T(8,128)S(1)} %pad.4), channel_id=1, source_target_pairs={{0,16},{16,0},{1,17},{17,1},{2,18},{18,2},{3,19},{19,3},{4,20},{20... | collective-permute-start | bytes 233480 | tf_op jit(solution)/shard_map/ppermute | solution.py:534
  8.0 31.3 %collective-permute-start.5 = (f32[2,152,128]{2,1,0:T(8,128)S(1)}, f32[2,152,128]{2,1,0:T(8,128)S(1)}, u32[]{:S(2)}, u32[]{:S(2)}) collective-permute-start(f32[2,152,128]{2,1,0:T(8,128)S(1)} %get-tuple-element.31), channel_id=1, source_target_pairs={{0,32},{32,64},{64,96},{96,0},{1,33},{33,65},{65,97},{97,1},{2,34}... | collective-permute-start | bytes 466952 | tf_op jit(solution)/shard_map/ppermute | solution.py:547
  12.9 26.4 %collective-permute-start.6 = (f32[2,152,128]{2,1,0:T(8,128)S(1)}, f32[2,152,128]{2,1,0:T(8,128)S(1)}, u32[]{:S(2)}, u32[]{:S(2)}) collective-permute-start(f32[2,152,128]{2,1,0:T(8,128)S(1)} %get-tuple-element.31), channel_id=1, source_target_pairs={{0,64},{32,96},{64,0},{96,32},{1,65},{33,97},{65,1},{97,33},{2,66}... | collective-permute-start | bytes 466952 | tf_op jit(solution)/shard_map/ppermute | solution.py:547
  17.2 22.1 %collective-permute-start.7 = (f32[2,152,128]{2,1,0:T(8,128)S(1)}, f32[2,152,128]{2,1,0:T(8,128)S(1)}, u32[]{:S(2)}, u32[]{:S(2)}) collective-permute-start(f32[2,152,128]{2,1,0:T(8,128)S(1)} %get-tuple-element.31), channel_id=1, source_target_pairs={{0,96},{32,0},{64,32},{96,64},{1,97},{33,1},{65,33},{97,65},{2,98}... | collective-permute-start | bytes 466952 | tf_op jit(solution)/shard_map/ppermute | solution.py:547
  20.5 5.5 %collective-permute-start = (f32[4,8,128]{2,1,0:T(8,128)S(1)}, f32[4,8,128]{2,1,0:T(8,128)S(1)}, u32[]{:S(2)}, u32[]{:S(2)}) collective-permute-start(f32[4,8,128]{2,1,0:T(8,128)S(1)} %get-tuple-element.15), channel_id=1, source_target_pairs={{0,32},{32,64},{64,96},{96,128},{128,160},{160,192},{192,224},{224... | collective-permute-start | bytes 49160 | tf_op jit(solution)/shard_map/ppermute | solution.py:540
  24.6 7.1 %collective-permute-start.1 = (f32[4,8,128]{2,1,0:T(8,128)S(1)}, f32[4,8,128]{2,1,0:T(8,128)S(1)}, u32[]{:S(2)}, u32[]{:S(2)}) collective-permute-start(f32[4,8,128]{2,1,0:T(8,128)S(1)} %get-tuple-element.16), channel_id=1, source_target_pairs={{32,0},{64,32},{96,64},{128,96},{160,128},{192,160},{224,192},{256... | collective-permute-start | bytes 49160 | tf_op jit(solution)/shard_map/ppermute | solution.py:541
  26.0 7.2 %collective-permute-start.2 = (f32[4,8,128]{2,1,0:T(8,128)S(1)}, f32[4,8,128]{2,1,0:T(8,128)S(1)}, u32[]{:S(2)}, u32[]{:S(2)}) collective-permute-start(f32[4,8,128]{2,1,0:T(8,128)S(1)} %get-tuple-element.17), channel_id=1, source_target_pairs={{0,8},{8,16},{16,24},{1,9},{9,17},{17,25},{2,10},{10,18},{18,26},{... | collective-permute-start | bytes 49160 | tf_op jit(solution)/shard_map/ppermute | solution.py:542
  31.7 3.1 %collective-permute-start.3 = (f32[4,8,128]{2,1,0:T(8,128)S(1)}, f32[4,8,128]{2,1,0:T(8,128)S(1)}, u32[]{:S(2)}, u32[]{:S(2)}) collective-permute-start(f32[4,8,128]{2,1,0:T(8,128)S(1)} %get-tuple-element.18), channel_id=1, source_target_pairs={{8,0},{16,8},{24,16},{9,1},{17,9},{25,17},{10,2},{18,10},{26,18},{... | collective-permute-start | bytes 49160 | tf_op jit(solution)/shard_map/ppermute | solution.py:543
  39.3 65.2 %all-to-all-start = ((f32[32,7,8,128]{3,2,1,0:T(8,128)}), f32[32,7,8,128]{3,2,1,0:T(8,128)S(1)}, u32[]{:S(2)}, u32[]{:S(2)}) async-start(f32[32,7,8,128]{3,2,1,0:T(8,128)} %get-tuple-element.26), calls=%async_computation | async-start | bytes 1835008 | tf_op jit(solution)/shard_map/all_to_all | solution.py:550
  52.4 42.7 %collective-permute-start.14 = (f32[4,2,152,128]{3,2,1,0:T(8,128)S(1)}, f32[4,2,152,128]{3,2,1,0:T(8,128)S(1)}, u32[]{:S(2)}, u32[]{:S(2)}) collective-permute-start(f32[4,2,152,128]{3,2,1,0:T(8,128)S(1)} %pad_maximum_fusion), channel_id=1, source_target_pairs={{0,128},{128,256},{256,384},{384,0},{1,129},{129,257},{257,385},{3... | collective-permute-start | bytes 1867784 | tf_op jit(solution)/shard_map/ppermute | solution.py:511
  60.1 38.7 %collective-permute-start.16 = (f32[4,2,152,128]{3,2,1,0:T(8,128)S(1)}, f32[4,2,152,128]{3,2,1,0:T(8,128)S(1)}, u32[]{:S(2)}, u32[]{:S(2)}) collective-permute-start(f32[4,2,152,128]{3,2,1,0:T(8,128)S(1)} %pad_maximum_fusion), channel_id=1, source_target_pairs={{0,384},{128,0},{256,128},{384,256},{1,385},{129,1},{257,129},{385... | collective-permute-start | bytes 1867784 | tf_op jit(solution)/shard_map/ppermute | solution.py:512
  95.9 15.4 %collective-permute-start.15 = (f32[2,2,152,128]{3,2,1,0:T(8,128)}, f32[2,2,152,128]{3,2,1,0:T(8,128)}, u32[]{:S(2)}, u32[]{:S(2)}) collective-permute-start(f32[2,2,152,128]{3,2,1,0:T(8,128)} %slice.18), channel_id=1, source_target_pairs={{0,128},{128,256},{256,384},{384,0},{1,129},{129,257},{257,385},{3... | collective-permute-start | bytes 933896 | tf_op jit(solution)/shard_map/ppermute | solution.py:515
  99.5 21.2 %collective-permute-start.17 = (f32[2,2,152,128]{3,2,1,0:T(8,128)}, f32[2,2,152,128]{3,2,1,0:T(8,128)}, u32[]{:S(2)}, u32[]{:S(2)}) collective-permute-start(f32[2,2,152,128]{3,2,1,0:T(8,128)} %slice.19), channel_id=1, source_target_pairs={{0,384},{128,0},{256,128},{384,256},{1,385},{129,1},{257,129},{385... | collective-permute-start | bytes 933896 | tf_op jit(solution)/shard_map/ppermute | solution.py:516
  121.8 37.9 %collective-permute-start.18 = (f32[4,4,2,152,128]{4,3,2,1,0:T(8,128)S(1)}, f32[4,4,2,152,128]{4,3,2,1,0:T(8,128)S(1)}, u32[]{:S(2)}, u32[]{:S(2)}) collective-permute-start(f32[4,4,2,152,128]{4,3,2,1,0:T(8,128)S(1)} %bitcast.15), channel_id=1, source_target_pairs={{0,8},{8,0},{1,9},{9,1},{2,10},{10,2},{3,11},{11,3},{4,12},{12,4},... | collective-permute-start | bytes 7471112 | tf_op jit(solution)/shard_map/ppermute | solution.py:554
  123.8 7.4 %collective-permute-start.8 = (f32[4,7,8,128]{3,2,1,0:T(8,128)S(1)}, f32[4,7,8,128]{3,2,1,0:T(8,128)S(1)}, u32[]{:S(2)}, u32[]{:S(2)}) collective-permute-start(f32[4,7,8,128]{3,2,1,0:T(8,128)S(1)} %bitcast_reduce_fusion), channel_id=1, source_target_pairs={{0,16},{16,0},{1,17},{17,1},{2,18},{18,2},{3,19},{19,3},{4,20},{20... | collective-permute-start | bytes 344072 | tf_op jit(solution)/shard_map/ppermute | solution.py:522
  131.2 11.9 %collective-permute-start.9 = (f32[2,4,7,8,128]{4,3,2,1,0:T(8,128)S(1)}, f32[2,4,7,8,128]{4,3,2,1,0:T(8,128)S(1)}, u32[]{:S(2)}, u32[]{:S(2)}) collective-permute-start(f32[2,4,7,8,128]{4,3,2,1,0:T(8,128)S(1)} %pad_maximum_fusion.1), channel_id=1, source_target_pairs={{0,128},{128,256},{256,384},{384,0},{1,129},{129,257},{257,385},{3... | collective-permute-start | bytes 688136 | tf_op jit(solution)/shard_map/ppermute | solution.py:511
  133.8 13.5 %collective-permute-start.11 = (f32[2,4,7,8,128]{4,3,2,1,0:T(8,128)S(1)}, f32[2,4,7,8,128]{4,3,2,1,0:T(8,128)S(1)}, u32[]{:S(2)}, u32[]{:S(2)}) collective-permute-start(f32[2,4,7,8,128]{4,3,2,1,0:T(8,128)S(1)} %pad_maximum_fusion.1), channel_id=1, source_target_pairs={{0,384},{128,0},{256,128},{384,256},{1,385},{129,1},{257,129},{385... | collective-permute-start | bytes 688136 | tf_op jit(solution)/shard_map/ppermute | solution.py:512
  143.1 10.7 %collective-permute-start.10 = (f32[1,4,7,8,128]{4,3,2,1,0:T(8,128)S(1)}, f32[1,4,7,8,128]{4,3,2,1,0:T(8,128)S(1)}, u32[]{:S(2)}, u32[]{:S(2)}) collective-permute-start(f32[1,4,7,8,128]{4,3,2,1,0:T(8,128)S(1)} %slice.16), channel_id=1, source_target_pairs={{0,128},{128,256},{256,384},{384,0},{1,129},{129,257},{257,385},{3... | collective-permute-start | bytes 344072 | tf_op jit(solution)/shard_map/ppermute | solution.py:515
  147.3 10.4 %collective-permute-start.12 = (f32[1,4,7,8,128]{4,3,2,1,0:T(8,128)S(1)}, f32[1,4,7,8,128]{4,3,2,1,0:T(8,128)S(1)}, u32[]{:S(2)}, u32[]{:S(2)}) collective-permute-start(f32[1,4,7,8,128]{4,3,2,1,0:T(8,128)S(1)} %slice.17), channel_id=1, source_target_pairs={{0,384},{128,0},{256,128},{384,256},{1,385},{129,1},{257,129},{385... | collective-permute-start | bytes 344072 | tf_op jit(solution)/shard_map/ppermute | solution.py:516
  157.8 4.4 %collective-permute-start.13 = (f32[4,2,4,7,8,128]{5,4,3,2,1,0:T(8,128)S(1)}, f32[4,2,4,7,8,128]{5,4,3,2,1,0:T(8,128)S(1)}, u32[]{:S(2)}, u32[]{:S(2)}) collective-permute-start(f32[4,2,4,7,8,128]{5,4,3,2,1,0:T(8,128)S(1)} %bitcast.17), channel_id=1, source_target_pairs={{0,8},{8,0},{1,9},{9,1},{2,10},{10,2},{3,11},{11,3},{4,12},{12,4},... | collective-permute-start | bytes 2752520 | tf_op jit(solution)/shard_map/ppermute | solution.py:525
  194.7 31.8 %all-to-all-start.1 = ((f32[32,7,8,128]{3,2,1,0:T(8,128)}), f32[32,7,8,128]{3,2,1,0:T(8,128)S(1)}, u32[]{:S(2)}, u32[]{:S(2)}) async-start(f32[32,7,8,128]{3,2,1,0:T(8,128)} %shard_map.98), calls=%async_computation.1 | async-start | bytes 1835008 | tf_op jit(solution)/shard_map/all_to_all | solution.py:557
  (3 other events, 68.6 us)

commit v5 on v4

--- a/solution.py
+++ b/solution.py
@@ -7,11 +7,12 @@
 from jax.sharding import Mesh
 from jax.sharding import PartitionSpec as P
 
-FLOW = ("z", "xh")
+FLOW = ("zh", "zl", "xh")
 CROSS = ("xl", "core")
-PLANE = ("z", "xh", "xl", "core")
-ROWS = ("xh", "y")
-SPLIT = (4, 4, 2, 2, 8)
+PLANE = ("zh", "zl", "xh", "xl", "core")
+RING_X = ("xh", "xl")
+ROWS = ("zh", "y")
+SPLIT = (4, 2, 2, 2, 2, 8)
 
 EY = 16
 NZ = 32
@@ -276,22 +277,30 @@
     )
 
 
+def places():
+    zh, zl = lax.axis_index("zh"), lax.axis_index("zl")
+    xh, xl = lax.axis_index("xh"), lax.axis_index("xl")
+    return zh, zl, xh, xl, lax.axis_index("core")
+
+
 def metric_kernel(same_ref, other_ref, q_ref):
-    z, xh = lax.axis_index("z"), lax.axis_index("xh")
-    xl, core = lax.axis_index("xl"), lax.axis_index("core")
+    zh, zl, xh, xl, core = places()
+    flip = [zl, 1 - zl]
 
     def chunk(quarter, carry):
         from_xl, half = quarter // 2, quarter % 2
-        flip = (xl + from_xl) % 2
-        back_z = [(z - half * 2 - s + 4) % 4 for s in range(2)]
-        back_h = [(xh - s + 4) % 4 for s in range(4)]
+        back_x = [(2 * xh + xl - 2 * s - from_xl + 4) % 4 for s in range(2)]
+        back_z = [(zh - half * 2 - s + 4) % 4 for s in range(2)]
         for ref, from_core in ((same_ref, core), (other_ref, 1 - core)):
             start = ((from_xl * 2 + from_core) * 2 + half) * 8
             here = pl.ds(pl.multiple_of(start, 8), 8)
             for tile in range(19):
                 rows = slice(8 * tile, 8 * tile + 8)
                 block = jnp.stack(
-                    [ref[back_z[s // 4], back_h[s % 4], flip, rows, :] for s in range(8)]
+                    [
+                        ref[back_x[s % 2], back_z[s // 4], flip[s // 2 % 2], rows, :]
+                        for s in range(8)
+                    ]
                 )
                 block = jnp.swapaxes(block, 0, 1)
                 for j in range(8):
@@ -318,27 +327,29 @@
 def solve_kernel(
     count_ref, same_ref, other_ref, q_ref, out_ref, r_ref, d_ref, im_ref, mk_ref, x_ref, t_ref
 ):
-    z, xh, y = lax.axis_index("z"), lax.axis_index("xh"), lax.axis_index("y")
-    xl, core = lax.axis_index("xl"), lax.axis_index("core")
+    zh, zl, xh, xl, core = places()
     e = xl * 2 + core
-    row_id = 4 * y + xh
+    row_id = 4 * lax.axis_index("y") + zh
     harmonic = jnp.where(row_id == 1, NZ // 2, row_id // 2).astype(jnp.float32)
     wavesq = harmonic * harmonic * (SPAN_UNIT * SPAN_UNIT)
-    own = pl.ds(pl.multiple_of((e * 2 + z // 2) * 8, 8), 8)
+    own = pl.ds(pl.multiple_of(e * 16, 16), 16)
     flipped = DERIV.T
     zero = jnp.zeros((8, 128), jnp.float32)
 
     def here(k):
         return pl.ds(pl.multiple_of(k * 8, 8), 8)
 
+    flip = [zl, 1 - zl]
+
     def chunk_in(quarter, carry):
         from_xl, half = quarter // 2, quarter % 2
+        back = [(2 * xh + xl - 2 * s - from_xl + 4) % 4 for s in range(2)]
         for ref, from_core in ((same_ref, core), (other_ref, 1 - core)):
             at = here((from_xl * 2 + from_core) * 2 + half)
-            flip = (xl + from_xl) % 2
-            back = [(z - half * 2 - s + 4) % 4 for s in range(2)]
             for i in range(7):
-                block = jnp.stack([ref[back[s // 4], flip, s % 4, i] for s in range(8)])
+                block = jnp.stack(
+                    [ref[back[s % 2], flip[s // 2 % 2], half * 2 + s // 4, i] for s in range(8)]
+                )
                 block = jnp.swapaxes(block, 0, 1)
                 for j in range(7):
                     n = i * 7 + j
@@ -350,7 +361,7 @@
 
     lax.fori_loop(0, 4, chunk_in, 0)
     for n in range(49):
-        x_ref[n] = zero
+        x_ref[n] = jnp.zeros((16, 128), jnp.float32)
 
     lane = lax.broadcasted_iota(jnp.int32, (64, 128), 1)
     spot = lax.broadcasted_iota(jnp.int32, (64, 128), 0)
@@ -434,7 +445,7 @@
         step = rho / total(lax.fori_loop(0, 8, image, zero))
         join()
         for n in range(49):
-            x_ref[n] = x_ref[n] + step * d_ref[n, own, :]
+            x_ref[n] = x_ref[n] + step[0:1] * d_ref[n, own, :]
 
         def descend(k, acc):
             at = here(k)
@@ -454,14 +465,15 @@
     lax.fori_loop(0, count_ref[row_id], sweep, (rho, zero))
 
     for i in range(7):
-        block = jnp.stack([x_ref[i * 7 + j] for j in range(7)] + [zero])
-        block = jnp.swapaxes(block, 0, 1)
-        for s in range(8):
-            t_ref[s, i] = block[s]
-    first = (z % 2) * 4
+        for half in range(2):
+            rows = slice(8 * half, 8 * half + 8)
+            block = jnp.stack([x_ref[i * 7 + j, rows, :] for j in range(7)] + [zero])
+            block = jnp.swapaxes(block, 0, 1)
+            for s in range(8):
+                t_ref[8 * half + s, i] = block[s]
     for to in range(4):
         for i in range(7):
-            value = t_ref[first + to, i]
+            value = t_ref[4 * to + 2 * zl + xh, i]
             for copy in range(8):
                 out_ref[to * 8 + copy, i] = value
 
@@ -476,8 +488,8 @@
         out_specs=vmem,
         scratch_shapes=[
             field, field, field, field,
-            pltpu.VMEM((49, 8, 128), jnp.float32),
-            pltpu.VMEM((8, 7, 8, 128), jnp.float32),
+            pltpu.VMEM((49, 16, 128), jnp.float32),
+            pltpu.VMEM((16, 7, 8, 128), jnp.float32),
         ],
         compiler_params=pltpu.CompilerParams(vmem_limit_bytes=40 * MIB),
     )(counts, same, other, metrics)
@@ -507,20 +519,20 @@
 TURNS = [[(at, (at + back) % 4) for at in range(4)] for back in range(1, 4)]
 
 
-def around(mine):
-    behind = lax.ppermute(mine, "z", TURNS[0])
-    before = lax.ppermute(mine, "z", TURNS[2])
+def around(mine, axis):
+    behind = lax.ppermute(mine, axis, TURNS[0])
+    before = lax.ppermute(mine, axis, TURNS[2])
     half = mine.shape[0] // 2
     far = [
-        lax.ppermute(behind[:half], "z", TURNS[0]),
-        lax.ppermute(before[half:], "z", TURNS[2]),
+        lax.ppermute(behind[:half], axis, TURNS[0]),
+        lax.ppermute(before[half:], axis, TURNS[2]),
     ]
     return behind, far, before
 
 
 def gather_row(mine):
-    pair = jnp.stack([mine, lax.ppermute(mine, "xl", SWAP)])
-    behind, far, before = around(pair)
+    pair = jnp.stack([mine, lax.ppermute(mine, "zl", SWAP)])
+    behind, far, before = around(pair, RING_X)
     same = jnp.concatenate([pair, behind, *far, before]).reshape(4, 2, 4, 7, 8, 128)
     return same, lax.ppermute(same, "core", SWAP)
 
@@ -531,9 +543,8 @@
 
 def local(stress, velocity_grad, velocity, metric, iteration_counts):
     packed = jnp.pad(metric.reshape(147, 128), ((0, 5), (0, 0)))
-    beside = lax.ppermute(packed, "xl", SWAP)
+    beside = lax.ppermute(packed, "zl", SWAP)
     right, left, up, down = pack_faces(stress)
-    pair = jnp.stack([after(packed, right), beside])
     ahead = [(c, c + 1) for c in range(15)]
     above = [(e, e + 1) for e in range(3)]
     faces = (
@@ -542,15 +553,18 @@
         lax.ppermute(up, CROSS, above),
         lax.ppermute(down, CROSS, [(b, a) for a, b in above]),
     )
+    pair = jnp.stack([after(packed, faces), beside])
+    behind, far, before = around(pair, "zh")
     faces = after(faces, pair)
     new_stress, parts = stress_step(stress, velocity_grad, velocity, faces)
-    ring = jnp.stack([pair] + [lax.ppermute(pair, "xh", turn) for turn in TURNS])
-    parts = after(parts, ring)
-    behind, far, before = around(ring)
+    parts = after(parts, (behind, before))
+    ring = jnp.concatenate([pair, behind, *far, before])
+    behind, far, before = around(ring, RING_X)
     parts = lax.all_to_all(parts, ROWS, 0, 0, tiled=True)
     mine = jnp.sum(parts.reshape(4, 8, 7, 8, 128), axis=1)
-    ring = after(ring, mine)
-    plane = jnp.concatenate([ring, behind, *far, before]).reshape(4, 4, 2, 152, 128)
+    ring = after(ring.reshape(4, 2, 152, 128), mine)
+    plane = [part.reshape(-1, 2, 152, 128) for part in (behind, *far, before)]
+    plane = jnp.concatenate([ring, *plane]).reshape(4, 4, 2, 152, 128)
     metrics = metric_fields(plane, lax.ppermute(plane, "core", SWAP))
     same, other = gather_row(mine)
     answer = solve(iteration_counts, same, other, metrics)

time: 229 us -> 220 us (0.961)
  the two profiles are of different devices: /device:TPU:8 before, /device:TPU:14 now
where the time goes in v5:
time: 220 us; the launch traced here: 219 us
  starting transfers between devices  86.9 us (40%)
  waiting for transfers between devices  82.6 us (38%)
  Pallas kernels  40.1 us (18%)
  local copies, waits for them, and re-layouts  7.75 us (4%)
    pallas_call x1, Pallas kernels, solve(): pl.pallas_call(solve_kernel, out_shape=jax.ShapeDtypeStruct((NZ, 7, 8, 12...  32.6 us
    all_to_all x1, waiting for transfers between devices, local(): answer = lax.all_to_all(answer, ROWS, 0, 0, tiled=True)  27.7 us
    ppermute x3, waiting for transfers between devices, around(): lax.ppermute(behind[:half], axis, TURNS[0])  21.3 us
    ppermute x3, starting transfers between devices, around(): behind = lax.ppermute(mine, axis, TURNS[0])  14.9 us
    ppermute x3, waiting for transfers between devices, around(): behind = lax.ppermute(mine, axis, TURNS[0])  14.7 us
    ppermute x3, starting transfers between devices, around(): lax.ppermute(behind[:half], axis, TURNS[0])  13.3 us
    ppermute x3, starting transfers between devices, around(): before = lax.ppermute(mine, axis, TURNS[2])  11.7 us
    all_to_all x1, starting transfers between devices, local(): parts = lax.all_to_all(parts, ROWS, 0, 0, tiled=True)  11.5 us
  transfers between devices with their start and end apart: 22, of which 12 were waited for; matrix products, arithmetic and copies ran while one was open for 2% of the time, Pallas kernels for 3%

profile of v5, /device:TPU:14, one launch (start us, length us, event | category | flops | bytes accessed | tf_op | source)
XLA Modules:
  0.0 218.6 jit_solution(16884495060125355518)
XLA Ops:
  1.7 4.3 %collective-permute-start.4 = (f32[152,128]{1,0:T(8,128)S(1)}, f32[152,128]{1,0:T(8,128)S(1)}, u32[]{:S(2)}, u32[]{:S(2)}) collective-permute-start(f32[152,128]{1,0:T(8,128)S(1)} %pad.4), channel_id=1, source_target_pairs={{0,64},{64,0},{1,65},{65,1},{2,66},{66,2},{3,67},{67,3},{4,68},{68... | collective-permute-start | bytes 233480 | tf_op jit(solution)/shard_map/ppermute | solution.py:546
  7.8 2.8 %collective-permute-start = (f32[4,8,128]{2,1,0:T(8,128)S(1)}, f32[4,8,128]{2,1,0:T(8,128)S(1)}, u32[]{:S(2)}, u32[]{:S(2)}) collective-permute-start(f32[4,8,128]{2,1,0:T(8,128)S(1)} %get-tuple-element.15), channel_id=1, source_target_pairs={{0,32},{32,64},{64,96},{96,128},{128,160},{160,192},{192,224},{224... | collective-permute-start | bytes 49160 | tf_op jit(solution)/shard_map/ppermute | solution.py:551
  10.6 4.6 %collective-permute-start.1 = (f32[4,8,128]{2,1,0:T(8,128)S(1)}, f32[4,8,128]{2,1,0:T(8,128)S(1)}, u32[]{:S(2)}, u32[]{:S(2)}) collective-permute-start(f32[4,8,128]{2,1,0:T(8,128)S(1)} %get-tuple-element.16), channel_id=1, source_target_pairs={{32,0},{64,32},{96,64},{128,96},{160,128},{192,160},{224,192},{256... | collective-permute-start | bytes 49160 | tf_op jit(solution)/shard_map/ppermute | solution.py:552
  17.1 3.6 %collective-permute-start.3 = (f32[4,8,128]{2,1,0:T(8,128)S(1)}, f32[4,8,128]{2,1,0:T(8,128)S(1)}, u32[]{:S(2)}, u32[]{:S(2)}) collective-permute-start(f32[4,8,128]{2,1,0:T(8,128)S(1)} %get-tuple-element.18), channel_id=1, source_target_pairs={{8,0},{16,8},{24,16},{9,1},{17,9},{25,17},{10,2},{18,10},{26,18},{... | collective-permute-start | bytes 49160 | tf_op jit(solution)/shard_map/ppermute | solution.py:554
  22.2 6.1 %collective-permute-start.5 = (f32[2,152,128]{2,1,0:T(8,128)S(1)}, f32[2,152,128]{2,1,0:T(8,128)S(1)}, u32[]{:S(2)}, u32[]{:S(2)}) collective-permute-start(f32[2,152,128]{2,1,0:T(8,128)S(1)} %pad_maximum_fusion.1), channel_id=1, source_target_pairs={{0,128},{128,256},{256,384},{384,0},{1,129},{129,257},{257,385},{3... | collective-permute-start | bytes 466952 | tf_op jit(solution)/shard_map/ppermute | solution.py:523
  28.3 5.9 %collective-permute-start.6 = (f32[2,152,128]{2,1,0:T(8,128)S(1)}, f32[2,152,128]{2,1,0:T(8,128)S(1)}, u32[]{:S(2)}, u32[]{:S(2)}) collective-permute-start(f32[2,152,128]{2,1,0:T(8,128)S(1)} %pad_maximum_fusion.1), channel_id=1, source_target_pairs={{0,384},{128,0},{256,128},{384,256},{1,385},{129,1},{257,129},{385... | collective-permute-start | bytes 466952 | tf_op jit(solution)/shard_map/ppermute | solution.py:524
  34.4 4.5 %shard_map.96 = (f32[6,4,7,7,128]{4,3,2,1,0:T(8,128)S(1)}, f32[32,7,8,128]{3,2,1,0:T(8,128)}) custom-call(f32[3072]{0:T(1024)S(1)} %copy-done.1, f32[6,4,7,7,128]{4,3,2,1,0:T(8,128)S(1)} %copy.11.s_ref, f32[9,4,7,7,128]{4,3,2,1,0:T(8,128)S(1)} %copy.12.g_ref, f32[2,4,7,7,128]{4,3,2,1,0:T(8,128)S(1)} %copy.13.v_ref, ...), custom_call_target="tpu_custom_call" | custom-call | tf_op jit(solution)/shard_map/pallas_call | solution.py:257
  40.2 11.5 %all-to-all-start = ((f32[32,7,8,128]{3,2,1,0:T(8,128)}), f32[32,7,8,128]{3,2,1,0:T(8,128)S(1)}, u32[]{:S(2)}, u32[]{:S(2)}) async-start(f32[32,7,8,128]{3,2,1,0:T(8,128)} %get-tuple-element.26), calls=%async_computation | async-start | bytes 1835008 | tf_op jit(solution)/shard_map/all_to_all | solution.py:563
  51.7 4.3 %collective-permute-start.13 = (f32[1,152,128]{2,1,0:T(8,128)S(1)}, f32[1,152,128]{2,1,0:T(8,128)S(1)}, u32[]{:S(2)}, u32[]{:S(2)}) collective-permute-start(f32[1,152,128]{2,1,0:T(8,128)S(1)} %slice.26), channel_id=1, source_target_pairs={{0,128},{128,256},{256,384},{384,0},{1,129},{129,257},{257,385},{3... | collective-permute-start | bytes 233480 | tf_op jit(solution)/shard_map/ppermute | solution.py:527
  56.0 3.7 %collective-permute-start.14 = (f32[1,152,128]{2,1,0:T(8,128)S(1)}, f32[1,152,128]{2,1,0:T(8,128)S(1)}, u32[]{:S(2)}, u32[]{:S(2)}) collective-permute-start(f32[1,152,128]{2,1,0:T(8,128)S(1)} %slice.27), channel_id=1, source_target_pairs={{0,384},{128,0},{256,128},{384,256},{1,385},{129,1},{257,129},{385... | collective-permute-start | bytes 233480 | tf_op jit(solution)/shard_map/ppermute | solution.py:528
  59.7 17.1 %collective-permute-done.13 = f32[1,152,128]{2,1,0:T(8,128)S(1)} collective-permute-done((f32[1,152,128]{2,1,0:T(8,128)S(1)}, f32[1,152,128]{2,1,0:T(8,128)S(1)}, u32[]{:S(2)}, u32[]{:S(2)}) %collective-permute-start.13) | collective-permute-done | bytes 77856 | tf_op jit(solution)/shard_map/ppermute | solution.py:527
  76.9 6.9 %collective-permute-start.15 = (f32[8,152,128]{2,1,0:T(8,128)S(1)}, f32[8,152,128]{2,1,0:T(8,128)S(1)}, u32[]{:S(2)}, u32[]{:S(2)}) collective-permute-start(f32[8,152,128]{2,1,0:T(8,128)S(1)} %constant_dynamic-update-slice_fusion.6), channel_id=1, source_target_pairs={{0,16},{16,32},{32,48},{48,0},{1,17},{17,33},{33,49},{49,1},{2,18}... | collective-permute-start | bytes 1867784 | tf_op jit(solution)/shard_map/ppermute | solution.py:523
  85.7 11.5 %collective-permute-done.15 = f32[8,152,128]{2,1,0:T(8,128)S(1)} collective-permute-done((f32[8,152,128]{2,1,0:T(8,128)S(1)}, f32[8,152,128]{2,1,0:T(8,128)S(1)}, u32[]{:S(2)}, u32[]{:S(2)}) %collective-permute-start.15) | collective-permute-done | bytes 622624 | tf_op jit(solution)/shard_map/ppermute | solution.py:523
  97.9 5.6 %collective-permute-start.16 = (f32[4,152,128]{2,1,0:T(8,128)}, f32[4,152,128]{2,1,0:T(8,128)}, u32[]{:S(2)}, u32[]{:S(2)}) collective-permute-start(f32[4,152,128]{2,1,0:T(8,128)} %slice.28), channel_id=1, source_target_pairs={{0,16},{16,32},{32,48},{48,0},{1,17},{17,33},{33,49},{49,1},{2,18}... | collective-permute-start | bytes 933896 | tf_op jit(solution)/shard_map/ppermute | solution.py:527
  106.4 3.4 %collective-permute-done.16 = f32[4,152,128]{2,1,0:T(8,128)} collective-permute-done((f32[4,152,128]{2,1,0:T(8,128)}, f32[4,152,128]{2,1,0:T(8,128)}, u32[]{:S(2)}, u32[]{:S(2)}) %collective-permute-start.16) | collective-permute-done | bytes 311328 | tf_op jit(solution)/shard_map/ppermute | solution.py:527
  110.7 5.1 %collective-permute-done.18 = f32[4,152,128]{2,1,0:T(8,128)} collective-permute-done((f32[4,152,128]{2,1,0:T(8,128)}, f32[4,152,128]{2,1,0:T(8,128)}, u32[]{:S(2)}, u32[]{:S(2)}) %collective-permute-start.18) | collective-permute-done | bytes 311328 | tf_op jit(solution)/shard_map/ppermute | solution.py:528
  120.7 5.5 %collective-permute-done.7 = f32[4,7,8,128]{3,2,1,0:T(8,128)S(1)} collective-permute-done((f32[4,7,8,128]{3,2,1,0:T(8,128)S(1)}, f32[4,7,8,128]{3,2,1,0:T(8,128)S(1)}, u32[]{:S(2)}, u32[]{:S(2)}) %collective-permute-start.7) | collective-permute-done | bytes 114720 | tf_op jit(solution)/shard_map/ppermute | solution.py:534
  128.2 3.9 %collective-permute-start.10 = (f32[2,4,7,8,128]{4,3,2,1,0:T(8,128)S(1)}, f32[2,4,7,8,128]{4,3,2,1,0:T(8,128)S(1)}, u32[]{:S(2)}, u32[]{:S(2)}) collective-permute-start(f32[2,4,7,8,128]{4,3,2,1,0:T(8,128)S(1)} %pad_maximum_fusion), channel_id=1, source_target_pairs={{0,48},{16,0},{32,16},{48,32},{1,49},{17,1},{33,17},{49,33},{2,50}... | collective-permute-start | bytes 688136 | tf_op jit(solution)/shard_map/ppermute | solution.py:524
  132.1 3.2 %collective-permute-done.8 = f32[2,4,7,8,128]{4,3,2,1,0:T(8,128)S(1)} collective-permute-done((f32[2,4,7,8,128]{4,3,2,1,0:T(8,128)S(1)}, f32[2,4,7,8,128]{4,3,2,1,0:T(8,128)S(1)}, u32[]{:S(2)}, u32[]{:S(2)}) %collective-permute-start.8) | collective-permute-done | bytes 229408 | tf_op jit(solution)/shard_map/ppermute | solution.py:523
  135.4 3.4 %collective-permute-start.9 = (f32[1,4,7,8,128]{4,3,2,1,0:T(8,128)S(1)}, f32[1,4,7,8,128]{4,3,2,1,0:T(8,128)S(1)}, u32[]{:S(2)}, u32[]{:S(2)}) collective-permute-start(f32[1,4,7,8,128]{4,3,2,1,0:T(8,128)S(1)} %slice.24), channel_id=1, source_target_pairs={{0,16},{16,32},{32,48},{48,0},{1,17},{17,33},{33,49},{49,1},{2,18}... | collective-permute-start | bytes 344072 | tf_op jit(solution)/shard_map/ppermute | solution.py:527
  142.1 4.6 %collective-permute-done.11 = f32[1,4,7,8,128]{4,3,2,1,0:T(8,128)S(1)} collective-permute-done((f32[1,4,7,8,128]{4,3,2,1,0:T(8,128)S(1)}, f32[1,4,7,8,128]{4,3,2,1,0:T(8,128)S(1)}, u32[]{:S(2)}, u32[]{:S(2)}) %collective-permute-start.11) | collective-permute-done | bytes 114720 | tf_op jit(solution)/shard_map/ppermute | solution.py:528
  151.1 32.6 %shard_map.98 = f32[32,7,8,128]{3,2,1,0:T(8,128)} custom-call(s32[32]{0:T(128)S(1)} %copy-done.3, f32[4,2,4,7,8,128]{5,4,3,2,1,0:T(8,128)S(1)} %bitcast.20, f32[4,2,4,7,8,128]{5,4,3,2,1,0:T(8,128)S(1)} %collective-permute-done.12.other_ref, f32[3,49,64,128]{3,2,1,0:T(8,128)S(1)} %shard_map.97.q_ref), custom_call_target="tpu_custom_call" | custom-call | tf_op jit(solution)/shard_map/pallas_call | solution.py:484
  183.8 4.5 %all-to-all-start.1 = ((f32[32,7,8,128]{3,2,1,0:T(8,128)}), f32[32,7,8,128]{3,2,1,0:T(8,128)S(1)}, u32[]{:S(2)}, u32[]{:S(2)}) async-start(f32[32,7,8,128]{3,2,1,0:T(8,128)} %shard_map.98), calls=%async_computation.1 | async-start | bytes 1835008 | tf_op jit(solution)/shard_map/all_to_all | solution.py:571
  189.3 27.7 %all-to-all-done.1.rows_ref = f32[32,7,8,128]{3,2,1,0:T(8,128)S(1)} async-done(((f32[32,7,8,128]{3,2,1,0:T(8,128)}), f32[32,7,8,128]{3,2,1,0:T(8,128)S(1)}, u32[]{:S(2)}, u32[]{:S(2)}) %all-to-all-start.1) | async-done | bytes 917536 | tf_op jit(solution)/shard_map/all_to_all | solution.py:571
  (70 shorter events, 31.1 us)
Async XLA Ops:
  0.6 33.8 %copy-start = (f32[7,8,128]{2,1,0:T(8,128)S(1)}, f32[7,8,128]{2,1,0:T(8,128)}, u32[]{:S(2)}) copy-start(f32[7,8,128]{2,1,0:T(8,128)} %constant.11.clone.dcol_ref) | copy-start | bytes 86020
  0.6 33.8 %copy-start.1 = (f32[3072]{0:T(1024)S(1)}, f32[3072]{0:T(1024)}, u32[]{:S(2)}) copy-start(f32[3072]{0:T(1024)} %constant.10.clone.coef_ref) | copy-start | bytes 36868
  1.7 20.5 %collective-permute-start.4 = (f32[152,128]{1,0:T(8,128)S(1)}, f32[152,128]{1,0:T(8,128)S(1)}, u32[]{:S(2)}, u32[]{:S(2)}) collective-permute-start(f32[152,128]{1,0:T(8,128)S(1)} %pad.4), channel_id=1, source_target_pairs={{0,64},{64,0},{1,65},{65,1},{2,66},{66,2},{3,67},{67,3},{4,68},{68... | collective-permute-start | bytes 233480 | tf_op jit(solution)/shard_map/ppermute | solution.py:546
  7.8 12.9 %collective-permute-start = (f32[4,8,128]{2,1,0:T(8,128)S(1)}, f32[4,8,128]{2,1,0:T(8,128)S(1)}, u32[]{:S(2)}, u32[]{:S(2)}) collective-permute-start(f32[4,8,128]{2,1,0:T(8,128)S(1)} %get-tuple-element.15), channel_id=1, source_target_pairs={{0,32},{32,64},{64,96},{96,128},{128,160},{160,192},{192,224},{224... | collective-permute-start | bytes 49160 | tf_op jit(solution)/shard_map/ppermute | solution.py:551
  10.6 10.2 %collective-permute-start.1 = (f32[4,8,128]{2,1,0:T(8,128)S(1)}, f32[4,8,128]{2,1,0:T(8,128)S(1)}, u32[]{:S(2)}, u32[]{:S(2)}) collective-permute-start(f32[4,8,128]{2,1,0:T(8,128)S(1)} %get-tuple-element.16), channel_id=1, source_target_pairs={{32,0},{64,32},{96,64},{128,96},{160,128},{192,160},{224,192},{256... | collective-permute-start | bytes 49160 | tf_op jit(solution)/shard_map/ppermute | solution.py:552
  15.2 5.6 %collective-permute-start.2 = (f32[4,8,128]{2,1,0:T(8,128)S(1)}, f32[4,8,128]{2,1,0:T(8,128)S(1)}, u32[]{:S(2)}, u32[]{:S(2)}) collective-permute-start(f32[4,8,128]{2,1,0:T(8,128)S(1)} %get-tuple-element.17), channel_id=1, source_target_pairs={{0,8},{8,16},{16,24},{1,9},{9,17},{17,25},{2,10},{10,18},{18,26},{... | collective-permute-start | bytes 49160 | tf_op jit(solution)/shard_map/ppermute | solution.py:553
  17.1 5.1 %collective-permute-start.3 = (f32[4,8,128]{2,1,0:T(8,128)S(1)}, f32[4,8,128]{2,1,0:T(8,128)S(1)}, u32[]{:S(2)}, u32[]{:S(2)}) collective-permute-start(f32[4,8,128]{2,1,0:T(8,128)S(1)} %get-tuple-element.18), channel_id=1, source_target_pairs={{8,0},{16,8},{24,16},{9,1},{17,9},{25,17},{10,2},{18,10},{26,18},{... | collective-permute-start | bytes 49160 | tf_op jit(solution)/shard_map/ppermute | solution.py:554
  22.2 16.7 %collective-permute-start.5 = (f32[2,152,128]{2,1,0:T(8,128)S(1)}, f32[2,152,128]{2,1,0:T(8,128)S(1)}, u32[]{:S(2)}, u32[]{:S(2)}) collective-permute-start(f32[2,152,128]{2,1,0:T(8,128)S(1)} %pad_maximum_fusion.1), channel_id=1, source_target_pairs={{0,128},{128,256},{256,384},{384,0},{1,129},{129,257},{257,385},{3... | collective-permute-start | bytes 466952 | tf_op jit(solution)/shard_map/ppermute | solution.py:523
  28.3 11.9 %collective-permute-start.6 = (f32[2,152,128]{2,1,0:T(8,128)S(1)}, f32[2,152,128]{2,1,0:T(8,128)S(1)}, u32[]{:S(2)}, u32[]{:S(2)}) collective-permute-start(f32[2,152,128]{2,1,0:T(8,128)S(1)} %pad_maximum_fusion.1), channel_id=1, source_target_pairs={{0,384},{128,0},{256,128},{384,256},{1,385},{129,1},{257,129},{385... | collective-permute-start | bytes 466952 | tf_op jit(solution)/shard_map/ppermute | solution.py:524
  40.2 66.0 %all-to-all-start = ((f32[32,7,8,128]{3,2,1,0:T(8,128)}), f32[32,7,8,128]{3,2,1,0:T(8,128)S(1)}, u32[]{:S(2)}, u32[]{:S(2)}) async-start(f32[32,7,8,128]{3,2,1,0:T(8,128)} %get-tuple-element.26), calls=%async_computation | async-start | bytes 1835008 | tf_op jit(solution)/shard_map/all_to_all | solution.py:563
  51.7 25.1 %collective-permute-start.13 = (f32[1,152,128]{2,1,0:T(8,128)S(1)}, f32[1,152,128]{2,1,0:T(8,128)S(1)}, u32[]{:S(2)}, u32[]{:S(2)}) collective-permute-start(f32[1,152,128]{2,1,0:T(8,128)S(1)} %slice.26), channel_id=1, source_target_pairs={{0,128},{128,256},{256,384},{384,0},{1,129},{129,257},{257,385},{3... | collective-permute-start | bytes 233480 | tf_op jit(solution)/shard_map/ppermute | solution.py:527
  56.0 20.8 %collective-permute-start.14 = (f32[1,152,128]{2,1,0:T(8,128)S(1)}, f32[1,152,128]{2,1,0:T(8,128)S(1)}, u32[]{:S(2)}, u32[]{:S(2)}) collective-permute-start(f32[1,152,128]{2,1,0:T(8,128)S(1)} %slice.27), channel_id=1, source_target_pairs={{0,384},{128,0},{256,128},{384,256},{1,385},{129,1},{257,129},{385... | collective-permute-start | bytes 233480 | tf_op jit(solution)/shard_map/ppermute | solution.py:528
  76.9 20.3 %collective-permute-start.15 = (f32[8,152,128]{2,1,0:T(8,128)S(1)}, f32[8,152,128]{2,1,0:T(8,128)S(1)}, u32[]{:S(2)}, u32[]{:S(2)}) collective-permute-start(f32[8,152,128]{2,1,0:T(8,128)S(1)} %constant_dynamic-update-slice_fusion.6), channel_id=1, source_target_pairs={{0,16},{16,32},{32,48},{48,0},{1,17},{17,33},{33,49},{49,1},{2,18}... | collective-permute-start | bytes 1867784 | tf_op jit(solution)/shard_map/ppermute | solution.py:523
  83.8 19.8 %collective-permute-start.17 = (f32[8,152,128]{2,1,0:T(8,128)S(1)}, f32[8,152,128]{2,1,0:T(8,128)S(1)}, u32[]{:S(2)}, u32[]{:S(2)}) collective-permute-start(f32[8,152,128]{2,1,0:T(8,128)S(1)} %constant_dynamic-update-slice_fusion.6), channel_id=1, source_target_pairs={{0,48},{16,0},{32,16},{48,32},{1,49},{17,1},{33,17},{49,33},{2,50}... | collective-permute-start | bytes 1867784 | tf_op jit(solution)/shard_map/ppermute | solution.py:524
  97.9 11.8 %collective-permute-start.16 = (f32[4,152,128]{2,1,0:T(8,128)}, f32[4,152,128]{2,1,0:T(8,128)}, u32[]{:S(2)}, u32[]{:S(2)}) collective-permute-start(f32[4,152,128]{2,1,0:T(8,128)} %slice.28), channel_id=1, source_target_pairs={{0,16},{16,32},{32,48},{48,0},{1,17},{17,33},{33,49},{49,1},{2,18}... | collective-permute-start | bytes 933896 | tf_op jit(solution)/shard_map/ppermute | solution.py:527
  104.3 11.5 %collective-permute-start.18 = (f32[4,152,128]{2,1,0:T(8,128)}, f32[4,152,128]{2,1,0:T(8,128)}, u32[]{:S(2)}, u32[]{:S(2)}) collective-permute-start(f32[4,152,128]{2,1,0:T(8,128)} %slice.29), channel_id=1, source_target_pairs={{0,48},{16,0},{32,16},{48,32},{1,49},{17,1},{33,17},{49,33},{2,50}... | collective-permute-start | bytes 933896 | tf_op jit(solution)/shard_map/ppermute | solution.py:528
  116.9 31.8 %collective-permute-start.19 = (f32[4,4,2,152,128]{4,3,2,1,0:T(8,128)S(1)}, f32[4,4,2,152,128]{4,3,2,1,0:T(8,128)S(1)}, u32[]{:S(2)}, u32[]{:S(2)}) collective-permute-start(f32[4,4,2,152,128]{4,3,2,1,0:T(8,128)S(1)} %bitcast.17), channel_id=1, source_target_pairs={{0,8},{8,0},{1,9},{9,1},{2,10},{10,2},{3,11},{11,3},{4,12},{12,4},... | collective-permute-start | bytes 7471112 | tf_op jit(solution)/shard_map/ppermute | solution.py:568
  118.8 7.4 %collective-permute-start.7 = (f32[4,7,8,128]{3,2,1,0:T(8,128)S(1)}, f32[4,7,8,128]{3,2,1,0:T(8,128)S(1)}, u32[]{:S(2)}, u32[]{:S(2)}) collective-permute-start(f32[4,7,8,128]{3,2,1,0:T(8,128)S(1)} %bitcast_reduce_fusion), channel_id=1, source_target_pairs={{0,64},{64,0},{1,65},{65,1},{2,66},{66,2},{3,67},{67,3},{4,68},{68... | collective-permute-start | bytes 344072 | tf_op jit(solution)/shard_map/ppermute | solution.py:534
  126.3 9.1 %collective-permute-start.8 = (f32[2,4,7,8,128]{4,3,2,1,0:T(8,128)S(1)}, f32[2,4,7,8,128]{4,3,2,1,0:T(8,128)S(1)}, u32[]{:S(2)}, u32[]{:S(2)}) collective-permute-start(f32[2,4,7,8,128]{4,3,2,1,0:T(8,128)S(1)} %pad_maximum_fusion), channel_id=1, source_target_pairs={{0,16},{16,32},{32,48},{48,0},{1,17},{17,33},{33,49},{49,1},{2,18}... | collective-permute-start | bytes 688136 | tf_op jit(solution)/shard_map/ppermute | solution.py:523
  128.2 10.6 %collective-permute-start.10 = (f32[2,4,7,8,128]{4,3,2,1,0:T(8,128)S(1)}, f32[2,4,7,8,128]{4,3,2,1,0:T(8,128)S(1)}, u32[]{:S(2)}, u32[]{:S(2)}) collective-permute-start(f32[2,4,7,8,128]{4,3,2,1,0:T(8,128)S(1)} %pad_maximum_fusion), channel_id=1, source_target_pairs={{0,48},{16,0},{32,16},{48,32},{1,49},{17,1},{33,17},{49,33},{2,50}... | collective-permute-start | bytes 688136 | tf_op jit(solution)/shard_map/ppermute | solution.py:524
  135.4 6.7 %collective-permute-start.9 = (f32[1,4,7,8,128]{4,3,2,1,0:T(8,128)S(1)}, f32[1,4,7,8,128]{4,3,2,1,0:T(8,128)S(1)}, u32[]{:S(2)}, u32[]{:S(2)}) collective-permute-start(f32[1,4,7,8,128]{4,3,2,1,0:T(8,128)S(1)} %slice.24), channel_id=1, source_target_pairs={{0,16},{16,32},{32,48},{48,0},{1,17},{17,33},{33,49},{49,1},{2,18}... | collective-permute-start | bytes 344072 | tf_op jit(solution)/shard_map/ppermute | solution.py:527
  138.8 7.9 %collective-permute-start.11 = (f32[1,4,7,8,128]{4,3,2,1,0:T(8,128)S(1)}, f32[1,4,7,8,128]{4,3,2,1,0:T(8,128)S(1)}, u32[]{:S(2)}, u32[]{:S(2)}) collective-permute-start(f32[1,4,7,8,128]{4,3,2,1,0:T(8,128)S(1)} %slice.25), channel_id=1, source_target_pairs={{0,48},{16,0},{32,16},{48,32},{1,49},{17,1},{33,17},{49,33},{2,50}... | collective-permute-start | bytes 344072 | tf_op jit(solution)/shard_map/ppermute | solution.py:528
  146.8 4.4 %collective-permute-start.12 = (f32[4,2,4,7,8,128]{5,4,3,2,1,0:T(8,128)S(1)}, f32[4,2,4,7,8,128]{5,4,3,2,1,0:T(8,128)S(1)}, u32[]{:S(2)}, u32[]{:S(2)}) collective-permute-start(f32[4,2,4,7,8,128]{5,4,3,2,1,0:T(8,128)S(1)} %bitcast.19), channel_id=1, source_target_pairs={{0,8},{8,0},{1,9},{9,1},{2,10},{10,2},{3,11},{11,3},{4,12},{12,4},... | collective-permute-start | bytes 2752520 | tf_op jit(solution)/shard_map/ppermute | solution.py:537
  183.8 33.3 %all-to-all-start.1 = ((f32[32,7,8,128]{3,2,1,0:T(8,128)}), f32[32,7,8,128]{3,2,1,0:T(8,128)S(1)}, u32[]{:S(2)}, u32[]{:S(2)}) async-start(f32[32,7,8,128]{3,2,1,0:T(8,128)} %shard_map.98), calls=%async_computation.1 | async-start | bytes 1835008 | tf_op jit(solution)/shard_map/all_to_all | solution.py:571
  (4 other events, 104.8 us)

commit v6 on v2

--- a/solution.py
+++ b/solution.py
@@ -10,9 +10,9 @@
 FLOW = ("z", "xh")
 CROSS = ("xl", "core")
 PLANE = ("z", "xh", "xl", "core")
-SPREAD = ("z", "xl", "core")
-ROWS = ("xh", "y")
-SPLIT = (4, 4, 2, 2, 8)
+RING_X = ("xh", "xl")
+ROWS = ("xh", "xl", "y")
+SPLIT = (8, 2, 2, 2, 8)
 
 EY = 16
 NZ = 32
@@ -278,11 +278,17 @@
 
 
 def metric_kernel(m_ref, q_ref):
+    x = 2 * lax.axis_index("xh") + lax.axis_index("xl")
+
     def chunk(k, carry):
+        from_xl, from_core, half = k // 4, k // 2 % 2, k % 2
         here = pl.ds(pl.multiple_of(k * 8, 8), 8)
-        source = [((k % 2) * 8 + s) * 4 + k // 2 for s in range(8)]
+        back = [(x - 2 * s - from_xl + 4) % 4 for s in range(2)]
         for tile in range(19):
-            block = jnp.stack([m_ref[at, 8 * tile : 8 * tile + 8, :] for at in source])
+            rows = slice(8 * tile, 8 * tile + 8)
+            block = jnp.stack(
+                [m_ref[(half * 4 + s // 2) * 2 + from_core, back[s % 2], rows, :] for s in range(8)]
+            )
             block = jnp.swapaxes(block, 0, 1)
             for j in range(8):
                 c, n = divmod(8 * tile + j, 49)
@@ -308,13 +314,11 @@
 def solve_kernel(
     count_ref, same_ref, other_ref, q_ref, out_ref, r_ref, d_ref, im_ref, mk_ref, x_ref, t_ref
 ):
-    z, xh, y = lax.axis_index("z"), lax.axis_index("xh"), lax.axis_index("y")
-    xl, core = lax.axis_index("xl"), lax.axis_index("core")
-    e = xl * 2 + core
-    row_id = 4 * y + xh
+    z, core = lax.axis_index("z"), lax.axis_index("core")
+    row_id = 4 * lax.axis_index("y") + 2 * lax.axis_index("xh") + lax.axis_index("xl")
     harmonic = jnp.where(row_id == 1, NZ // 2, row_id // 2).astype(jnp.float32)
     wavesq = harmonic * harmonic * (SPAN_UNIT * SPAN_UNIT)
-    own = pl.ds(pl.multiple_of((e * 2 + z // 2) * 8, 8), 8)
+    own = [pl.ds(pl.multiple_of(((2 * to + core) * 2 + z // 4) * 8, 8), 8) for to in range(2)]
     flipped = DERIV.T
     zero = jnp.zeros((8, 128), jnp.float32)
 
@@ -325,10 +329,10 @@
         from_xl, half = quarter // 2, quarter % 2
         for ref, from_core in ((same_ref, core), (other_ref, 1 - core)):
             at = here((from_xl * 2 + from_core) * 2 + half)
-            flip = (xl + from_xl) % 2
-            back = [(z - half * 2 - s + 4) % 4 for s in range(2)]
             for i in range(7):
-                block = jnp.stack([ref[flip, back[s // 4], s % 4, i] for s in range(8)])
+                block = jnp.stack(
+                    [ref[half * 4 + s // 2, 2 * (s % 2) + from_xl, i] for s in range(8)]
+                )
                 block = jnp.swapaxes(block, 0, 1)
                 for j in range(7):
                     n = i * 7 + j
@@ -340,7 +344,8 @@
 
     lax.fori_loop(0, 4, chunk_in, 0)
     for n in range(49):
-        x_ref[n] = zero
+        x_ref[0, n] = zero
+        x_ref[1, n] = zero
 
     lane = lax.broadcasted_iota(jnp.int32, (64, 128), 1)
     spot = lax.broadcasted_iota(jnp.int32, (64, 128), 0)
@@ -424,7 +429,8 @@
         step = rho / total(lax.fori_loop(0, 8, image, zero))
         join()
         for n in range(49):
-            x_ref[n] = x_ref[n] + step * d_ref[n, own, :]
+            for to in range(2):
+                x_ref[to, n] = x_ref[to, n] + step * d_ref[n, own[to], :]
 
         def descend(k, acc):
             at = here(k)
@@ -444,14 +450,14 @@
     lax.fori_loop(0, count_ref[row_id], sweep, (rho, zero))
 
     for i in range(7):
-        block = jnp.stack([x_ref[i * 7 + j] for j in range(7)] + [zero])
-        block = jnp.swapaxes(block, 0, 1)
-        for s in range(8):
-            t_ref[s, i] = block[s]
-    first = (z % 2) * 4
+        for to in range(2):
+            block = jnp.stack([x_ref[to, i * 7 + j] for j in range(7)] + [zero])
+            block = jnp.swapaxes(block, 0, 1)
+            for s in range(8):
+                t_ref[to, s, i] = block[s]
     for to in range(4):
         for i in range(7):
-            value = t_ref[first + to, i]
+            value = t_ref[to % 2, z % 4 * 2 + to // 2, i]
             for copy in range(8):
                 out_ref[to * 8 + copy, i] = value
 
@@ -466,8 +472,8 @@
         out_specs=vmem,
         scratch_shapes=[
             field, field, field, field,
-            pltpu.VMEM((49, 8, 128), jnp.float32),
-            pltpu.VMEM((8, 7, 8, 128), jnp.float32),
+            pltpu.VMEM((2, 49, 8, 128), jnp.float32),
+            pltpu.VMEM((2, 8, 7, 8, 128), jnp.float32),
         ],
         compiler_params=pltpu.CompilerParams(vmem_limit_bytes=40 * MIB),
     )(counts, same, other, metrics)
@@ -493,20 +499,17 @@
     )(jnp.asarray(plane_coefs()), rows)
 
 
-def gather_row(mine):
-    swap = [(0, 1), (1, 0)]
-    turns = [[(z, (z + back) % 4) for z in range(4)] for back in range(1, 4)]
-    beside = lax.ppermute(mine, "xl", swap)
-    pieces = [mine] + [lax.ppermute(mine, "z", turn) for turn in turns]
-    pieces += [beside] + [lax.ppermute(beside, "z", turn) for turn in turns]
-    same = jnp.stack(pieces).reshape(2, 4, 4, 7, 8, 128)
-    return same, lax.ppermute(same, "core", swap)
+SWAP = [(0, 1), (1, 0)]
+TURNS = [[(at, (at + back) % 4) for at in range(4)] for back in range(1, 4)]
+
+
+def after(value, other):
+    return lax.optimization_barrier((value, other))[0]
 
 
 def local(stress, velocity_grad, velocity, metric, iteration_counts):
     packed = jnp.pad(metric.reshape(147, 128), ((0, 5), (0, 0)))
-    gathered = lax.all_gather(packed, PLANE)
-    metrics = metric_fields(gathered)
+    turned = [lax.ppermute(packed, RING_X, turn) for turn in TURNS]
     right, left, up, down = pack_faces(stress)
     ahead = [(c, c + 1) for c in range(15)]
     above = [(e, e + 1) for e in range(3)]
@@ -516,10 +519,14 @@
         lax.ppermute(up, CROSS, above),
         lax.ppermute(down, CROSS, [(b, a) for a, b in above]),
     )
+    ring = jnp.stack([after(packed, right)] + turned)
+    faces = after(faces, ring)
+    metrics = metric_fields(lax.all_gather(ring, ("z", "core")))
     new_stress, parts = stress_step(stress, velocity_grad, velocity, faces)
     parts = lax.all_to_all(parts, ROWS, 0, 0, tiled=True)
     mine = jnp.sum(parts.reshape(4, 8, 7, 8, 128), axis=1)
-    same, other = gather_row(mine)
+    same = lax.all_gather(mine, "z")
+    other = lax.ppermute(same, "core", SWAP)
     answer = solve(iteration_counts, same, other, metrics)
     answer = lax.all_to_all(answer, ROWS, 0, 0, tiled=True)
     return new_stress, pressure_planes(answer)

time: 192 us -> 187 us (0.974)
  blocking collectives: 39.5 us -> 69.3 us
  starting transfers between devices: 55.2 us -> 33.1 us
  waiting for transfers between devices: 36.3 us -> 28.6 us
  Pallas kernels: 35.1 us -> 31.6 us
  local copies, waits for them, and re-layouts: 10.6 us -> 8.42 us
    all_gather x0 -> x1, blocking collectives: none -> 32.9 us  [local(): same = lax.all_gather(mine, 'z')]
    ppermute x8 -> x4, starting transfers between devices: 36.6 us -> 12.2 us  [the longest x3 10.2 us: local(): turned = [lax.ppermute(packed, RING_X, turn) for turn in TURNS]]
    ppermute x8 -> x4, waiting for transfers between devices: 9.53 us -> 2.84 us  [the longest x3 2.83 us: local(): turned = [lax.ppermute(packed, RING_X, turn) for turn in TURNS]]
    pallas_call x1, Pallas kernels: 28.9 us -> 25.3 us  [solve(): pl.pallas_call(solve_kernel, out_shape=jax.ShapeDtypeStruct((NZ, 7, 8, 12...]
    all_to_all x1, blocking collectives: 39.5 us -> 36.3 us  [local(): parts = lax.all_to_all(parts, ROWS, 0, 0, tiled=True)]
    unnamed x22 -> x15, local copies, waits for them, and re-layouts: 9.03 us -> 7.51 us
  transfers between devices with their start and end apart: 14 -> 10, of which waited for: 3 -> 3; matrix products, arithmetic and copies ran while one was open for 2% -> 2% of each run, Pallas kernels for 3% -> 3%
where the time goes in v6:
time: 187 us; the launch traced here: 186 us
  blocking collectives  69.3 us (37%)
  starting transfers between devices  33.1 us (18%)
  Pallas kernels  31.6 us (17%)
  waiting for transfers between devices  28.6 us (15%)
  between operations  14.3 us (8%)
  local copies, waits for them, and re-layouts  8.42 us (5%)
    all_to_all x1, blocking collectives, local(): parts = lax.all_to_all(parts, ROWS, 0, 0, tiled=True)  36.3 us
    all_gather x1, blocking collectives, local(): same = lax.all_gather(mine, 'z')  32.9 us
    all_to_all x1, waiting for transfers between devices, local(): answer = lax.all_to_all(answer, ROWS, 0, 0, tiled=True)  25.7 us
    pallas_call x1, Pallas kernels, solve(): pl.pallas_call(solve_kernel, out_shape=jax.ShapeDtypeStruct((NZ, 7, 8, 12...  25.3 us
    all_to_all x1, starting transfers between devices, local(): answer = lax.all_to_all(answer, ROWS, 0, 0, tiled=True)  10.9 us
    ppermute x3, starting transfers between devices, local(): turned = [lax.ppermute(packed, RING_X, turn) for turn in TURNS]  10.2 us
    unnamed x15, local copies, waits for them, and re-layouts  7.51 us
    ppermute x1, starting transfers between devices, local(): lax.ppermute(right, FLOW, ahead)  6.05 us
  transfers between devices with their start and end apart: 10, of which 3 were waited for; matrix products, arithmetic and copies ran while one was open for 2% of the time, Pallas kernels for 3%

profile of v6, /device:TPU:8, one launch (start us, length us, event | category | flops | bytes accessed | tf_op | source)
XLA Modules:
  0.0 186.0 jit_solution(6949201475896516571)
XLA Ops:
  7.2 0.9 reshape.10
  8.1 4.7 %collective-permute-start.6 = (f32[152,128]{1,0:T(8,128)S(1)}, f32[152,128]{1,0:T(8,128)S(1)}, u32[]{:S(2)}, u32[]{:S(2)}) collective-permute-start(f32[152,128]{1,0:T(8,128)S(1)} %pad.4), channel_id=1, source_target_pairs={{0,48},{16,0},{32,16},{48,32},{1,49},{17,1},{33,17},{49,33},{2,50}... | collective-permute-start | bytes 233480 | tf_op jit(solution)/shard_map/ppermute | solution.py:512
  12.8 2.7 %collective-permute-start.5 = (f32[152,128]{1,0:T(8,128)S(1)}, f32[152,128]{1,0:T(8,128)S(1)}, u32[]{:S(2)}, u32[]{:S(2)}) collective-permute-start(f32[152,128]{1,0:T(8,128)S(1)} %pad.4), channel_id=1, source_target_pairs={{0,32},{16,48},{32,0},{48,16},{1,33},{17,49},{33,1},{49,17},{2,34}... | collective-permute-start | bytes 233480 | tf_op jit(solution)/shard_map/ppermute | solution.py:512
  15.5 2.8 %collective-permute-start.4 = (f32[152,128]{1,0:T(8,128)S(1)}, f32[152,128]{1,0:T(8,128)S(1)}, u32[]{:S(2)}, u32[]{:S(2)}) collective-permute-start(f32[152,128]{1,0:T(8,128)S(1)} %pad.4), channel_id=1, source_target_pairs={{0,16},{16,32},{32,48},{48,0},{1,17},{17,33},{33,49},{49,1},{2,18}... | collective-permute-start | bytes 233480 | tf_op jit(solution)/shard_map/ppermute | solution.py:512
  18.3 1.2 copy.17.s_ref
  20.2 0.8 collective-permute-done.5
  21.0 2.0 %collective-permute-done.4 = f32[152,128]{1,0:T(8,128)S(1)} collective-permute-done((f32[152,128]{1,0:T(8,128)S(1)}, f32[152,128]{1,0:T(8,128)S(1)}, u32[]{:S(2)}, u32[]{:S(2)}) %collective-permute-start.4) | collective-permute-done | bytes 77856 | tf_op jit(solution)/shard_map/ppermute | solution.py:512
  23.8 1.3 collective-permute-start.1
  25.1 1.3 collective-permute-start.2
  26.4 1.3 collective-permute-start.3
  27.7 6.1 %collective-permute-start = (f32[4,8,128]{2,1,0:T(8,128)S(1)}, f32[4,8,128]{2,1,0:T(8,128)S(1)}, u32[]{:S(2)}, u32[]{:S(2)}) collective-permute-start(f32[4,8,128]{2,1,0:T(8,128)S(1)} %get-tuple-element.13), channel_id=1, source_target_pairs={{0,32},{32,64},{64,96},{96,128},{128,160},{160,192},{192,224},{224... | collective-permute-start | bytes 49160 | tf_op jit(solution)/shard_map/ppermute | solution.py:517
  33.8 1.0 copy.19.v_ref
  34.7 1.3 copy.18.g_ref
  36.1 3.6 %shard_map.96 = (f32[6,4,7,7,128]{4,3,2,1,0:T(8,128)S(1)}, f32[32,7,8,128]{3,2,1,0:T(8,128)S(1)}) custom-call(f32[3072]{0:T(1024)S(1)} %copy-done.2, f32[6,4,7,7,128]{4,3,2,1,0:T(8,128)S(1)} %copy.17.s_ref, f32[9,4,7,7,128]{4,3,2,1,0:T(8,128)S(1)} %copy.18.g_ref, f32[2,4,7,7,128]{4,3,2,1,0:T(8,128)S(1)} %copy.19.v_ref, ...), custom_call_target="tpu_custom_call" | custom-call | tf_op jit(solution)/shard_map/pallas_call | solution.py:257
  39.7 36.3 %all_to_all.10 = f32[32,7,8,128]{3,2,1,0:T(8,128)S(1)} all-to-all(f32[32,7,8,128]{3,2,1,0:T(8,128)S(1)} %get-tuple-element.23), channel_id=1, replica_groups=mesh['z'=8,'xh'=2,'xl'=2,'core'=2,'y'=8] {'xh','xl','y'}, dimensions={0} | all-to-all | bytes 1835008 | tf_op jit(solution)/shard_map/all_to_all | solution.py:526
  76.1 32.9 %all-gather = f32[32,7,8,128]{3,2,1,0:T(8,128)S(1)} all-gather(f32[4,7,8,128]{3,2,1,0:T(8,128)S(1)} %bitcast_reduce_fusion), channel_id=2, replica_groups=mesh['z'=8,'xh'=2,'xl'=2,'core'=2,'y'=8] {'z'}, dimensions={0}, use_global_device_ids=true | all-gather | bytes 1032192 | tf_op jit(solution)/shard_map/all_gather | solution.py:528
  109.0 2.0 %collective-permute-start.7 = (f32[8,4,7,8,128]{4,3,2,1,0:T(8,128)S(1)}, f32[8,4,7,8,128]{4,3,2,1,0:T(8,128)S(1)}, u32[]{:S(2)}, u32[]{:S(2)}) collective-permute-start(f32[8,4,7,8,128]{4,3,2,1,0:T(8,128)S(1)} %bitcast.9), channel_id=1, source_target_pairs={{0,8},{8,0},{1,9},{9,1},{2,10},{10,2},{3,11},{11,3},{4,12},{12,4},... | collective-permute-start | bytes 2752520 | tf_op jit(solution)/shard_map/ppermute | solution.py:529
  111.1 2.4 %copy-done = f32[64,152,128]{2,1,0:T(8,128)S(1)} copy-done((f32[64,152,128]{2,1,0:T(8,128)S(1)}, f32[64,152,128]{2,1,0:T(8,128)}, u32[]{:S(2)}) %copy-start) | copy-done | bytes 4980760
  113.5 1.2 shard_map.97.q_ref
  114.7 25.3 %shard_map.98 = f32[32,7,8,128]{3,2,1,0:T(8,128)} custom-call(s32[32]{0:T(128)S(1)} %copy-done.4, f32[8,4,7,8,128]{4,3,2,1,0:T(8,128)S(1)} %bitcast.10, f32[8,4,7,8,128]{4,3,2,1,0:T(8,128)S(1)} %collective-permute-done.7.other_ref, f32[3,49,64,128]{3,2,1,0:T(8,128)S(1)} %shard_map.97.q_ref), custom_call_target="tpu_custom_call" | custom-call | tf_op jit(solution)/shard_map/pallas_call | solution.py:468
  140.0 10.9 %all-to-all-start.1 = ((f32[32,7,8,128]{3,2,1,0:T(8,128)}), f32[32,7,8,128]{3,2,1,0:T(8,128)S(1)}, u32[]{:S(2)}, u32[]{:S(2)}) async-start(f32[32,7,8,128]{3,2,1,0:T(8,128)} %shard_map.98), calls=%async_computation.1 | async-start | bytes 1835008 | tf_op jit(solution)/shard_map/all_to_all | solution.py:531
  151.0 1.0 copy.20
  151.9 25.7 %all-to-all-done.1.rows_ref = f32[32,7,8,128]{3,2,1,0:T(8,128)S(1)} async-done(((f32[32,7,8,128]{3,2,1,0:T(8,128)}), f32[32,7,8,128]{3,2,1,0:T(8,128)S(1)}, u32[]{:S(2)}, u32[]{:S(2)}) %all-to-all-start.1) | async-done | bytes 917536 | tf_op jit(solution)/shard_map/all_to_all | solution.py:531
  177.6 0.9 shard_map.99
  (23 shorter events, 2.3 us)
Async XLA Ops:
  7.2 28.9 %copy-start.1 = (f32[7,8,128]{2,1,0:T(8,128)S(1)}, f32[7,8,128]{2,1,0:T(8,128)}, u32[]{:S(2)}) copy-start(f32[7,8,128]{2,1,0:T(8,128)} %constant.11.clone.dcol_ref) | copy-start | bytes 86020
  7.2 28.9 %copy-start.2 = (f32[3072]{0:T(1024)S(1)}, f32[3072]{0:T(1024)}, u32[]{:S(2)}) copy-start(f32[3072]{0:T(1024)} %constant.10.clone.coef_ref) | copy-start | bytes 36868
  7.2 103.9 %all-gather.4.cloned.1.call-start = ((), (), s32[]{:S(2)}) async-start(), calls=%async_computation.2 | async-start | bytes 5292032 | tf_op jit(solution)/shard_map/all_gather | solution.py:524
  8.1 12.1 %collective-permute-start.6 = (f32[152,128]{1,0:T(8,128)S(1)}, f32[152,128]{1,0:T(8,128)S(1)}, u32[]{:S(2)}, u32[]{:S(2)}) collective-permute-start(f32[152,128]{1,0:T(8,128)S(1)} %pad.4), channel_id=1, source_target_pairs={{0,48},{16,0},{32,16},{48,32},{1,49},{17,1},{33,17},{49,33},{2,50}... | collective-permute-start | bytes 233480 | tf_op jit(solution)/shard_map/ppermute | solution.py:512
  12.8 8.2 %collective-permute-start.5 = (f32[152,128]{1,0:T(8,128)S(1)}, f32[152,128]{1,0:T(8,128)S(1)}, u32[]{:S(2)}, u32[]{:S(2)}) collective-permute-start(f32[152,128]{1,0:T(8,128)S(1)} %pad.4), channel_id=1, source_target_pairs={{0,32},{16,48},{32,0},{48,16},{1,33},{17,49},{33,1},{49,17},{2,34}... | collective-permute-start | bytes 233480 | tf_op jit(solution)/shard_map/ppermute | solution.py:512
  15.5 7.5 %collective-permute-start.4 = (f32[152,128]{1,0:T(8,128)S(1)}, f32[152,128]{1,0:T(8,128)S(1)}, u32[]{:S(2)}, u32[]{:S(2)}) collective-permute-start(f32[152,128]{1,0:T(8,128)S(1)} %pad.4), channel_id=1, source_target_pairs={{0,16},{16,32},{32,48},{48,0},{1,17},{17,33},{33,49},{49,1},{2,18}... | collective-permute-start | bytes 233480 | tf_op jit(solution)/shard_map/ppermute | solution.py:512
  23.8 12.3 %collective-permute-start.1 = (f32[4,8,128]{2,1,0:T(8,128)S(1)}, f32[4,8,128]{2,1,0:T(8,128)S(1)}, u32[]{:S(2)}, u32[]{:S(2)}) collective-permute-start(f32[4,8,128]{2,1,0:T(8,128)S(1)} %get-tuple-element.14), channel_id=1, source_target_pairs={{32,0},{64,32},{96,64},{128,96},{160,128},{192,160},{224,192},{256... | collective-permute-start | bytes 49160 | tf_op jit(solution)/shard_map/ppermute | solution.py:518
  25.1 11.0 %collective-permute-start.2 = (f32[4,8,128]{2,1,0:T(8,128)S(1)}, f32[4,8,128]{2,1,0:T(8,128)S(1)}, u32[]{:S(2)}, u32[]{:S(2)}) collective-permute-start(f32[4,8,128]{2,1,0:T(8,128)S(1)} %get-tuple-element.15), channel_id=1, source_target_pairs={{0,8},{8,16},{16,24},{1,9},{9,17},{17,25},{2,10},{10,18},{18,26},{... | collective-permute-start | bytes 49160 | tf_op jit(solution)/shard_map/ppermute | solution.py:519
  26.4 9.7 %collective-permute-start.3 = (f32[4,8,128]{2,1,0:T(8,128)S(1)}, f32[4,8,128]{2,1,0:T(8,128)S(1)}, u32[]{:S(2)}, u32[]{:S(2)}) collective-permute-start(f32[4,8,128]{2,1,0:T(8,128)S(1)} %get-tuple-element.16), channel_id=1, source_target_pairs={{8,0},{16,8},{24,16},{9,1},{17,9},{25,17},{10,2},{18,10},{26,18},{... | collective-permute-start | bytes 49160 | tf_op jit(solution)/shard_map/ppermute | solution.py:520
  27.7 8.4 %collective-permute-start = (f32[4,8,128]{2,1,0:T(8,128)S(1)}, f32[4,8,128]{2,1,0:T(8,128)S(1)}, u32[]{:S(2)}, u32[]{:S(2)}) collective-permute-start(f32[4,8,128]{2,1,0:T(8,128)S(1)} %get-tuple-element.13), channel_id=1, source_target_pairs={{0,32},{32,64},{64,96},{96,128},{128,160},{160,192},{192,224},{224... | collective-permute-start | bytes 49160 | tf_op jit(solution)/shard_map/ppermute | solution.py:517
  109.0 5.7 %copy-start.4 = (s32[32]{0:T(128)S(1)}, s32[32]{0:T(128)}, u32[]{:S(2)}) copy-start(s32[32]{0:T(128)} %count_ref.1) | copy-start | bytes 388
  109.0 5.7 %collective-permute-start.7 = (f32[8,4,7,8,128]{4,3,2,1,0:T(8,128)S(1)}, f32[8,4,7,8,128]{4,3,2,1,0:T(8,128)S(1)}, u32[]{:S(2)}, u32[]{:S(2)}) collective-permute-start(f32[8,4,7,8,128]{4,3,2,1,0:T(8,128)S(1)} %bitcast.9), channel_id=1, source_target_pairs={{0,8},{8,0},{1,9},{9,1},{2,10},{10,2},{3,11},{11,3},{4,12},{12,4},... | collective-permute-start | bytes 2752520 | tf_op jit(solution)/shard_map/ppermute | solution.py:529
  111.1 2.4 %copy-start = (f32[64,152,128]{2,1,0:T(8,128)S(1)}, f32[64,152,128]{2,1,0:T(8,128)}, u32[]{:S(2)}) copy-start(f32[64,152,128]{2,1,0:T(8,128)} %all-gather.4.cloned.1.call-done) | copy-start | bytes 14942212
  114.7 63.0 %copy-start.3 = (f32[1024]{0:T(1024)S(1)}, f32[1024]{0:T(1024)}, u32[]{:S(2)}) copy-start(f32[1024]{0:T(1024)} %constant.12.clone.coef_ref) | copy-start | bytes 12292
  140.0 37.6 %all-to-all-start.1 = ((f32[32,7,8,128]{3,2,1,0:T(8,128)}), f32[32,7,8,128]{3,2,1,0:T(8,128)S(1)}, u32[]{:S(2)}, u32[]{:S(2)}) async-start(f32[32,7,8,128]{3,2,1,0:T(8,128)} %shard_map.98), calls=%async_computation.1 | async-start | bytes 1835008 | tf_op jit(solution)/shard_map/all_to_all | solution.py:531
Sparse Core Ops, SparseCore 0:
  23.9 49.0 all-gather.3

commit v7 on v6

--- a/solution.py
+++ b/solution.py
@@ -7,12 +7,12 @@
 from jax.sharding import Mesh
 from jax.sharding import PartitionSpec as P
 
-FLOW = ("z", "xh")
+FLOW = ("zh", "zl", "xh")
 CROSS = ("xl", "core")
-PLANE = ("z", "xh", "xl", "core")
+PLANE = ("zh", "zl", "xh", "xl", "core")
 RING_X = ("xh", "xl")
 ROWS = ("xh", "xl", "y")
-SPLIT = (8, 2, 2, 2, 8)
+SPLIT = (4, 2, 2, 2, 2, 8)
 
 EY = 16
 NZ = 32
@@ -314,7 +314,9 @@
 def solve_kernel(
     count_ref, same_ref, other_ref, q_ref, out_ref, r_ref, d_ref, im_ref, mk_ref, x_ref, t_ref
 ):
-    z, core = lax.axis_index("z"), lax.axis_index("core")
+    zl, core = lax.axis_index("zl"), lax.axis_index("core")
+    z = 2 * lax.axis_index("zh") + zl
+    flip = [zl, 1 - zl]
     row_id = 4 * lax.axis_index("y") + 2 * lax.axis_index("xh") + lax.axis_index("xl")
     harmonic = jnp.where(row_id == 1, NZ // 2, row_id // 2).astype(jnp.float32)
     wavesq = harmonic * harmonic * (SPAN_UNIT * SPAN_UNIT)
@@ -331,7 +333,10 @@
             at = here((from_xl * 2 + from_core) * 2 + half)
             for i in range(7):
                 block = jnp.stack(
-                    [ref[half * 4 + s // 2, 2 * (s % 2) + from_xl, i] for s in range(8)]
+                    [
+                        ref[half * 2 + s // 4, flip[s // 2 % 2], 2 * (s % 2) + from_xl, i]
+                        for s in range(8)
+                    ]
                 )
                 block = jnp.swapaxes(block, 0, 1)
                 for j in range(7):
@@ -509,7 +514,6 @@
 
 def local(stress, velocity_grad, velocity, metric, iteration_counts):
     packed = jnp.pad(metric.reshape(147, 128), ((0, 5), (0, 0)))
-    turned = [lax.ppermute(packed, RING_X, turn) for turn in TURNS]
     right, left, up, down = pack_faces(stress)
     ahead = [(c, c + 1) for c in range(15)]
     above = [(e, e + 1) for e in range(3)]
@@ -519,13 +523,15 @@
         lax.ppermute(up, CROSS, above),
         lax.ppermute(down, CROSS, [(b, a) for a, b in above]),
     )
-    ring = jnp.stack([after(packed, right)] + turned)
-    faces = after(faces, ring)
-    metrics = metric_fields(lax.all_gather(ring, ("z", "core")))
+    packed = after(packed, faces)
+    turned = [lax.ppermute(packed, RING_X, turn) for turn in TURNS]
     new_stress, parts = stress_step(stress, velocity_grad, velocity, faces)
-    parts = lax.all_to_all(parts, ROWS, 0, 0, tiled=True)
+    ring = jnp.stack([after(packed, parts)] + turned)
+    metrics = metric_fields(lax.all_gather(ring, ("zh", "zl", "core")))
+    parts = lax.all_to_all(after(parts, ring), ROWS, 0, 0, tiled=True)
     mine = jnp.sum(parts.reshape(4, 8, 7, 8, 128), axis=1)
-    same = lax.all_gather(mine, "z")
+    pair = jnp.stack([mine, lax.ppermute(mine, "zl", SWAP)])
+    same = lax.all_gather(pair, "zh")
     other = lax.ppermute(same, "core", SWAP)
     answer = solve(iteration_counts, same, other, metrics)
     answer = lax.all_to_all(answer, ROWS, 0, 0, tiled=True)

time: 187 us -> 190 us (1.016)
  blocking collectives: 69.3 us -> 59.6 us
  Pallas kernels: 31.6 us -> 39 us
  waiting for transfers between devices: 28.6 us -> 33.2 us
    all_gather x1, blocking collectives: 32.9 us -> 23.7 us  [local(): same = lax.all_gather(pair, 'zh')]
    pallas_call x1, Pallas kernels: 25.3 us -> 32.7 us  [solve(): pl.pallas_call(solve_kernel, out_shape=jax.ShapeDtypeStruct((NZ, 7, 8, 12...]
    all_to_all x1, starting transfers between devices: 10.9 us -> 3.96 us  [local(): answer = lax.all_to_all(answer, ROWS, 0, 0, tiled=True)]
    ppermute x0 -> x1, starting transfers between devices: none -> 5.49 us  [local(): pair = jnp.stack([mine, lax.ppermute(mine, 'zl', SWAP)])]
    ppermute x0 -> x1, waiting for transfers between devices: none -> 5.4 us  [local(): pair = jnp.stack([mine, lax.ppermute(mine, 'zl', SWAP)])]
    ppermute x3, waiting for transfers between devices: 2.83 us -> 0.01 us  [local(): turned = [lax.ppermute(packed, RING_X, turn) for turn in TURNS]]
    ppermute x1, waiting for transfers between devices: 0.01 us -> 2.15 us  [local(): lax.ppermute(left, FLOW, [(b, a) for a, b in ahead])]
  transfers between devices with their start and end apart: 10 -> 11, of which waited for: 3 -> 3; matrix products, arithmetic and copies ran while one was open for 2% -> 2% of each run, Pallas kernels for 3% -> 3%
where the time goes in v7:
time: 190 us; the launch traced here: 189 us
  blocking collectives  59.6 us (31%)
  Pallas kernels  39 us (21%)
  waiting for transfers between devices  33.2 us (17%)
  starting transfers between devices  32.1 us (17%)
  between operations  14.2 us (7%)
  local copies, waits for them, and re-layouts  9.86 us (5%)
    all_to_all x1, blocking collectives, local(): parts = lax.all_to_all(after(parts, ring), ROWS, 0, 0, tiled=True)  35.9 us
    pallas_call x1, Pallas kernels, solve(): pl.pallas_call(solve_kernel, out_shape=jax.ShapeDtypeStruct((NZ, 7, 8, 12...  32.7 us
    all_to_all x1, waiting for transfers between devices, local(): answer = lax.all_to_all(answer, ROWS, 0, 0, tiled=True)  25.6 us
    all_gather x1, blocking collectives, local(): same = lax.all_gather(pair, 'zh')  23.7 us
    ppermute x3, starting transfers between devices, local(): turned = [lax.ppermute(packed, RING_X, turn) for turn in TURNS]  11.6 us
    unnamed x15, local copies, waits for them, and re-layouts  8.95 us
    ppermute x1, starting transfers between devices, local(): pair = jnp.stack([mine, lax.ppermute(mine, 'zl', SWAP)])  5.49 us
    ppermute x1, waiting for transfers between devices, local(): pair = jnp.stack([mine, lax.ppermute(mine, 'zl', SWAP)])  5.4 us
  transfers between devices with their start and end apart: 11, of which 3 were waited for; matrix products, arithmetic and copies ran while one was open for 2% of the time, Pallas kernels for 3%

profile of v7, /device:TPU:8, one launch (start us, length us, event | category | flops | bytes accessed | tf_op | source)
XLA Modules:
  0.0 188.9 jit_solution(14221466099660966499)
XLA Ops:
  7.2 1.2 copy.17.s_ref
  9.1 4.9 %collective-permute-start = (f32[4,8,128]{2,1,0:T(8,128)S(1)}, f32[4,8,128]{2,1,0:T(8,128)S(1)}, u32[]{:S(2)}, u32[]{:S(2)}) collective-permute-start(f32[4,8,128]{2,1,0:T(8,128)S(1)} %get-tuple-element.11), channel_id=1, source_target_pairs={{0,32},{32,64},{64,96},{96,128},{128,160},{160,192},{192,224},{224... | collective-permute-start | bytes 49160 | tf_op jit(solution)/shard_map/ppermute | solution.py:521
  14.0 1.3 collective-permute-start.1
  15.3 1.5 collective-permute-start.2
  16.8 1.3 collective-permute-start.3
  18.1 0.9 reshape.10
  19.0 2.1 %collective-permute-done.1.right_ref = f32[4,8,128]{2,1,0:T(8,128)S(1)} collective-permute-done((f32[4,8,128]{2,1,0:T(8,128)S(1)}, f32[4,8,128]{2,1,0:T(8,128)S(1)}, u32[]{:S(2)}, u32[]{:S(2)}) %collective-permute-start.1) | collective-permute-done | bytes 16416 | tf_op jit(solution)/shard_map/ppermute | solution.py:522
  21.1 6.9 %collective-permute-start.6 = (f32[152,128]{1,0:T(8,128)S(1)}, f32[152,128]{1,0:T(8,128)S(1)}, u32[]{:S(2)}, u32[]{:S(2)}) collective-permute-start(f32[152,128]{1,0:T(8,128)S(1)} %pad.4), channel_id=1, source_target_pairs={{0,48},{16,0},{32,16},{48,32},{1,49},{17,1},{33,17},{49,33},{2,50}... | collective-permute-start | bytes 233480 | tf_op jit(solution)/shard_map/ppermute | solution.py:527
  28.1 1.9 %collective-permute-start.5 = (f32[152,128]{1,0:T(8,128)S(1)}, f32[152,128]{1,0:T(8,128)S(1)}, u32[]{:S(2)}, u32[]{:S(2)}) collective-permute-start(f32[152,128]{1,0:T(8,128)S(1)} %pad.4), channel_id=1, source_target_pairs={{0,32},{16,48},{32,0},{48,16},{1,33},{17,49},{33,1},{49,17},{2,34}... | collective-permute-start | bytes 233480 | tf_op jit(solution)/shard_map/ppermute | solution.py:527
  30.0 2.8 %collective-permute-start.4 = (f32[152,128]{1,0:T(8,128)S(1)}, f32[152,128]{1,0:T(8,128)S(1)}, u32[]{:S(2)}, u32[]{:S(2)}) collective-permute-start(f32[152,128]{1,0:T(8,128)S(1)} %pad.4), channel_id=1, source_target_pairs={{0,16},{16,32},{32,48},{48,0},{1,17},{17,33},{33,49},{49,1},{2,18}... | collective-permute-start | bytes 233480 | tf_op jit(solution)/shard_map/ppermute | solution.py:527
  32.8 1.0 copy.19.v_ref
  33.8 1.3 copy.18.g_ref
  36.5 3.6 %shard_map.96 = (f32[6,4,7,7,128]{4,3,2,1,0:T(8,128)S(1)}, f32[32,7,8,128]{3,2,1,0:T(8,128)S(1)}) custom-call(f32[3072]{0:T(1024)S(1)} %copy-done.2, f32[6,4,7,7,128]{4,3,2,1,0:T(8,128)S(1)} %copy.17.s_ref, f32[9,4,7,7,128]{4,3,2,1,0:T(8,128)S(1)} %copy.18.g_ref, f32[2,4,7,7,128]{4,3,2,1,0:T(8,128)S(1)} %copy.19.v_ref, ...), custom_call_target="tpu_custom_call" | custom-call | tf_op jit(solution)/shard_map/pallas_call | solution.py:257
  40.9 35.9 %all_to_all.10 = f32[32,7,8,128]{3,2,1,0:T(8,128)S(1)} all-to-all(f32[32,7,8,128]{3,2,1,0:T(8,128)S(1)} %get-tuple-element.19), channel_id=1, replica_groups=mesh['zh'=4,'zl'=2,'xh'=2,'xl'=2,'core'=2,'y'=8] {'xh','xl','y'}, dimensions={0} | all-to-all | bytes 1835008 | tf_op jit(solution)/shard_map/all_to_all | solution.py:531
  76.9 5.5 %collective-permute-start.7 = (f32[4,7,8,128]{3,2,1,0:T(8,128)S(1)}, f32[4,7,8,128]{3,2,1,0:T(8,128)S(1)}, u32[]{:S(2)}, u32[]{:S(2)}) collective-permute-start(f32[4,7,8,128]{3,2,1,0:T(8,128)S(1)} %bitcast_reduce_fusion), channel_id=1, source_target_pairs={{0,64},{64,0},{1,65},{65,1},{2,66},{66,2},{3,67},{67,3},{4,68},{68... | collective-permute-start | bytes 344072 | tf_op jit(solution)/shard_map/ppermute | solution.py:533
  82.4 5.4 %collective-permute-done.7 = f32[4,7,8,128]{3,2,1,0:T(8,128)S(1)} collective-permute-done((f32[4,7,8,128]{3,2,1,0:T(8,128)S(1)}, f32[4,7,8,128]{3,2,1,0:T(8,128)S(1)}, u32[]{:S(2)}, u32[]{:S(2)}) %collective-permute-start.7) | collective-permute-done | bytes 114720 | tf_op jit(solution)/shard_map/ppermute | solution.py:533
  87.8 23.7 %all-gather = f32[8,4,7,8,128]{4,3,2,1,0:T(8,128)S(1)} all-gather(f32[2,4,7,8,128]{4,3,2,1,0:T(8,128)S(1)} %pad_maximum_fusion.1), channel_id=2, replica_groups=mesh['zh'=4,'zl'=2,'xh'=2,'xl'=2,'core'=2,'y'=8] {'zh'}, dimensions={0}, use_global_device_ids=true | all-gather | bytes 1146880 | tf_op jit(solution)/shard_map/all_gather | solution.py:534
  111.5 2.0 %collective-permute-start.8 = (f32[4,2,4,7,8,128]{5,4,3,2,1,0:T(8,128)S(1)}, f32[4,2,4,7,8,128]{5,4,3,2,1,0:T(8,128)S(1)}, u32[]{:S(2)}, u32[]{:S(2)}) collective-permute-start(f32[4,2,4,7,8,128]{5,4,3,2,1,0:T(8,128)S(1)} %bitcast.11), channel_id=1, source_target_pairs={{0,8},{8,0},{1,9},{9,1},{2,10},{10,2},{3,11},{11,3},{4,12},{12,4},... | collective-permute-start | bytes 2752520 | tf_op jit(solution)/shard_map/ppermute | solution.py:535
  113.6 2.4 %copy-done = f32[64,152,128]{2,1,0:T(8,128)S(1)} copy-done((f32[64,152,128]{2,1,0:T(8,128)S(1)}, f32[64,152,128]{2,1,0:T(8,128)}, u32[]{:S(2)}) %copy-start) | copy-done | bytes 4980760
  116.0 1.2 shard_map.97.q_ref
  117.2 32.7 %shard_map.98 = f32[32,7,8,128]{3,2,1,0:T(8,128)} custom-call(s32[32]{0:T(128)S(1)} %copy-done.4, f32[4,2,4,7,8,128]{5,4,3,2,1,0:T(8,128)S(1)} %bitcast.12, f32[4,2,4,7,8,128]{5,4,3,2,1,0:T(8,128)S(1)} %collective-permute-done.8.other_ref, f32[3,49,64,128]{3,2,1,0:T(8,128)S(1)} %shard_map.97.q_ref), custom_call_target="tpu_custom_call" | custom-call | tf_op jit(solution)/shard_map/pallas_call | solution.py:473
  149.9 4.0 %all-to-all-start.1 = ((f32[32,7,8,128]{3,2,1,0:T(8,128)}), f32[32,7,8,128]{3,2,1,0:T(8,128)S(1)}, u32[]{:S(2)}, u32[]{:S(2)}) async-start(f32[32,7,8,128]{3,2,1,0:T(8,128)} %shard_map.98), calls=%async_computation.1 | async-start | bytes 1835008 | tf_op jit(solution)/shard_map/all_to_all | solution.py:537
  153.9 1.0 copy.20
  154.9 25.6 %all-to-all-done.1.rows_ref = f32[32,7,8,128]{3,2,1,0:T(8,128)S(1)} async-done(((f32[32,7,8,128]{3,2,1,0:T(8,128)}), f32[32,7,8,128]{3,2,1,0:T(8,128)S(1)}, u32[]{:S(2)}, u32[]{:S(2)}) %all-to-all-start.1) | async-done | bytes 917536 | tf_op jit(solution)/shard_map/all_to_all | solution.py:537
  (26 shorter events, 4.6 us)
Async XLA Ops:
  7.2 106.4 %all-gather.4.cloned.1.call-start = ((), (), s32[]{:S(2)}) async-start(), calls=%async_computation.2 | async-start | bytes 5292032 | tf_op jit(solution)/shard_map/all_gather | solution.py:530
  9.1 9.9 %collective-permute-start = (f32[4,8,128]{2,1,0:T(8,128)S(1)}, f32[4,8,128]{2,1,0:T(8,128)S(1)}, u32[]{:S(2)}, u32[]{:S(2)}) collective-permute-start(f32[4,8,128]{2,1,0:T(8,128)S(1)} %get-tuple-element.11), channel_id=1, source_target_pairs={{0,32},{32,64},{64,96},{96,128},{128,160},{160,192},{192,224},{224... | collective-permute-start | bytes 49160 | tf_op jit(solution)/shard_map/ppermute | solution.py:521
  14.0 7.1 %collective-permute-start.1 = (f32[4,8,128]{2,1,0:T(8,128)S(1)}, f32[4,8,128]{2,1,0:T(8,128)S(1)}, u32[]{:S(2)}, u32[]{:S(2)}) collective-permute-start(f32[4,8,128]{2,1,0:T(8,128)S(1)} %get-tuple-element.12), channel_id=1, source_target_pairs={{32,0},{64,32},{96,64},{128,96},{160,128},{192,160},{224,192},{256... | collective-permute-start | bytes 49160 | tf_op jit(solution)/shard_map/ppermute | solution.py:522
  15.3 5.8 %collective-permute-start.2 = (f32[4,8,128]{2,1,0:T(8,128)S(1)}, f32[4,8,128]{2,1,0:T(8,128)S(1)}, u32[]{:S(2)}, u32[]{:S(2)}) collective-permute-start(f32[4,8,128]{2,1,0:T(8,128)S(1)} %get-tuple-element.13), channel_id=1, source_target_pairs={{0,8},{8,16},{16,24},{1,9},{9,17},{17,25},{2,10},{10,18},{18,26},{... | collective-permute-start | bytes 49160 | tf_op jit(solution)/shard_map/ppermute | solution.py:523
  16.8 4.4 %collective-permute-start.3 = (f32[4,8,128]{2,1,0:T(8,128)S(1)}, f32[4,8,128]{2,1,0:T(8,128)S(1)}, u32[]{:S(2)}, u32[]{:S(2)}) collective-permute-start(f32[4,8,128]{2,1,0:T(8,128)S(1)} %get-tuple-element.14), channel_id=1, source_target_pairs={{8,0},{16,8},{24,16},{9,1},{17,9},{25,17},{10,2},{18,10},{26,18},{... | collective-permute-start | bytes 49160 | tf_op jit(solution)/shard_map/ppermute | solution.py:524
  21.1 19.0 %collective-permute-start.6 = (f32[152,128]{1,0:T(8,128)S(1)}, f32[152,128]{1,0:T(8,128)S(1)}, u32[]{:S(2)}, u32[]{:S(2)}) collective-permute-start(f32[152,128]{1,0:T(8,128)S(1)} %pad.4), channel_id=1, source_target_pairs={{0,48},{16,0},{32,16},{48,32},{1,49},{17,1},{33,17},{49,33},{2,50}... | collective-permute-start | bytes 233480 | tf_op jit(solution)/shard_map/ppermute | solution.py:527
  28.1 12.0 %collective-permute-start.5 = (f32[152,128]{1,0:T(8,128)S(1)}, f32[152,128]{1,0:T(8,128)S(1)}, u32[]{:S(2)}, u32[]{:S(2)}) collective-permute-start(f32[152,128]{1,0:T(8,128)S(1)} %pad.4), channel_id=1, source_target_pairs={{0,32},{16,48},{32,0},{48,16},{1,33},{17,49},{33,1},{49,17},{2,34}... | collective-permute-start | bytes 233480 | tf_op jit(solution)/shard_map/ppermute | solution.py:527
  30.0 10.1 %collective-permute-start.4 = (f32[152,128]{1,0:T(8,128)S(1)}, f32[152,128]{1,0:T(8,128)S(1)}, u32[]{:S(2)}, u32[]{:S(2)}) collective-permute-start(f32[152,128]{1,0:T(8,128)S(1)} %pad.4), channel_id=1, source_target_pairs={{0,16},{16,32},{32,48},{48,0},{1,17},{17,33},{33,49},{49,1},{2,18}... | collective-permute-start | bytes 233480 | tf_op jit(solution)/shard_map/ppermute | solution.py:527
  35.1 0.8 copy-start.1
  35.8 0.7 copy-start.2
  76.9 10.9 %collective-permute-start.7 = (f32[4,7,8,128]{3,2,1,0:T(8,128)S(1)}, f32[4,7,8,128]{3,2,1,0:T(8,128)S(1)}, u32[]{:S(2)}, u32[]{:S(2)}) collective-permute-start(f32[4,7,8,128]{3,2,1,0:T(8,128)S(1)} %bitcast_reduce_fusion), channel_id=1, source_target_pairs={{0,64},{64,0},{1,65},{65,1},{2,66},{66,2},{3,67},{67,3},{4,68},{68... | collective-permute-start | bytes 344072 | tf_op jit(solution)/shard_map/ppermute | solution.py:533
  111.5 5.7 %copy-start.4 = (s32[32]{0:T(128)S(1)}, s32[32]{0:T(128)}, u32[]{:S(2)}) copy-start(s32[32]{0:T(128)} %count_ref.1) | copy-start | bytes 388
  111.5 5.7 %collective-permute-start.8 = (f32[4,2,4,7,8,128]{5,4,3,2,1,0:T(8,128)S(1)}, f32[4,2,4,7,8,128]{5,4,3,2,1,0:T(8,128)S(1)}, u32[]{:S(2)}, u32[]{:S(2)}) collective-permute-start(f32[4,2,4,7,8,128]{5,4,3,2,1,0:T(8,128)S(1)} %bitcast.11), channel_id=1, source_target_pairs={{0,8},{8,0},{1,9},{9,1},{2,10},{10,2},{3,11},{11,3},{4,12},{12,4},... | collective-permute-start | bytes 2752520 | tf_op jit(solution)/shard_map/ppermute | solution.py:535
  113.6 2.4 %copy-start = (f32[64,152,128]{2,1,0:T(8,128)S(1)}, f32[64,152,128]{2,1,0:T(8,128)}, u32[]{:S(2)}) copy-start(f32[64,152,128]{2,1,0:T(8,128)} %all-gather.4.cloned.1.call-done) | copy-start | bytes 14942212
  117.2 63.3 %copy-start.3 = (f32[1024]{0:T(1024)S(1)}, f32[1024]{0:T(1024)}, u32[]{:S(2)}) copy-start(f32[1024]{0:T(1024)} %constant.12.clone.coef_ref) | copy-start | bytes 12292
  149.9 30.6 %all-to-all-start.1 = ((f32[32,7,8,128]{3,2,1,0:T(8,128)}), f32[32,7,8,128]{3,2,1,0:T(8,128)S(1)}, u32[]{:S(2)}, u32[]{:S(2)}) async-start(f32[32,7,8,128]{3,2,1,0:T(8,128)} %shard_map.98), calls=%async_computation.1 | async-start | bytes 1835008 | tf_op jit(solution)/shard_map/all_to_all | solution.py:537
Sparse Core Ops, SparseCore 0:
  41.0 54.4 all-gather.3

commit v8 on v7

--- a/solution.py
+++ b/solution.py
@@ -11,7 +11,7 @@
 CROSS = ("xl", "core")
 PLANE = ("zh", "zl", "xh", "xl", "core")
 RING_X = ("xh", "xl")
-ROWS = ("xh", "xl", "y")
+ROWS = ("zh", "y")
 SPLIT = (4, 2, 2, 2, 2, 8)
 
 EY = 16
@@ -314,18 +314,20 @@
 def solve_kernel(
     count_ref, same_ref, other_ref, q_ref, out_ref, r_ref, d_ref, im_ref, mk_ref, x_ref, t_ref
 ):
-    zl, core = lax.axis_index("zl"), lax.axis_index("core")
-    z = 2 * lax.axis_index("zh") + zl
-    flip = [zl, 1 - zl]
-    row_id = 4 * lax.axis_index("y") + 2 * lax.axis_index("xh") + lax.axis_index("xl")
+    zh, zl = lax.axis_index("zh"), lax.axis_index("zl")
+    xh, xl, core = lax.axis_index("xh"), lax.axis_index("xl"), lax.axis_index("core")
+    e = xl * 2 + core
+    row_id = 4 * lax.axis_index("y") + zh
     harmonic = jnp.where(row_id == 1, NZ // 2, row_id // 2).astype(jnp.float32)
     wavesq = harmonic * harmonic * (SPAN_UNIT * SPAN_UNIT)
-    own = [pl.ds(pl.multiple_of(((2 * to + core) * 2 + z // 4) * 8, 8), 8) for to in range(2)]
+    own = pl.ds(pl.multiple_of(e * 16, 16), 16)
     flipped = DERIV.T
     zero = jnp.zeros((8, 128), jnp.float32)
 
     def here(k):
         return pl.ds(pl.multiple_of(k * 8, 8), 8)
+
+    flip = [zl, 1 - zl]
 
     def chunk_in(quarter, carry):
         from_xl, half = quarter // 2, quarter % 2
@@ -334,7 +336,7 @@
             for i in range(7):
                 block = jnp.stack(
                     [
-                        ref[half * 2 + s // 4, flip[s // 2 % 2], 2 * (s % 2) + from_xl, i]
+                        ref[2 * (s % 2) + from_xl, flip[s // 2 % 2], half * 2 + s // 4, i]
                         for s in range(8)
                     ]
                 )
@@ -349,8 +351,7 @@
 
     lax.fori_loop(0, 4, chunk_in, 0)
     for n in range(49):
-        x_ref[0, n] = zero
-        x_ref[1, n] = zero
+        x_ref[n] = jnp.zeros((16, 128), jnp.float32)
 
     lane = lax.broadcasted_iota(jnp.int32, (64, 128), 1)
     spot = lax.broadcasted_iota(jnp.int32, (64, 128), 0)
@@ -434,8 +435,7 @@
         step = rho / total(lax.fori_loop(0, 8, image, zero))
         join()
         for n in range(49):
-            for to in range(2):
-                x_ref[to, n] = x_ref[to, n] + step * d_ref[n, own[to], :]
+            x_ref[n] = x_ref[n] + step[0:1] * d_ref[n, own, :]
 
         def descend(k, acc):
             at = here(k)
@@ -455,14 +455,15 @@
     lax.fori_loop(0, count_ref[row_id], sweep, (rho, zero))
 
     for i in range(7):
-        for to in range(2):
-            block = jnp.stack([x_ref[to, i * 7 + j] for j in range(7)] + [zero])
+        for half in range(2):
+            rows = slice(8 * half, 8 * half + 8)
+            block = jnp.stack([x_ref[i * 7 + j, rows, :] for j in range(7)] + [zero])
             block = jnp.swapaxes(block, 0, 1)
             for s in range(8):
-                t_ref[to, s, i] = block[s]
+                t_ref[8 * half + s, i] = block[s]
     for to in range(4):
         for i in range(7):
-            value = t_ref[to % 2, z % 4 * 2 + to // 2, i]
+            value = t_ref[4 * to + 2 * zl + xh, i]
             for copy in range(8):
                 out_ref[to * 8 + copy, i] = value
 
@@ -477,8 +478,8 @@
         out_specs=vmem,
         scratch_shapes=[
             field, field, field, field,
-            pltpu.VMEM((2, 49, 8, 128), jnp.float32),
-            pltpu.VMEM((2, 8, 7, 8, 128), jnp.float32),
+            pltpu.VMEM((49, 16, 128), jnp.float32),
+            pltpu.VMEM((16, 7, 8, 128), jnp.float32),
         ],
         compiler_params=pltpu.CompilerParams(vmem_limit_bytes=40 * MIB),
     )(counts, same, other, metrics)
@@ -523,15 +524,14 @@
         lax.ppermute(up, CROSS, above),
         lax.ppermute(down, CROSS, [(b, a) for a, b in above]),
     )
-    packed = after(packed, faces)
-    turned = [lax.ppermute(packed, RING_X, turn) for turn in TURNS]
     new_stress, parts = stress_step(stress, velocity_grad, velocity, faces)
-    ring = jnp.stack([after(packed, parts)] + turned)
+    packed = after(packed, parts)
+    ring = jnp.stack([packed] + [lax.ppermute(packed, RING_X, turn) for turn in TURNS])
     metrics = metric_fields(lax.all_gather(ring, ("zh", "zl", "core")))
-    parts = lax.all_to_all(after(parts, ring), ROWS, 0, 0, tiled=True)
+    parts = lax.all_to_all(parts, ROWS, 0, 0, tiled=True)
     mine = jnp.sum(parts.reshape(4, 8, 7, 8, 128), axis=1)
     pair = jnp.stack([mine, lax.ppermute(mine, "zl", SWAP)])
-    same = lax.all_gather(pair, "zh")
+    same = lax.all_gather(pair, RING_X)
     other = lax.ppermute(same, "core", SWAP)
     answer = solve(iteration_counts, same, other, metrics)
     answer = lax.all_to_all(answer, ROWS, 0, 0, tiled=True)

time: 190 us -> 194 us (1.021)
  waiting for transfers between devices: 33.2 us -> 38.8 us
  Pallas kernels: 39 us -> 35.2 us
  starting transfers between devices: 32.1 us -> 35.9 us
    all_gather x1, blocking collectives: 23.7 us -> 14 us  [local(): same = lax.all_gather(pair, RING_X)]
    all_to_all x1, blocking collectives: 35.9 us -> 44.4 us  [local(): parts = lax.all_to_all(parts, ROWS, 0, 0, tiled=True)]
    all_to_all x1, starting transfers between devices: 3.96 us -> 8.79 us  [local(): answer = lax.all_to_all(answer, ROWS, 0, 0, tiled=True)]
    ppermute x3, waiting for transfers between devices: 0.01 us -> 4.83 us  [local(): lax.ppermute(packed, RING_X, turn)]
    pallas_call x1, Pallas kernels: 32.7 us -> 29 us  [solve(): pl.pallas_call(solve_kernel, out_shape=jax.ShapeDtypeStruct((NZ, 7, 8, 12...]
    ppermute x1, starting transfers between devices: 5.49 us -> 2.78 us  [local(): pair = jnp.stack([mine, lax.ppermute(mine, 'zl', SWAP)])]
    ppermute x1, waiting for transfers between devices: 2.15 us -> 0.01 us  [local(): lax.ppermute(left, FLOW, [(b, a) for a, b in ahead])]
    all_to_all x1, waiting for transfers between devices: 25.6 us -> 27.7 us  [local(): answer = lax.all_to_all(answer, ROWS, 0, 0, tiled=True)]
  transfers between devices with their start and end apart: 11 -> 11, of which waited for: 3 -> 4; matrix products, arithmetic and copies ran while one was open for 2% -> 2% of each run, Pallas kernels for 3% -> 1%
where the time goes in v8:
time: 194 us; the launch traced here: 193 us
  blocking collectives  58.4 us (30%)
  waiting for transfers between devices  38.8 us (20%)
  starting transfers between devices  35.9 us (19%)
  Pallas kernels  35.2 us (18%)
  between operations  14.3 us (7%)
  local copies, waits for them, and re-layouts  9.85 us (5%)
    all_to_all x1, blocking collectives, local(): parts = lax.all_to_all(parts, ROWS, 0, 0, tiled=True)  44.4 us
    pallas_call x1, Pallas kernels, solve(): pl.pallas_call(solve_kernel, out_shape=jax.ShapeDtypeStruct((NZ, 7, 8, 12...  29 us
    all_to_all x1, waiting for transfers between devices, local(): answer = lax.all_to_all(answer, ROWS, 0, 0, tiled=True)  27.7 us
    all_gather x1, blocking collectives, local(): same = lax.all_gather(pair, RING_X)  14 us
    ppermute x3, starting transfers between devices, local(): lax.ppermute(packed, RING_X, turn)  13.3 us
    unnamed x15, local copies, waits for them, and re-layouts  8.94 us
    all_to_all x1, starting transfers between devices, local(): answer = lax.all_to_all(answer, ROWS, 0, 0, tiled=True)  8.79 us
    ppermute x1, waiting for transfers between devices, local(): pair = jnp.stack([mine, lax.ppermute(mine, 'zl', SWAP)])  6.2 us
  transfers between devices with their start and end apart: 11, of which 4 were waited for; matrix products, arithmetic and copies ran while one was open for 2% of the time, Pallas kernels for 1%

profile of v8, /device:TPU:8, one launch (start us, length us, event | category | flops | bytes accessed | tf_op | source)
XLA Modules:
  0.0 193.3 jit_solution(1616973655795473356)
XLA Ops:
  7.2 1.2 copy.17.s_ref
  9.1 4.9 %collective-permute-start = (f32[4,8,128]{2,1,0:T(8,128)S(1)}, f32[4,8,128]{2,1,0:T(8,128)S(1)}, u32[]{:S(2)}, u32[]{:S(2)}) collective-permute-start(f32[4,8,128]{2,1,0:T(8,128)S(1)} %get-tuple-element.9), channel_id=1, source_target_pairs={{0,32},{32,64},{64,96},{96,128},{128,160},{160,192},{192,224},{224... | collective-permute-start | bytes 49160 | tf_op jit(solution)/shard_map/ppermute | solution.py:522
  14.0 1.3 collective-permute-start.1
  15.3 1.5 collective-permute-start.2
  16.8 1.3 collective-permute-start.3
  19.0 1.0 copy.19.v_ref
  19.9 1.3 copy.18.g_ref
  22.8 3.6 %shard_map.96 = (f32[6,4,7,7,128]{4,3,2,1,0:T(8,128)S(1)}, f32[32,7,8,128]{3,2,1,0:T(8,128)S(1)}) custom-call(f32[3072]{0:T(1024)S(1)} %copy-done.2, f32[6,4,7,7,128]{4,3,2,1,0:T(8,128)S(1)} %copy.17.s_ref, f32[9,4,7,7,128]{4,3,2,1,0:T(8,128)S(1)} %copy.18.g_ref, f32[2,4,7,7,128]{4,3,2,1,0:T(8,128)S(1)} %copy.19.v_ref, ...), custom_call_target="tpu_custom_call" | custom-call | tf_op jit(solution)/shard_map/pallas_call | solution.py:257
  26.3 8.6 %collective-permute-start.8 = (f32[152,128]{1,0:T(8,128)S(1)}, f32[152,128]{1,0:T(8,128)S(1)}, u32[]{:S(2)}, u32[]{:S(2)}) collective-permute-start(f32[152,128]{1,0:T(8,128)S(1)} %pad.4), channel_id=1, source_target_pairs={{0,48},{16,0},{32,16},{48,32},{1,49},{17,1},{33,17},{49,33},{2,50}... | collective-permute-start | bytes 233480 | tf_op jit(solution)/shard_map/ppermute | solution.py:529
  35.0 1.9 collective-permute-start.7
  36.9 2.8 %collective-permute-start.6 = (f32[152,128]{1,0:T(8,128)S(1)}, f32[152,128]{1,0:T(8,128)S(1)}, u32[]{:S(2)}, u32[]{:S(2)}) collective-permute-start(f32[152,128]{1,0:T(8,128)S(1)} %pad.4), channel_id=1, source_target_pairs={{0,16},{16,32},{32,48},{48,0},{1,17},{17,33},{33,49},{49,1},{2,18}... | collective-permute-start | bytes 233480 | tf_op jit(solution)/shard_map/ppermute | solution.py:529
  39.7 3.5 %collective-permute-done.7 = f32[152,128]{1,0:T(8,128)S(1)} collective-permute-done((f32[152,128]{1,0:T(8,128)S(1)}, f32[152,128]{1,0:T(8,128)S(1)}, u32[]{:S(2)}, u32[]{:S(2)}) %collective-permute-start.7) | collective-permute-done | bytes 77856 | tf_op jit(solution)/shard_map/ppermute | solution.py:529
  43.1 1.4 collective-permute-done.6
  45.3 44.4 %all_to_all.10 = f32[32,7,8,128]{3,2,1,0:T(8,128)S(1)} all-to-all(f32[32,7,8,128]{3,2,1,0:T(8,128)S(1)} %get-tuple-element.14), channel_id=1, replica_groups=mesh['zh'=4,'zl'=2,'xh'=2,'xl'=2,'core'=2,'y'=8] {'zh','y'}, dimensions={0} | all-to-all | bytes 1835008 | tf_op jit(solution)/shard_map/all_to_all | solution.py:531
  89.7 2.8 %collective-permute-start.4 = (f32[4,7,8,128]{3,2,1,0:T(8,128)S(1)}, f32[4,7,8,128]{3,2,1,0:T(8,128)S(1)}, u32[]{:S(2)}, u32[]{:S(2)}) collective-permute-start(f32[4,7,8,128]{3,2,1,0:T(8,128)S(1)} %bitcast_reduce_fusion), channel_id=1, source_target_pairs={{0,64},{64,0},{1,65},{65,1},{2,66},{66,2},{3,67},{67,3},{4,68},{68... | collective-permute-start | bytes 344072 | tf_op jit(solution)/shard_map/ppermute | solution.py:533
  92.5 6.2 %collective-permute-done.4 = f32[4,7,8,128]{3,2,1,0:T(8,128)S(1)} collective-permute-done((f32[4,7,8,128]{3,2,1,0:T(8,128)S(1)}, f32[4,7,8,128]{3,2,1,0:T(8,128)S(1)}, u32[]{:S(2)}, u32[]{:S(2)}) %collective-permute-start.4) | collective-permute-done | bytes 114720 | tf_op jit(solution)/shard_map/ppermute | solution.py:533
  98.7 14.0 %all-gather = f32[8,4,7,8,128]{4,3,2,1,0:T(8,128)S(1)} all-gather(f32[2,4,7,8,128]{4,3,2,1,0:T(8,128)S(1)} %pad_maximum_fusion.1), channel_id=2, replica_groups=mesh['zh'=4,'zl'=2,'xh'=2,'xl'=2,'core'=2,'y'=8] {'xh','xl'}, dimensions={0}, use_global_device_ids=true | all-gather | bytes 1146880 | tf_op jit(solution)/shard_map/all_gather | solution.py:534
  112.7 2.0 %collective-permute-start.5 = (f32[4,2,4,7,8,128]{5,4,3,2,1,0:T(8,128)S(1)}, f32[4,2,4,7,8,128]{5,4,3,2,1,0:T(8,128)S(1)}, u32[]{:S(2)}, u32[]{:S(2)}) collective-permute-start(f32[4,2,4,7,8,128]{5,4,3,2,1,0:T(8,128)S(1)} %bitcast.11), channel_id=1, source_target_pairs={{0,8},{8,0},{1,9},{9,1},{2,10},{10,2},{3,11},{11,3},{4,12},{12,4},... | collective-permute-start | bytes 2752520 | tf_op jit(solution)/shard_map/ppermute | solution.py:535
  114.8 2.4 %copy-done = f32[64,152,128]{2,1,0:T(8,128)S(1)} copy-done((f32[64,152,128]{2,1,0:T(8,128)S(1)}, f32[64,152,128]{2,1,0:T(8,128)}, u32[]{:S(2)}) %copy-start) | copy-done | bytes 4980760
  117.2 1.2 shard_map.97.q_ref
  118.4 29.0 %shard_map.98 = f32[32,7,8,128]{3,2,1,0:T(8,128)} custom-call(s32[32]{0:T(128)S(1)} %copy-done.4, f32[4,2,4,7,8,128]{5,4,3,2,1,0:T(8,128)S(1)} %bitcast.12, f32[4,2,4,7,8,128]{5,4,3,2,1,0:T(8,128)S(1)} %collective-permute-done.5.other_ref, f32[3,49,64,128]{3,2,1,0:T(8,128)S(1)} %shard_map.97.q_ref), custom_call_target="tpu_custom_call" | custom-call | tf_op jit(solution)/shard_map/pallas_call | solution.py:474
  147.4 8.8 %all-to-all-start.1 = ((f32[32,7,8,128]{3,2,1,0:T(8,128)}), f32[32,7,8,128]{3,2,1,0:T(8,128)S(1)}, u32[]{:S(2)}, u32[]{:S(2)}) async-start(f32[32,7,8,128]{3,2,1,0:T(8,128)} %shard_map.98), calls=%async_computation.1 | async-start | bytes 1835008 | tf_op jit(solution)/shard_map/all_to_all | solution.py:537
  156.2 1.0 copy.20
  157.2 27.7 %all-to-all-done.1.rows_ref = f32[32,7,8,128]{3,2,1,0:T(8,128)S(1)} async-done(((f32[32,7,8,128]{3,2,1,0:T(8,128)}), f32[32,7,8,128]{3,2,1,0:T(8,128)S(1)}, u32[]{:S(2)}, u32[]{:S(2)}) %all-to-all-start.1) | async-done | bytes 917536 | tf_op jit(solution)/shard_map/all_to_all | solution.py:537
  (26 shorter events, 5.5 us)
Async XLA Ops:
  7.2 107.6 %all-gather.4.cloned.1.call-start = ((), (), s32[]{:S(2)}) async-start(), calls=%async_computation.2 | async-start | bytes 5292032 | tf_op jit(solution)/shard_map/all_gather | solution.py:530
  9.1 12.2 %collective-permute-start = (f32[4,8,128]{2,1,0:T(8,128)S(1)}, f32[4,8,128]{2,1,0:T(8,128)S(1)}, u32[]{:S(2)}, u32[]{:S(2)}) collective-permute-start(f32[4,8,128]{2,1,0:T(8,128)S(1)} %get-tuple-element.9), channel_id=1, source_target_pairs={{0,32},{32,64},{64,96},{96,128},{128,160},{160,192},{192,224},{224... | collective-permute-start | bytes 49160 | tf_op jit(solution)/shard_map/ppermute | solution.py:522
  14.0 7.3 %collective-permute-start.1 = (f32[4,8,128]{2,1,0:T(8,128)S(1)}, f32[4,8,128]{2,1,0:T(8,128)S(1)}, u32[]{:S(2)}, u32[]{:S(2)}) collective-permute-start(f32[4,8,128]{2,1,0:T(8,128)S(1)} %get-tuple-element.10), channel_id=1, source_target_pairs={{32,0},{64,32},{96,64},{128,96},{160,128},{192,160},{224,192},{256... | collective-permute-start | bytes 49160 | tf_op jit(solution)/shard_map/ppermute | solution.py:523
  15.3 6.0 %collective-permute-start.2 = (f32[4,8,128]{2,1,0:T(8,128)S(1)}, f32[4,8,128]{2,1,0:T(8,128)S(1)}, u32[]{:S(2)}, u32[]{:S(2)}) collective-permute-start(f32[4,8,128]{2,1,0:T(8,128)S(1)} %get-tuple-element.11), channel_id=1, source_target_pairs={{0,8},{8,16},{16,24},{1,9},{9,17},{17,25},{2,10},{10,18},{18,26},{... | collective-permute-start | bytes 49160 | tf_op jit(solution)/shard_map/ppermute | solution.py:524
  16.8 4.5 %collective-permute-start.3 = (f32[4,8,128]{2,1,0:T(8,128)S(1)}, f32[4,8,128]{2,1,0:T(8,128)S(1)}, u32[]{:S(2)}, u32[]{:S(2)}) collective-permute-start(f32[4,8,128]{2,1,0:T(8,128)S(1)} %get-tuple-element.12), channel_id=1, source_target_pairs={{8,0},{16,8},{24,16},{9,1},{17,9},{25,17},{10,2},{18,10},{26,18},{... | collective-permute-start | bytes 49160 | tf_op jit(solution)/shard_map/ppermute | solution.py:525
  21.3 0.8 copy-start.1
  22.1 0.7 copy-start.2
  26.3 13.3 %collective-permute-start.8 = (f32[152,128]{1,0:T(8,128)S(1)}, f32[152,128]{1,0:T(8,128)S(1)}, u32[]{:S(2)}, u32[]{:S(2)}) collective-permute-start(f32[152,128]{1,0:T(8,128)S(1)} %pad.4), channel_id=1, source_target_pairs={{0,48},{16,0},{32,16},{48,32},{1,49},{17,1},{33,17},{49,33},{2,50}... | collective-permute-start | bytes 233480 | tf_op jit(solution)/shard_map/ppermute | solution.py:529
  35.0 8.2 %collective-permute-start.7 = (f32[152,128]{1,0:T(8,128)S(1)}, f32[152,128]{1,0:T(8,128)S(1)}, u32[]{:S(2)}, u32[]{:S(2)}) collective-permute-start(f32[152,128]{1,0:T(8,128)S(1)} %pad.4), channel_id=1, source_target_pairs={{0,32},{16,48},{32,0},{48,16},{1,33},{17,49},{33,1},{49,17},{2,34}... | collective-permute-start | bytes 233480 | tf_op jit(solution)/shard_map/ppermute | solution.py:529
  36.9 7.6 %collective-permute-start.6 = (f32[152,128]{1,0:T(8,128)S(1)}, f32[152,128]{1,0:T(8,128)S(1)}, u32[]{:S(2)}, u32[]{:S(2)}) collective-permute-start(f32[152,128]{1,0:T(8,128)S(1)} %pad.4), channel_id=1, source_target_pairs={{0,16},{16,32},{32,48},{48,0},{1,17},{17,33},{33,49},{49,1},{2,18}... | collective-permute-start | bytes 233480 | tf_op jit(solution)/shard_map/ppermute | solution.py:529
  89.7 9.0 %collective-permute-start.4 = (f32[4,7,8,128]{3,2,1,0:T(8,128)S(1)}, f32[4,7,8,128]{3,2,1,0:T(8,128)S(1)}, u32[]{:S(2)}, u32[]{:S(2)}) collective-permute-start(f32[4,7,8,128]{3,2,1,0:T(8,128)S(1)} %bitcast_reduce_fusion), channel_id=1, source_target_pairs={{0,64},{64,0},{1,65},{65,1},{2,66},{66,2},{3,67},{67,3},{4,68},{68... | collective-permute-start | bytes 344072 | tf_op jit(solution)/shard_map/ppermute | solution.py:533
  112.7 5.7 %copy-start.4 = (s32[32]{0:T(128)S(1)}, s32[32]{0:T(128)}, u32[]{:S(2)}) copy-start(s32[32]{0:T(128)} %count_ref.1) | copy-start | bytes 388
  112.7 5.7 %collective-permute-start.5 = (f32[4,2,4,7,8,128]{5,4,3,2,1,0:T(8,128)S(1)}, f32[4,2,4,7,8,128]{5,4,3,2,1,0:T(8,128)S(1)}, u32[]{:S(2)}, u32[]{:S(2)}) collective-permute-start(f32[4,2,4,7,8,128]{5,4,3,2,1,0:T(8,128)S(1)} %bitcast.11), channel_id=1, source_target_pairs={{0,8},{8,0},{1,9},{9,1},{2,10},{10,2},{3,11},{11,3},{4,12},{12,4},... | collective-permute-start | bytes 2752520 | tf_op jit(solution)/shard_map/ppermute | solution.py:535
  114.8 2.4 %copy-start = (f32[64,152,128]{2,1,0:T(8,128)S(1)}, f32[64,152,128]{2,1,0:T(8,128)}, u32[]{:S(2)}) copy-start(f32[64,152,128]{2,1,0:T(8,128)} %all-gather.4.cloned.1.call-done) | copy-start | bytes 14942212
  118.4 66.5 %copy-start.3 = (f32[1024]{0:T(1024)S(1)}, f32[1024]{0:T(1024)}, u32[]{:S(2)}) copy-start(f32[1024]{0:T(1024)} %constant.12.clone.coef_ref) | copy-start | bytes 12292
  147.4 37.5 %all-to-all-start.1 = ((f32[32,7,8,128]{3,2,1,0:T(8,128)}), f32[32,7,8,128]{3,2,1,0:T(8,128)S(1)}, u32[]{:S(2)}, u32[]{:S(2)}) async-start(f32[32,7,8,128]{3,2,1,0:T(8,128)} %shard_map.98), calls=%async_computation.1 | async-start | bytes 1835008 | tf_op jit(solution)/shard_map/all_to_all | solution.py:537
Sparse Core Ops, SparseCore 0:
  45.4 67.9 all-gather.3

commit v9 on v7

--- a/solution.py
+++ b/solution.py
@@ -149,8 +149,8 @@
 
 
 def stress_kernel(
-    coef_ref, s_ref, g_ref, v_ref, left_ref, right_ref, below_ref, above_ref, dcol_ref,
-    new_ref, rows_ref, t_ref, d_ref, n_ref, f_ref, p_ref, lb_ref,
+    coef_ref, s_ref, g_ref, v_ref, left_ref, right_ref, below_ref, above_ref,
+    new_ref, rows_ref, t_ref, d_ref, n_ref, f_ref, p_ref, lb_ref, dcol_ref,
 ):
     lane = lanes()
     inner = lane % 16
@@ -165,6 +165,11 @@
         return total
 
     zero = jnp.zeros((8, 128), jnp.float32)
+    for m in range(7):
+        column = zero
+        for j in range(7):
+            column = jnp.where(row == j, float(twice[j, m]), column)
+        dcol_ref[m] = column
     for i in range(7):
         for c in range(6):
             t_ref[c, i] = zero
@@ -251,8 +256,6 @@
 
 
 def stress_step(stress, grad, velocity, faces):
-    dcol = np.zeros((7, 8, 128))
-    dcol[:, :7, :] = 2.0 * DERIV.T[:, :, None]
     vmem = pl.BlockSpec(memory_space=pltpu.VMEM)
     return pl.pallas_call(
         stress_kernel,
@@ -260,7 +263,7 @@
             jax.ShapeDtypeStruct((6, 4, 7, 7, 128), jnp.float32),
             jax.ShapeDtypeStruct((NZ, 7, 8, 128), jnp.float32),
         ],
-        in_specs=[pl.BlockSpec(memory_space=pltpu.SMEM)] + [vmem] * 8,
+        in_specs=[pl.BlockSpec(memory_space=pltpu.SMEM)] + [vmem] * 7,
         out_specs=[vmem] * 2,
         scratch_shapes=[
             pltpu.VMEM((6, 7, 8, 128), jnp.float32),
@@ -269,12 +272,10 @@
             pltpu.VMEM((7, 8, 128), jnp.float32),
             pltpu.VMEM((3, 4, 7, 8, 128), jnp.float32),
             pltpu.VMEM((11, 7, 8, 128), jnp.float32),
+            pltpu.VMEM((7, 8, 128), jnp.float32),
         ],
         compiler_params=pltpu.CompilerParams(vmem_limit_bytes=24 * MIB),
-    )(
-        jnp.asarray(source_coefs()), stress, grad, velocity, *faces,
-        jnp.asarray(dcol, jnp.float32),
-    )
+    )(jnp.asarray(source_coefs()), stress, grad, velocity, *faces)
 
 
 def metric_kernel(m_ref, q_ref):
@@ -432,7 +433,6 @@
             return acc
 
         step = rho / total(lax.fori_loop(0, 8, image, zero))
-        join()
         for n in range(49):
             for to in range(2):
                 x_ref[to, n] = x_ref[to, n] + step * d_ref[n, own[to], :]
@@ -449,10 +449,15 @@
                 acc = acc + square(line, 0.5 if i in (0, 6) else 1.0)
             return acc
 
-        fresh = total(lax.fori_loop(0, 8, descend, zero))
-        return fresh, fresh / rho
-
-    lax.fori_loop(0, count_ref[row_id], sweep, (rho, zero))
+        def proceed():
+            join()
+            fresh = total(lax.fori_loop(0, 8, descend, zero))
+            return fresh, fresh / rho
+
+        return lax.cond(t + 1 < count, proceed, lambda: (rho, beta))
+
+    count = count_ref[row_id]
+    lax.fori_loop(0, count, sweep, (rho, zero))
 
     for i in range(7):
         for to in range(2):
@@ -514,6 +519,7 @@
 
 def local(stress, velocity_grad, velocity, metric, iteration_counts):
     packed = jnp.pad(metric.reshape(147, 128), ((0, 5), (0, 0)))
+    turned = [lax.ppermute(packed, RING_X, turn) for turn in TURNS]
     right, left, up, down = pack_faces(stress)
     ahead = [(c, c + 1) for c in range(15)]
     above = [(e, e + 1) for e in range(3)]
@@ -523,12 +529,11 @@
         lax.ppermute(up, CROSS, above),
         lax.ppermute(down, CROSS, [(b, a) for a, b in above]),
     )
-    packed = after(packed, faces)
-    turned = [lax.ppermute(packed, RING_X, turn) for turn in TURNS]
+    ring = jnp.stack([after(packed, right)] + turned)
+    faces = after(faces, ring)
+    metrics = metric_fields(lax.all_gather(ring, ("zh", "zl", "core")))
     new_stress, parts = stress_step(stress, velocity_grad, velocity, faces)
-    ring = jnp.stack([after(packed, parts)] + turned)
-    metrics = metric_fields(lax.all_gather(ring, ("zh", "zl", "core")))
-    parts = lax.all_to_all(after(parts, ring), ROWS, 0, 0, tiled=True)
+    parts = lax.all_to_all(parts, ROWS, 0, 0, tiled=True)
     mine = jnp.sum(parts.reshape(4, 8, 7, 8, 128), axis=1)
     pair = jnp.stack([mine, lax.ppermute(mine, "zl", SWAP)])
     same = lax.all_gather(pair, "zh")

time: 190 us -> 186 us (0.979)
  the two profiles are of different devices: /device:TPU:8 before, /device:TPU:72 now
where the time goes in v9:
time: 186 us; the launch traced here: 185 us
  blocking collectives  58.8 us (32%)
  starting transfers between devices  37.2 us (20%)
  waiting for transfers between devices  34.2 us (18%)
  Pallas kernels  31.4 us (17%)
  between operations  14.2 us (8%)
  local copies, waits for them, and re-layouts  8.41 us (5%)
    all_to_all x1, blocking collectives, local(): parts = lax.all_to_all(parts, ROWS, 0, 0, tiled=True)  35.5 us
    all_to_all x1, waiting for transfers between devices, local(): answer = lax.all_to_all(answer, ROWS, 0, 0, tiled=True)  25.6 us
    pallas_call x1, Pallas kernels, solve(): pl.pallas_call(solve_kernel, out_shape=jax.ShapeDtypeStruct((NZ, 7, 8, 12...  25 us
    all_gather x1, blocking collectives, local(): same = lax.all_gather(pair, 'zh')  23.4 us
    all_to_all x1, starting transfers between devices, local(): answer = lax.all_to_all(answer, ROWS, 0, 0, tiled=True)  13.1 us
    ppermute x3, starting transfers between devices, local(): turned = [lax.ppermute(packed, RING_X, turn) for turn in TURNS]  10.2 us
    unnamed x13, local copies, waits for them, and re-layouts  7.51 us
    ppermute x1, starting transfers between devices, local(): lax.ppermute(right, FLOW, ahead)  4.83 us
  transfers between devices with their start and end apart: 11, of which 5 were waited for; matrix products, arithmetic and copies ran while one was open for 2% of the time, Pallas kernels for 3%

profile of v9, /device:TPU:72, one launch (start us, length us, event | category | flops | bytes accessed | tf_op | source)
XLA Modules:
  0.0 185.0 jit_solution(9539585742177432015)
XLA Ops:
  7.2 0.9 reshape.10
  8.1 4.7 %collective-permute-start.6 = (f32[152,128]{1,0:T(8,128)S(1)}, f32[152,128]{1,0:T(8,128)S(1)}, u32[]{:S(2)}, u32[]{:S(2)}) collective-permute-start(f32[152,128]{1,0:T(8,128)S(1)} %pad.4), channel_id=1, source_target_pairs={{0,48},{16,0},{32,16},{48,32},{1,49},{17,1},{33,17},{49,33},{2,50}... | collective-permute-start | bytes 233480 | tf_op jit(solution)/shard_map/ppermute | solution.py:522
  12.8 2.7 %collective-permute-start.5 = (f32[152,128]{1,0:T(8,128)S(1)}, f32[152,128]{1,0:T(8,128)S(1)}, u32[]{:S(2)}, u32[]{:S(2)}) collective-permute-start(f32[152,128]{1,0:T(8,128)S(1)} %pad.4), channel_id=1, source_target_pairs={{0,32},{16,48},{32,0},{48,16},{1,33},{17,49},{33,1},{49,17},{2,34}... | collective-permute-start | bytes 233480 | tf_op jit(solution)/shard_map/ppermute | solution.py:522
  15.5 2.8 %collective-permute-start.4 = (f32[152,128]{1,0:T(8,128)S(1)}, f32[152,128]{1,0:T(8,128)S(1)}, u32[]{:S(2)}, u32[]{:S(2)}) collective-permute-start(f32[152,128]{1,0:T(8,128)S(1)} %pad.4), channel_id=1, source_target_pairs={{0,16},{16,32},{32,48},{48,0},{1,17},{17,33},{33,49},{49,1},{2,18}... | collective-permute-start | bytes 233480 | tf_op jit(solution)/shard_map/ppermute | solution.py:522
  18.3 1.2 copy.16.s_ref
  21.0 2.0 %collective-permute-done.4 = f32[152,128]{1,0:T(8,128)S(1)} collective-permute-done((f32[152,128]{1,0:T(8,128)S(1)}, f32[152,128]{1,0:T(8,128)S(1)}, u32[]{:S(2)}, u32[]{:S(2)}) %collective-permute-start.4) | collective-permute-done | bytes 77856 | tf_op jit(solution)/shard_map/ppermute | solution.py:522
  23.8 2.5 %collective-permute-start.1 = (f32[4,8,128]{2,1,0:T(8,128)S(1)}, f32[4,8,128]{2,1,0:T(8,128)S(1)}, u32[]{:S(2)}, u32[]{:S(2)}) collective-permute-start(f32[4,8,128]{2,1,0:T(8,128)S(1)} %get-tuple-element.14), channel_id=1, source_target_pairs={{32,0},{64,32},{96,64},{128,96},{160,128},{192,160},{224,192},{256... | collective-permute-start | bytes 49160 | tf_op jit(solution)/shard_map/ppermute | solution.py:528
  26.3 1.3 collective-permute-start.2
  27.6 1.3 collective-permute-start.3
  28.9 4.8 %collective-permute-start = (f32[4,8,128]{2,1,0:T(8,128)S(1)}, f32[4,8,128]{2,1,0:T(8,128)S(1)}, u32[]{:S(2)}, u32[]{:S(2)}) collective-permute-start(f32[4,8,128]{2,1,0:T(8,128)S(1)} %get-tuple-element.13), channel_id=1, source_target_pairs={{0,32},{32,64},{64,96},{96,128},{128,160},{160,192},{192,224},{224... | collective-permute-start | bytes 49160 | tf_op jit(solution)/shard_map/ppermute | solution.py:527
  33.8 1.0 copy.18.v_ref
  34.7 1.3 copy.17.g_ref
  37.0 3.6 %shard_map.87 = (f32[6,4,7,7,128]{4,3,2,1,0:T(8,128)S(1)}, f32[32,7,8,128]{3,2,1,0:T(8,128)S(1)}) custom-call(f32[3072]{0:T(1024)S(1)} %copy-done.1, f32[6,4,7,7,128]{4,3,2,1,0:T(8,128)S(1)} %copy.16.s_ref, f32[9,4,7,7,128]{4,3,2,1,0:T(8,128)S(1)} %copy.17.g_ref, f32[2,4,7,7,128]{4,3,2,1,0:T(8,128)S(1)} %copy.18.v_ref, ...), custom_call_target="tpu_custom_call" | custom-call | tf_op jit(solution)/shard_map/pallas_call | solution.py:260
  40.6 35.5 %all_to_all.10 = f32[32,7,8,128]{3,2,1,0:T(8,128)S(1)} all-to-all(f32[32,7,8,128]{3,2,1,0:T(8,128)S(1)} %get-tuple-element.23), channel_id=1, replica_groups=mesh['zh'=4,'zl'=2,'xh'=2,'xl'=2,'core'=2,'y'=8] {'xh','xl','y'}, dimensions={0} | all-to-all | bytes 1835008 | tf_op jit(solution)/shard_map/all_to_all | solution.py:536
  76.1 1.9 %collective-permute-start.7 = (f32[4,7,8,128]{3,2,1,0:T(8,128)S(1)}, f32[4,7,8,128]{3,2,1,0:T(8,128)S(1)}, u32[]{:S(2)}, u32[]{:S(2)}) collective-permute-start(f32[4,7,8,128]{3,2,1,0:T(8,128)S(1)} %bitcast_reduce_fusion), channel_id=1, source_target_pairs={{0,64},{64,0},{1,65},{65,1},{2,66},{66,2},{3,67},{67,3},{4,68},{68... | collective-permute-start | bytes 344072 | tf_op jit(solution)/shard_map/ppermute | solution.py:538
  78.0 4.8 %collective-permute-done.7 = f32[4,7,8,128]{3,2,1,0:T(8,128)S(1)} collective-permute-done((f32[4,7,8,128]{3,2,1,0:T(8,128)S(1)}, f32[4,7,8,128]{3,2,1,0:T(8,128)S(1)}, u32[]{:S(2)}, u32[]{:S(2)}) %collective-permute-start.7) | collective-permute-done | bytes 114720 | tf_op jit(solution)/shard_map/ppermute | solution.py:538
  82.8 23.4 %all-gather = f32[8,4,7,8,128]{4,3,2,1,0:T(8,128)S(1)} all-gather(f32[2,4,7,8,128]{4,3,2,1,0:T(8,128)S(1)} %pad_maximum_fusion.1), channel_id=2, replica_groups=mesh['zh'=4,'zl'=2,'xh'=2,'xl'=2,'core'=2,'y'=8] {'zh'}, dimensions={0}, use_global_device_ids=true | all-gather | bytes 1146880 | tf_op jit(solution)/shard_map/all_gather | solution.py:539
  106.2 2.0 %collective-permute-start.8 = (f32[4,2,4,7,8,128]{5,4,3,2,1,0:T(8,128)S(1)}, f32[4,2,4,7,8,128]{5,4,3,2,1,0:T(8,128)S(1)}, u32[]{:S(2)}, u32[]{:S(2)}) collective-permute-start(f32[4,2,4,7,8,128]{5,4,3,2,1,0:T(8,128)S(1)} %bitcast.11), channel_id=1, source_target_pairs={{0,8},{8,0},{1,9},{9,1},{2,10},{10,2},{3,11},{11,3},{4,12},{12,4},... | collective-permute-start | bytes 2752520 | tf_op jit(solution)/shard_map/ppermute | solution.py:540
  108.3 2.4 %copy-done = f32[64,152,128]{2,1,0:T(8,128)S(1)} copy-done((f32[64,152,128]{2,1,0:T(8,128)S(1)}, f32[64,152,128]{2,1,0:T(8,128)}, u32[]{:S(2)}) %copy-start) | copy-done | bytes 4980760
  110.7 1.2 shard_map.88.q_ref
  111.9 25.0 %shard_map.89 = f32[32,7,8,128]{3,2,1,0:T(8,128)} custom-call(s32[32]{0:T(128)S(1)} %copy-done.3, f32[4,2,4,7,8,128]{5,4,3,2,1,0:T(8,128)S(1)} %bitcast.12, f32[4,2,4,7,8,128]{5,4,3,2,1,0:T(8,128)S(1)} %collective-permute-done.8.other_ref, f32[3,49,64,128]{3,2,1,0:T(8,128)S(1)} %shard_map.88.q_ref), custom_call_target="tpu_custom_call" | custom-call | tf_op jit(solution)/shard_map/pallas_call | solution.py:478
  136.9 13.1 %all-to-all-start.1 = ((f32[32,7,8,128]{3,2,1,0:T(8,128)}), f32[32,7,8,128]{3,2,1,0:T(8,128)S(1)}, u32[]{:S(2)}, u32[]{:S(2)}) async-start(f32[32,7,8,128]{3,2,1,0:T(8,128)} %shard_map.89), calls=%async_computation.1 | async-start | bytes 1835008 | tf_op jit(solution)/shard_map/all_to_all | solution.py:542
  150.0 1.0 copy.19
  151.0 25.6 %all-to-all-done.1.rows_ref = f32[32,7,8,128]{3,2,1,0:T(8,128)S(1)} async-done(((f32[32,7,8,128]{3,2,1,0:T(8,128)}), f32[32,7,8,128]{3,2,1,0:T(8,128)S(1)}, u32[]{:S(2)}, u32[]{:S(2)}) %all-to-all-start.1) | async-done | bytes 917536 | tf_op jit(solution)/shard_map/all_to_all | solution.py:542
  (24 shorter events, 4.8 us)
Async XLA Ops:
  7.2 29.8 %copy-start.1 = (f32[3072]{0:T(1024)S(1)}, f32[3072]{0:T(1024)}, u32[]{:S(2)}) copy-start(f32[3072]{0:T(1024)} %constant.8.clone.coef_ref) | copy-start | bytes 36868
  7.2 101.1 %all-gather.4.cloned.1.call-start = ((), (), s32[]{:S(2)}) async-start(), calls=%async_computation.2 | async-start | bytes 5292032 | tf_op jit(solution)/shard_map/all_gather | solution.py:534
  8.1 12.1 %collective-permute-start.6 = (f32[152,128]{1,0:T(8,128)S(1)}, f32[152,128]{1,0:T(8,128)S(1)}, u32[]{:S(2)}, u32[]{:S(2)}) collective-permute-start(f32[152,128]{1,0:T(8,128)S(1)} %pad.4), channel_id=1, source_target_pairs={{0,48},{16,0},{32,16},{48,32},{1,49},{17,1},{33,17},{49,33},{2,50}... | collective-permute-start | bytes 233480 | tf_op jit(solution)/shard_map/ppermute | solution.py:522
  12.8 8.2 %collective-permute-start.5 = (f32[152,128]{1,0:T(8,128)S(1)}, f32[152,128]{1,0:T(8,128)S(1)}, u32[]{:S(2)}, u32[]{:S(2)}) collective-permute-start(f32[152,128]{1,0:T(8,128)S(1)} %pad.4), channel_id=1, source_target_pairs={{0,32},{16,48},{32,0},{48,16},{1,33},{17,49},{33,1},{49,17},{2,34}... | collective-permute-start | bytes 233480 | tf_op jit(solution)/shard_map/ppermute | solution.py:522
  15.5 7.5 %collective-permute-start.4 = (f32[152,128]{1,0:T(8,128)S(1)}, f32[152,128]{1,0:T(8,128)S(1)}, u32[]{:S(2)}, u32[]{:S(2)}) collective-permute-start(f32[152,128]{1,0:T(8,128)S(1)} %pad.4), channel_id=1, source_target_pairs={{0,16},{16,32},{32,48},{48,0},{1,17},{17,33},{33,49},{49,1},{2,18}... | collective-permute-start | bytes 233480 | tf_op jit(solution)/shard_map/ppermute | solution.py:522
  23.8 12.3 %collective-permute-start.1 = (f32[4,8,128]{2,1,0:T(8,128)S(1)}, f32[4,8,128]{2,1,0:T(8,128)S(1)}, u32[]{:S(2)}, u32[]{:S(2)}) collective-permute-start(f32[4,8,128]{2,1,0:T(8,128)S(1)} %get-tuple-element.14), channel_id=1, source_target_pairs={{32,0},{64,32},{96,64},{128,96},{160,128},{192,160},{224,192},{256... | collective-permute-start | bytes 49160 | tf_op jit(solution)/shard_map/ppermute | solution.py:528
  26.3 9.7 %collective-permute-start.2 = (f32[4,8,128]{2,1,0:T(8,128)S(1)}, f32[4,8,128]{2,1,0:T(8,128)S(1)}, u32[]{:S(2)}, u32[]{:S(2)}) collective-permute-start(f32[4,8,128]{2,1,0:T(8,128)S(1)} %get-tuple-element.15), channel_id=1, source_target_pairs={{0,8},{8,16},{16,24},{1,9},{9,17},{17,25},{2,10},{10,18},{18,26},{... | collective-permute-start | bytes 49160 | tf_op jit(solution)/shard_map/ppermute | solution.py:529
  27.6 8.5 %collective-permute-start.3 = (f32[4,8,128]{2,1,0:T(8,128)S(1)}, f32[4,8,128]{2,1,0:T(8,128)S(1)}, u32[]{:S(2)}, u32[]{:S(2)}) collective-permute-start(f32[4,8,128]{2,1,0:T(8,128)S(1)} %get-tuple-element.16), channel_id=1, source_target_pairs={{8,0},{16,8},{24,16},{9,1},{17,9},{25,17},{10,2},{18,10},{26,18},{... | collective-permute-start | bytes 49160 | tf_op jit(solution)/shard_map/ppermute | solution.py:530
  28.9 8.1 %collective-permute-start = (f32[4,8,128]{2,1,0:T(8,128)S(1)}, f32[4,8,128]{2,1,0:T(8,128)S(1)}, u32[]{:S(2)}, u32[]{:S(2)}) collective-permute-start(f32[4,8,128]{2,1,0:T(8,128)S(1)} %get-tuple-element.13), channel_id=1, source_target_pairs={{0,32},{32,64},{64,96},{96,128},{128,160},{160,192},{192,224},{224... | collective-permute-start | bytes 49160 | tf_op jit(solution)/shard_map/ppermute | solution.py:527
  76.1 6.7 %collective-permute-start.7 = (f32[4,7,8,128]{3,2,1,0:T(8,128)S(1)}, f32[4,7,8,128]{3,2,1,0:T(8,128)S(1)}, u32[]{:S(2)}, u32[]{:S(2)}) collective-permute-start(f32[4,7,8,128]{3,2,1,0:T(8,128)S(1)} %bitcast_reduce_fusion), channel_id=1, source_target_pairs={{0,64},{64,0},{1,65},{65,1},{2,66},{66,2},{3,67},{67,3},{4,68},{68... | collective-permute-start | bytes 344072 | tf_op jit(solution)/shard_map/ppermute | solution.py:538
  106.2 5.7 %copy-start.3 = (s32[32]{0:T(128)S(1)}, s32[32]{0:T(128)}, u32[]{:S(2)}) copy-start(s32[32]{0:T(128)} %count_ref.1) | copy-start | bytes 388
  106.2 5.7 %collective-permute-start.8 = (f32[4,2,4,7,8,128]{5,4,3,2,1,0:T(8,128)S(1)}, f32[4,2,4,7,8,128]{5,4,3,2,1,0:T(8,128)S(1)}, u32[]{:S(2)}, u32[]{:S(2)}) collective-permute-start(f32[4,2,4,7,8,128]{5,4,3,2,1,0:T(8,128)S(1)} %bitcast.11), channel_id=1, source_target_pairs={{0,8},{8,0},{1,9},{9,1},{2,10},{10,2},{3,11},{11,3},{4,12},{12,4},... | collective-permute-start | bytes 2752520 | tf_op jit(solution)/shard_map/ppermute | solution.py:540
  108.3 2.4 %copy-start = (f32[64,152,128]{2,1,0:T(8,128)S(1)}, f32[64,152,128]{2,1,0:T(8,128)}, u32[]{:S(2)}) copy-start(f32[64,152,128]{2,1,0:T(8,128)} %all-gather.4.cloned.1.call-done) | copy-start | bytes 14942212
  111.8 64.8 %copy-start.2 = (f32[1024]{0:T(1024)S(1)}, f32[1024]{0:T(1024)}, u32[]{:S(2)}) copy-start(f32[1024]{0:T(1024)} %constant.9.clone.coef_ref) | copy-start | bytes 12292
  136.9 39.7 %all-to-all-start.1 = ((f32[32,7,8,128]{3,2,1,0:T(8,128)}), f32[32,7,8,128]{3,2,1,0:T(8,128)S(1)}, u32[]{:S(2)}, u32[]{:S(2)}) async-start(f32[32,7,8,128]{3,2,1,0:T(8,128)} %shard_map.89), calls=%async_computation.1 | async-start | bytes 1835008 | tf_op jit(solution)/shard_map/all_to_all | solution.py:542
Sparse Core Ops, SparseCore 0:
  23.9 48.1 all-gather.3

commit v10 on v9

--- a/solution.py
+++ b/solution.py
@@ -312,6 +312,15 @@
     )(gathered)
 
 
+def by_chunks(body, start, together):
+    def several(k, carry):
+        for step in range(together):
+            carry = body(k * together + step, carry)
+        return carry
+
+    return lax.fori_loop(0, 8 // together, several, start)
+
+
 def solve_kernel(
     count_ref, same_ref, other_ref, q_ref, out_ref, r_ref, d_ref, im_ref, mk_ref, x_ref, t_ref
 ):
@@ -399,7 +408,7 @@
         return acc
 
     join()
-    rho = total(lax.fori_loop(0, 8, set_residual, zero))
+    rho = total(by_chunks(set_residual, zero, 8))
 
     def sweep(t, state):
         rho, beta = state
@@ -432,7 +441,7 @@
                 acc = acc + tree_sum([part[j] * line[j] for j in range(7)])
             return acc
 
-        step = rho / total(lax.fori_loop(0, 8, image, zero))
+        step = rho / total(by_chunks(image, zero, 2))
         for n in range(49):
             for to in range(2):
                 x_ref[to, n] = x_ref[to, n] + step * d_ref[n, own[to], :]
@@ -451,7 +460,7 @@
 
         def proceed():
             join()
-            fresh = total(lax.fori_loop(0, 8, descend, zero))
+            fresh = total(by_chunks(descend, zero, 8))
             return fresh, fresh / rho
 
         return lax.cond(t + 1 < count, proceed, lambda: (rho, beta))

time: 186 us -> 183 us (0.984)
  the two profiles are of different devices: /device:TPU:72 before, /device:TPU:8 now
where the time goes in v10:
time: 183 us
  blocking collectives  63.5 us (35%)
  Pallas kernels  34.5 us (19%)
  waiting for transfers between devices  30.9 us (17%)
  starting transfers between devices  30.7 us (17%)
  between operations  14.3 us (8%)
  local copies, waits for them, and re-layouts  8.41 us (5%)
    all_to_all x1, blocking collectives, local(): parts = lax.all_to_all(parts, ROWS, 0, 0, tiled=True)  36.3 us
    pallas_call x1, Pallas kernels, solve(): pl.pallas_call(solve_kernel, out_shape=jax.ShapeDtypeStruct((NZ, 7, 8, 12...  28.1 us
    all_gather x1, blocking collectives, local(): same = lax.all_gather(pair, 'zh')  27.2 us
    all_to_all x1, waiting for transfers between devices, local(): answer = lax.all_to_all(answer, ROWS, 0, 0, tiled=True)  25.3 us
    ppermute x3, starting transfers between devices, local(): turned = [lax.ppermute(packed, RING_X, turn) for turn in TURNS]  10.2 us
    unnamed x13, local copies, waits for them, and re-layouts  7.51 us
    ppermute x1, starting transfers between devices, local(): lax.ppermute(right, FLOW, ahead)  6.05 us
    ppermute x1, starting transfers between devices, local(): pair = jnp.stack([mine, lax.ppermute(mine, 'zl', SWAP)])  4.28 us
  transfers between devices with their start and end apart: 11, of which 4 were waited for; matrix products, arithmetic and copies ran while one was open for 2% of the time, Pallas kernels for 3%

profile of v10, /device:TPU:8, one launch (start us, length us, event | category | flops | bytes accessed | tf_op | source)
XLA Modules:
  0.0 183.0 jit_solution(17793448842166368782)
XLA Ops:
  7.2 0.9 reshape.10
  8.1 4.7 %collective-permute-start.6 = (f32[152,128]{1,0:T(8,128)S(1)}, f32[152,128]{1,0:T(8,128)S(1)}, u32[]{:S(2)}, u32[]{:S(2)}) collective-permute-start(f32[152,128]{1,0:T(8,128)S(1)} %pad.4), channel_id=1, source_target_pairs={{0,48},{16,0},{32,16},{48,32},{1,49},{17,1},{33,17},{49,33},{2,50}... | collective-permute-start | bytes 233480 | tf_op jit(solution)/shard_map/ppermute | solution.py:531
  12.8 2.7 %collective-permute-start.5 = (f32[152,128]{1,0:T(8,128)S(1)}, f32[152,128]{1,0:T(8,128)S(1)}, u32[]{:S(2)}, u32[]{:S(2)}) collective-permute-start(f32[152,128]{1,0:T(8,128)S(1)} %pad.4), channel_id=1, source_target_pairs={{0,32},{16,48},{32,0},{48,16},{1,33},{17,49},{33,1},{49,17},{2,34}... | collective-permute-start | bytes 233480 | tf_op jit(solution)/shard_map/ppermute | solution.py:531
  15.5 2.8 %collective-permute-start.4 = (f32[152,128]{1,0:T(8,128)S(1)}, f32[152,128]{1,0:T(8,128)S(1)}, u32[]{:S(2)}, u32[]{:S(2)}) collective-permute-start(f32[152,128]{1,0:T(8,128)S(1)} %pad.4), channel_id=1, source_target_pairs={{0,16},{16,32},{32,48},{48,0},{1,17},{17,33},{33,49},{49,1},{2,18}... | collective-permute-start | bytes 233480 | tf_op jit(solution)/shard_map/ppermute | solution.py:531
  18.3 1.2 copy.16.s_ref
  21.0 2.0 %collective-permute-done.4 = f32[152,128]{1,0:T(8,128)S(1)} collective-permute-done((f32[152,128]{1,0:T(8,128)S(1)}, f32[152,128]{1,0:T(8,128)S(1)}, u32[]{:S(2)}, u32[]{:S(2)}) %collective-permute-start.4) | collective-permute-done | bytes 77856 | tf_op jit(solution)/shard_map/ppermute | solution.py:531
  23.8 1.3 collective-permute-start.1
  25.1 1.3 collective-permute-start.2
  26.4 1.3 collective-permute-start.3
  27.7 6.1 %collective-permute-start = (f32[4,8,128]{2,1,0:T(8,128)S(1)}, f32[4,8,128]{2,1,0:T(8,128)S(1)}, u32[]{:S(2)}, u32[]{:S(2)}) collective-permute-start(f32[4,8,128]{2,1,0:T(8,128)S(1)} %get-tuple-element.13), channel_id=1, source_target_pairs={{0,32},{32,64},{64,96},{96,128},{128,160},{160,192},{192,224},{224... | collective-permute-start | bytes 49160 | tf_op jit(solution)/shard_map/ppermute | solution.py:536
  33.8 1.0 copy.18.v_ref
  34.7 1.3 copy.17.g_ref
  36.1 3.6 %shard_map.87 = (f32[6,4,7,7,128]{4,3,2,1,0:T(8,128)S(1)}, f32[32,7,8,128]{3,2,1,0:T(8,128)S(1)}) custom-call(f32[3072]{0:T(1024)S(1)} %copy-done.1, f32[6,4,7,7,128]{4,3,2,1,0:T(8,128)S(1)} %copy.16.s_ref, f32[9,4,7,7,128]{4,3,2,1,0:T(8,128)S(1)} %copy.17.g_ref, f32[2,4,7,7,128]{4,3,2,1,0:T(8,128)S(1)} %copy.18.v_ref, ...), custom_call_target="tpu_custom_call" | custom-call | tf_op jit(solution)/shard_map/pallas_call | solution.py:260
  39.7 36.3 %all_to_all.10 = f32[32,7,8,128]{3,2,1,0:T(8,128)S(1)} all-to-all(f32[32,7,8,128]{3,2,1,0:T(8,128)S(1)} %get-tuple-element.23), channel_id=1, replica_groups=mesh['zh'=4,'zl'=2,'xh'=2,'xl'=2,'core'=2,'y'=8] {'xh','xl','y'}, dimensions={0} | all-to-all | bytes 1835008 | tf_op jit(solution)/shard_map/all_to_all | solution.py:545
  76.1 4.3 %collective-permute-start.7 = (f32[4,7,8,128]{3,2,1,0:T(8,128)S(1)}, f32[4,7,8,128]{3,2,1,0:T(8,128)S(1)}, u32[]{:S(2)}, u32[]{:S(2)}) collective-permute-start(f32[4,7,8,128]{3,2,1,0:T(8,128)S(1)} %bitcast_reduce_fusion), channel_id=1, source_target_pairs={{0,64},{64,0},{1,65},{65,1},{2,66},{66,2},{3,67},{67,3},{4,68},{68... | collective-permute-start | bytes 344072 | tf_op jit(solution)/shard_map/ppermute | solution.py:547
  80.4 2.8 %collective-permute-done.7 = f32[4,7,8,128]{3,2,1,0:T(8,128)S(1)} collective-permute-done((f32[4,7,8,128]{3,2,1,0:T(8,128)S(1)}, f32[4,7,8,128]{3,2,1,0:T(8,128)S(1)}, u32[]{:S(2)}, u32[]{:S(2)}) %collective-permute-start.7) | collective-permute-done | bytes 114720 | tf_op jit(solution)/shard_map/ppermute | solution.py:547
  83.2 27.2 %all-gather = f32[8,4,7,8,128]{4,3,2,1,0:T(8,128)S(1)} all-gather(f32[2,4,7,8,128]{4,3,2,1,0:T(8,128)S(1)} %pad_maximum_fusion.1), channel_id=2, replica_groups=mesh['zh'=4,'zl'=2,'xh'=2,'xl'=2,'core'=2,'y'=8] {'zh'}, dimensions={0}, use_global_device_ids=true | all-gather | bytes 1146880 | tf_op jit(solution)/shard_map/all_gather | solution.py:548
  110.3 2.0 %collective-permute-start.8 = (f32[4,2,4,7,8,128]{5,4,3,2,1,0:T(8,128)S(1)}, f32[4,2,4,7,8,128]{5,4,3,2,1,0:T(8,128)S(1)}, u32[]{:S(2)}, u32[]{:S(2)}) collective-permute-start(f32[4,2,4,7,8,128]{5,4,3,2,1,0:T(8,128)S(1)} %bitcast.11), channel_id=1, source_target_pairs={{0,8},{8,0},{1,9},{9,1},{2,10},{10,2},{3,11},{11,3},{4,12},{12,4},... | collective-permute-start | bytes 2752520 | tf_op jit(solution)/shard_map/ppermute | solution.py:549
  112.4 2.4 %copy-done = f32[64,152,128]{2,1,0:T(8,128)S(1)} copy-done((f32[64,152,128]{2,1,0:T(8,128)S(1)}, f32[64,152,128]{2,1,0:T(8,128)}, u32[]{:S(2)}) %copy-start) | copy-done | bytes 4980760
  114.8 1.2 shard_map.88.q_ref
  116.0 28.1 %shard_map.89 = f32[32,7,8,128]{3,2,1,0:T(8,128)} custom-call(s32[32]{0:T(128)S(1)} %copy-done.3, f32[4,2,4,7,8,128]{5,4,3,2,1,0:T(8,128)S(1)} %bitcast.12, f32[4,2,4,7,8,128]{5,4,3,2,1,0:T(8,128)S(1)} %collective-permute-done.8.other_ref, f32[3,49,64,128]{3,2,1,0:T(8,128)S(1)} %shard_map.88.q_ref), custom_call_target="tpu_custom_call" | custom-call | tf_op jit(solution)/shard_map/pallas_call | solution.py:487
  144.1 4.2 %all-to-all-start.1 = ((f32[32,7,8,128]{3,2,1,0:T(8,128)}), f32[32,7,8,128]{3,2,1,0:T(8,128)S(1)}, u32[]{:S(2)}, u32[]{:S(2)}) async-start(f32[32,7,8,128]{3,2,1,0:T(8,128)} %shard_map.89), calls=%async_computation.1 | async-start | bytes 1835008 | tf_op jit(solution)/shard_map/all_to_all | solution.py:551
  148.4 1.0 copy.19
  149.4 25.3 %all-to-all-done.1.rows_ref = f32[32,7,8,128]{3,2,1,0:T(8,128)S(1)} async-done(((f32[32,7,8,128]{3,2,1,0:T(8,128)}), f32[32,7,8,128]{3,2,1,0:T(8,128)S(1)}, u32[]{:S(2)}, u32[]{:S(2)}) %all-to-all-start.1) | async-done | bytes 917536 | tf_op jit(solution)/shard_map/all_to_all | solution.py:551
  (24 shorter events, 3.9 us)
Async XLA Ops:
  7.2 28.9 %copy-start.1 = (f32[3072]{0:T(1024)S(1)}, f32[3072]{0:T(1024)}, u32[]{:S(2)}) copy-start(f32[3072]{0:T(1024)} %constant.8.clone.coef_ref) | copy-start | bytes 36868
  7.2 105.2 %all-gather.4.cloned.1.call-start = ((), (), s32[]{:S(2)}) async-start(), calls=%async_computation.2 | async-start | bytes 5292032 | tf_op jit(solution)/shard_map/all_gather | solution.py:543
  8.1 12.1 %collective-permute-start.6 = (f32[152,128]{1,0:T(8,128)S(1)}, f32[152,128]{1,0:T(8,128)S(1)}, u32[]{:S(2)}, u32[]{:S(2)}) collective-permute-start(f32[152,128]{1,0:T(8,128)S(1)} %pad.4), channel_id=1, source_target_pairs={{0,48},{16,0},{32,16},{48,32},{1,49},{17,1},{33,17},{49,33},{2,50}... | collective-permute-start | bytes 233480 | tf_op jit(solution)/shard_map/ppermute | solution.py:531
  12.8 8.2 %collective-permute-start.5 = (f32[152,128]{1,0:T(8,128)S(1)}, f32[152,128]{1,0:T(8,128)S(1)}, u32[]{:S(2)}, u32[]{:S(2)}) collective-permute-start(f32[152,128]{1,0:T(8,128)S(1)} %pad.4), channel_id=1, source_target_pairs={{0,32},{16,48},{32,0},{48,16},{1,33},{17,49},{33,1},{49,17},{2,34}... | collective-permute-start | bytes 233480 | tf_op jit(solution)/shard_map/ppermute | solution.py:531
  15.5 7.5 %collective-permute-start.4 = (f32[152,128]{1,0:T(8,128)S(1)}, f32[152,128]{1,0:T(8,128)S(1)}, u32[]{:S(2)}, u32[]{:S(2)}) collective-permute-start(f32[152,128]{1,0:T(8,128)S(1)} %pad.4), channel_id=1, source_target_pairs={{0,16},{16,32},{32,48},{48,0},{1,17},{17,33},{33,49},{49,1},{2,18}... | collective-permute-start | bytes 233480 | tf_op jit(solution)/shard_map/ppermute | solution.py:531
  23.8 12.3 %collective-permute-start.1 = (f32[4,8,128]{2,1,0:T(8,128)S(1)}, f32[4,8,128]{2,1,0:T(8,128)S(1)}, u32[]{:S(2)}, u32[]{:S(2)}) collective-permute-start(f32[4,8,128]{2,1,0:T(8,128)S(1)} %get-tuple-element.14), channel_id=1, source_target_pairs={{32,0},{64,32},{96,64},{128,96},{160,128},{192,160},{224,192},{256... | collective-permute-start | bytes 49160 | tf_op jit(solution)/shard_map/ppermute | solution.py:537
  25.1 11.0 %collective-permute-start.2 = (f32[4,8,128]{2,1,0:T(8,128)S(1)}, f32[4,8,128]{2,1,0:T(8,128)S(1)}, u32[]{:S(2)}, u32[]{:S(2)}) collective-permute-start(f32[4,8,128]{2,1,0:T(8,128)S(1)} %get-tuple-element.15), channel_id=1, source_target_pairs={{0,8},{8,16},{16,24},{1,9},{9,17},{17,25},{2,10},{10,18},{18,26},{... | collective-permute-start | bytes 49160 | tf_op jit(solution)/shard_map/ppermute | solution.py:538
  26.4 9.7 %collective-permute-start.3 = (f32[4,8,128]{2,1,0:T(8,128)S(1)}, f32[4,8,128]{2,1,0:T(8,128)S(1)}, u32[]{:S(2)}, u32[]{:S(2)}) collective-permute-start(f32[4,8,128]{2,1,0:T(8,128)S(1)} %get-tuple-element.16), channel_id=1, source_target_pairs={{8,0},{16,8},{24,16},{9,1},{17,9},{25,17},{10,2},{18,10},{26,18},{... | collective-permute-start | bytes 49160 | tf_op jit(solution)/shard_map/ppermute | solution.py:539
  27.7 8.4 %collective-permute-start = (f32[4,8,128]{2,1,0:T(8,128)S(1)}, f32[4,8,128]{2,1,0:T(8,128)S(1)}, u32[]{:S(2)}, u32[]{:S(2)}) collective-permute-start(f32[4,8,128]{2,1,0:T(8,128)S(1)} %get-tuple-element.13), channel_id=1, source_target_pairs={{0,32},{32,64},{64,96},{96,128},{128,160},{160,192},{192,224},{224... | collective-permute-start | bytes 49160 | tf_op jit(solution)/shard_map/ppermute | solution.py:536
  76.1 7.0 %collective-permute-start.7 = (f32[4,7,8,128]{3,2,1,0:T(8,128)S(1)}, f32[4,7,8,128]{3,2,1,0:T(8,128)S(1)}, u32[]{:S(2)}, u32[]{:S(2)}) collective-permute-start(f32[4,7,8,128]{3,2,1,0:T(8,128)S(1)} %bitcast_reduce_fusion), channel_id=1, source_target_pairs={{0,64},{64,0},{1,65},{65,1},{2,66},{66,2},{3,67},{67,3},{4,68},{68... | collective-permute-start | bytes 344072 | tf_op jit(solution)/shard_map/ppermute | solution.py:547
  110.3 5.7 %copy-start.3 = (s32[32]{0:T(128)S(1)}, s32[32]{0:T(128)}, u32[]{:S(2)}) copy-start(s32[32]{0:T(128)} %count_ref.1) | copy-start | bytes 388
  110.3 5.7 %collective-permute-start.8 = (f32[4,2,4,7,8,128]{5,4,3,2,1,0:T(8,128)S(1)}, f32[4,2,4,7,8,128]{5,4,3,2,1,0:T(8,128)S(1)}, u32[]{:S(2)}, u32[]{:S(2)}) collective-permute-start(f32[4,2,4,7,8,128]{5,4,3,2,1,0:T(8,128)S(1)} %bitcast.11), channel_id=1, source_target_pairs={{0,8},{8,0},{1,9},{9,1},{2,10},{10,2},{3,11},{11,3},{4,12},{12,4},... | collective-permute-start | bytes 2752520 | tf_op jit(solution)/shard_map/ppermute | solution.py:549
  112.4 2.4 %copy-start = (f32[64,152,128]{2,1,0:T(8,128)S(1)}, f32[64,152,128]{2,1,0:T(8,128)}, u32[]{:S(2)}) copy-start(f32[64,152,128]{2,1,0:T(8,128)} %all-gather.4.cloned.1.call-done) | copy-start | bytes 14942212
  116.0 58.6 %copy-start.2 = (f32[1024]{0:T(1024)S(1)}, f32[1024]{0:T(1024)}, u32[]{:S(2)}) copy-start(f32[1024]{0:T(1024)} %constant.9.clone.coef_ref) | copy-start | bytes 12292
  144.1 30.5 %all-to-all-start.1 = ((f32[32,7,8,128]{3,2,1,0:T(8,128)}), f32[32,7,8,128]{3,2,1,0:T(8,128)S(1)}, u32[]{:S(2)}, u32[]{:S(2)}) async-start(f32[32,7,8,128]{3,2,1,0:T(8,128)} %shard_map.89), calls=%async_computation.1 | async-start | bytes 1835008 | tf_op jit(solution)/shard_map/all_to_all | solution.py:551
Sparse Core Ops, SparseCore 0:
  23.9 49.0 all-gather.3
